TPU v7x, 32 devices: a whole 2x2x4 slice. The times are simulated.
32 devices in a mesh: seq: 8 (over z, core), row: 4 (over y, x).
Axes of the slice: x: 2, y: 2, z: 4, core: 2. Of those that a mesh axis runs over, the one named last changes fastest.
Arguments:
- inputs: bfloat16 [32, 1024, 512], P('row', 'seq'), may hold values from -6 to 6
- lengths: int32 [32], P('row'), may hold values from 128 to 1024, as said below
- norm_gain: float32 [512], replicated, may hold values from 0.5 to 1.5
- conv_weight: float32 [4, 512], replicated, may hold values from -3 to 3
- gate_weight: bfloat16 [512, 1024], replicated, may hold values from -0.25 to 0.25
- gate_bias: float32 [1024], replicated, may hold values from -9.5 to -2.5
- cand_weight: bfloat16 [512, 1024], replicated, may hold values from -0.25 to 0.25
- out_weight: bfloat16 [1024, 512], replicated, may hold values from -1.5 to 1.5
- mlp_gain: float32 [512], replicated, may hold values from 0.5 to 1.5
- up_weight: bfloat16 [512, 2048], replicated, may hold values from -0.25 to 0.25
- down_weight: bfloat16 [2048, 512], replicated, may hold values from -0.125 to 0.125
- cotangent: bfloat16 [32, 1024, 512], P('row', 'seq'), may hold values from -6 to 6
Outputs:
- output: bfloat16 [32, 1024, 512], P('row', 'seq')
- input_grad: bfloat16 [32, 1024, 512], P('row', 'seq')
- norm_gain_grad: float32 [512], replicated
- conv_weight_grad: float32 [4, 512], replicated
- gate_weight_grad: float32 [512, 1024], replicated
- gate_bias_grad: float32 [1024], replicated
- cand_weight_grad: float32 [512, 1024], replicated
- out_weight_grad: float32 [1024, 512], replicated
- mlp_gain_grad: float32 [512], replicated
- up_weight_grad: float32 [512, 2048], replicated
- down_weight_grad: float32 [2048, 512], replicated
Inputs may be any that keep to these rules, and one draw needn't show every extreme that they name: `lengths`: within each aligned block of 8 rows at least one row has length 1024.
All inputs are finite; a program needn't handle non-finite values.
Results may differ from a plain program's by a relative error of at most 0.018.
Values may be sent and summed in bfloat16 or wider, within the bound.
No kernel may reach another device: no remote copies, remote signals or barrier semaphores. Data moves between devices by JAX's collectives and lax.ppermute only.
A program may use at most 128 MiB of HBM per device.

v0:
```python
import functools

import jax
import jax.numpy as jnp
import numpy as np
from jax import lax
from jax.experimental import pallas as pl
from jax.experimental.pallas import tpu as pltpu
from jax.sharding import PartitionSpec as P

epsilon = 1e-06
f32 = jnp.float32
bf16 = jnp.bfloat16
R = 8
PERM = 256
SCALARS = 4
SLOTS = 32
PIECE1 = 128
PIECE2 = 96


def nn(a, b):
    return lax.dot_general(a, b, (((1,), (0,)), ((), ())), preferred_element_type=f32)


def nt(a, b):
    return lax.dot_general(a, b, (((1,), (1,)), ((), ())), preferred_element_type=f32)


def tn(a, b):
    return lax.dot_general(a, b, (((0,), (0,)), ((), ())), preferred_element_type=f32)


def token_order():
    out = np.arange(PERM)
    source = (out % R) * (PERM // R) + out // R
    to_pm = np.zeros((PERM, PERM), np.float32)
    to_pm[out, source] = 1
    return jnp.asarray(to_pm, bf16), jnp.asarray(to_pm.T, bf16)


def position_major(perm, block):
    span = PERM // R
    parts = []
    for s in range(block.shape[1] // span):
        part = block[:, s * span : (s + 1) * span, :].reshape(PERM, block.shape[2])
        parts.append(nn(perm, part))
    return parts[0] if len(parts) == 1 else jnp.concatenate(parts, 0)


def row_major(perm, tokens):
    span = PERM // R
    parts = []
    for s in range(tokens.shape[0] // PERM):
        part = nn(perm, tokens[s * PERM : (s + 1) * PERM]).astype(bf16)
        parts.append(part.reshape(R, span, tokens.shape[1]))
    return parts[0] if len(parts) == 1 else jnp.concatenate(parts, 1)


def eight(t):
    return pl.ds(pl.multiple_of(t * R, R), R)


def sixteen(t):
    return pl.ds(pl.multiple_of(t * 2 * R, 2 * R), 2 * R)


def normed_edge(edge, gain):
    e = edge.astype(f32)
    inv = lax.rsqrt(jnp.mean(e * e, -1, keepdims=True) + epsilon)
    return (e * inv * gain).astype(bf16).astype(f32)


def set_limits(scal, limit):
    row = lax.broadcasted_iota(jnp.int32, limit.shape, 0)
    value = jnp.zeros(limit.shape, jnp.int32)
    for r in range(R):
        value = jnp.where(row == r, scal[SCALARS + r], value)
    limit[...] = value


def halves(ref, pair):
    both = ref[sixteen(pair), :].astype(f32)
    return both[:R], both[R:]


def norm_kernel(x, perm, gain, u_out):
    xp = position_major(perm[...], x[...])
    inv = lax.rsqrt(jnp.mean(xp * xp, -1, keepdims=True) + epsilon)
    u_out[...] = (xp * inv * gain[...]).astype(bf16)


def front_kernel(scal, u, edge, gain, convw, wg, bias, wc, c_out, zl_out, kh_out, ends, ext, state, limit):
    step = pl.program_id(0)
    m = u.shape[0]
    tb = m // R
    halo = edge.shape[0]
    taps = convw.shape[0]

    @pl.when(step == 0)
    def _():
        set_limits(scal, limit)
        ext[0:halo, :] = normed_edge(edge[...], gain[...])
        state[0:R, :] = jnp.ones((R, state.shape[1]), f32)
        state[R:, :] = jnp.zeros((R, state.shape[1]), f32)

    ext[halo:, :] = u[...].astype(f32)
    conv = convw[0:1, :] * ext[halo:, :]
    for k in range(1, taps):
        lo = halo - k * R
        conv = conv + convw[k : k + 1, :] * ext[lo : lo + m, :]
    ext[0:halo, :] = ext[m : m + halo, :]
    cb = conv.astype(bf16)
    c_out[...] = cb
    kz = nn(cb, wg[...]) + bias[...]
    zs = 1.0 / (1.0 + jnp.exp(-kz))
    width = zs.shape[1]
    zs = zs.reshape(tb, R, width)
    pos = scal[0] + step * tb + lax.broadcasted_iota(jnp.int32, (tb, R, width), 0)
    zl_out[...] = jnp.where(pos < limit[...][None], zs, 0.0).reshape(m, width).astype(bf16)
    kh_out[...] = nn(cb, wc[...]).astype(bf16)

    def body(u, carry):
        prod, h = carry
        za, zb = halves(zl_out, u)
        ka, kb = halves(kh_out, u)
        a = 1.0 - za
        b = 1.0 - zb
        return prod * (a * b), (h * a + za * ka) * b + zb * kb

    prod, h = lax.fori_loop(0, tb // 2, body, (state[0:R, :], state[R:, :]), unroll=4)
    state[0:R, :] = prod
    state[R:, :] = h
    ends[0:R, :] = prod
    ends[R:, :] = h


def gelu_parts(p):
    k0 = 0.7978845608028654
    inner = p * (k0 + (k0 * 0.044715) * (p * p))
    th = jnp.tanh(inner)
    ht = 0.5 + 0.5 * th
    return p * ht, ht + (1.0 - th * th) * (1.5 * inner - k0 * p)


def da_kernel(g, perm, wd, gl_out, da_out):
    gl = position_major(perm[...], g[...]).astype(bf16)
    gl_out[...] = gl
    da_out[...] = nt(gl, wd[...]).astype(bf16)


def core_kernel(scal, x, perm, gl, da, zl, zl_next, kh, kh_next, zl_before, other, *refs, fchunk, hops, blocks):
    msgs = refs[:hops]
    wo, mgain, wu = refs[hops : hops + 3]
    r1_out, y_out, hp_out, n2_out, act_out, dp_out, dm_out, dr1_out, dh_out, back, mg = refs[hops + 3 : hops + 14]
    state, limit, run, acc, ys, hps, dhs = refs[hops + 14 :]
    step = pl.program_id(0)
    tb = x.shape[1]
    m = tb * R
    width, feed = wu.shape
    hidden = wo.shape[0]
    first = scal[0] + step * tb

    def scan_pair(zs, ks, start, u, h):
        t = u * 2
        za, zb = halves(zs, u)
        ka, kb = halves(ks, u)
        ha = h - za * h + za * ka
        hb = ha - zb * ha + zb * kb
        hps[sixteen(u), :] = jnp.concatenate([h, ha], 0).astype(bf16)
        ya = jnp.where(start + t < limit[...], ha, 0.0)
        yb = jnp.where(start + t + 1 < limit[...], hb, 0.0)
        ys[sixteen(u), :] = jnp.concatenate([ya, yb], 0).astype(bf16)
        return hb

    def adjoint_pair(zs, ds, u, prod, total):
        za, zb = halves(zs, u)
        da, db = halves(ds, u)
        pa = prod - za * prod
        pb = pa - zb * pa
        return pb, total + (pa * da + pb * db)

    @pl.when(step == 0)
    def _():
        set_limits(scal, limit)
        h = jnp.zeros((R, hidden), f32)
        for msg in reversed(msgs):
            both = msg[...].astype(f32)
            h = jnp.exp(both[0:R, :]) * h + both[R:, :]
        h = jnp.where(scal[1] == 1, other[0:R, :] * h + other[R:, :], h)
        run[...] = jnp.ones((R, hidden), f32)
        back[...] = jnp.zeros(back.shape, f32)
        mg[...] = jnp.zeros(mg.shape, f32)
        dhs[...] = jnp.zeros(dhs.shape, bf16)
        state[...] = lax.fori_loop(0, tb // 2, lambda u, h: scan_pair(zl, kh, scal[0], u, h), h, unroll=2)

    hp_out[...] = hps[...]
    y = ys[...]
    y_out[...] = y
    r1 = position_major(perm[...], x[...]) + nn(y, wo[...])
    r1_out[...] = r1
    inv = lax.rsqrt(jnp.mean(r1 * r1, -1, keepdims=True) + epsilon)
    n2 = (r1 * inv * mgain[...]).astype(bf16)
    n2_out[...] = n2
    chunks = feed // fchunk
    pairs = tb // 2 // chunks
    for f in range(chunks):
        cols = slice(f * fchunk, (f + 1) * fchunk)
        a, slope = gelu_parts(nn(n2, wu[:, cols]).astype(bf16))
        act_out[:, cols] = a
        dpb = da[:, cols] * slope
        dp_out[:, cols] = dpb
        part = nt(dpb, wu[:, cols])
        acc[...] = acc[...] + part if f else part
        h, prod, total = state[...], run[...], back[...]
        for u in range(f * pairs, (f + 1) * pairs):
            h = scan_pair(zl_next, kh_next, first + tb, u, h)
            prod, total = adjoint_pair(zl_before, dhs, u, prod, total)
        state[...] = h
        run[...] = jnp.where(step == 0, 1.0, prod)
        back[...] = total
    dn2 = acc[...]
    r1 = r1_out[...]
    mg[...] += jnp.sum((dn2 * r1 * inv).reshape(tb, R, width), 0)
    s = mgain[...] * dn2
    mean = jnp.mean(s * r1, -1, keepdims=True)
    dr1 = gl[...].astype(f32) + inv * (s - r1 * (inv * inv * mean))
    dr1_out[...] = dr1
    dm = dr1.astype(bf16)
    dm_out[...] = dm
    dh = nt(dm, wo[...]).reshape(tb, R, hidden)
    pos = first + lax.broadcasted_iota(jnp.int32, (tb, R, hidden), 0)
    dh = jnp.where(pos < limit[...][None], dh, 0.0).reshape(m, hidden).astype(bf16)
    dh_out[...] = dh
    dhs[...] = dh

    @pl.when(step == blocks - 1)
    def _():
        carry = lax.fori_loop(
            0, tb // 2, lambda u, carry: adjoint_pair(zl, dhs, u, *carry), (run[...], back[...]), unroll=4
        )
        back[...] = carry[1]


def put_rows(dst, sel, piece, at, rows, part):
    for i in range(SLOTS // 2):
        pos = pl.multiple_of((i ^ sel) * piece + at, 16)
        dst[pl.ds(pos, rows), :] = part[i * rows : (i + 1) * rows]


def ffn_grad_kernel(scal, act, gl, n2, dp, dst, *, pick):
    step = pl.program_id(0)
    sel = scal[2 + pick]
    width = gl.shape[1]
    rows1 = act.shape[1] * 4 // SLOTS
    rows2 = n2.shape[1] * 2 // SLOTS
    part = tn(act[...], gl[...]).astype(bf16)
    per = act.shape[1] // rows1
    for i in range(per):
        pos = ((step * per + i) ^ sel) * PIECE1
        dst[pl.ds(pl.multiple_of(pos, 16), rows1), :] = part[i * rows1 : (i + 1) * rows1]
    columns = dp.shape[1] // width
    for q in range(columns):
        part = tn(n2[...], dp[:, q * width : (q + 1) * width]).astype(bf16)
        put_rows(dst, sel, PIECE1, rows1 + (step * columns + q) * rows2, rows2, part)


def gate_grad_kernel(scal, c, dkz, dkh, y, dm, dst, *, pick):
    sel = scal[2 + pick]
    width = dm.shape[1]
    rows = c.shape[1] * 2 // SLOTS
    at = 0
    for grads in (dkz, dkh):
        for q in range(grads.shape[1] // width):
            part = tn(c[...], grads[:, q * width : (q + 1) * width]).astype(bf16)
            put_rows(dst, sel, PIECE2, at, rows, part)
            at += rows
    put_rows(dst, sel, PIECE2, at, y.shape[1] * 2 // SLOTS, tn(y[...], dm[...]).astype(bf16))


def gate_kernel(scal, dh, zl, kh, hp, other, fother, *refs, blocks, hops):
    msgs = refs[:hops]
    wg, wc = refs[hops : hops + 2]
    dkz, dkh, edge_out, bias_out = refs[hops + 3 : hops + 7]
    state = refs[hops + 7]
    step = pl.program_id(0)
    m = dh.shape[0]
    tb = m // R
    block = blocks - 1 - step

    @pl.when(step == 0)
    def _():
        mm = jnp.zeros(state.shape, f32)
        for msg in reversed(msgs):
            both = msg[...].astype(f32)
            mm = jnp.exp(both[0:R, :]) * mm + both[R:, :]
        state[...] = jnp.where(scal[1] == 0, fother[...] + other[0:R, :] * mm, mm)
        bias_out[...] = jnp.zeros(bias_out.shape, f32)

    def body(u, carry):
        mm, bias = carry
        w = tb // 2 - 1 - u
        ha, hb = halves(hp, w)
        za, zb = halves(zl, w)
        da, db = halves(dh, w)
        ka, kb = halves(kh, w)
        lam = db + mm
        sb = lam * zb
        mm = lam - sb
        kb = (sb - sb * zb) * (kb - hb)
        lam = da + mm
        sa = lam * za
        mm = lam - sa
        ka = (sa - sa * za) * (ka - ha)
        kk = jnp.concatenate([ka, kb], 0).astype(bf16)
        dkz[sixteen(w), :] = kk
        dkh[sixteen(w), :] = jnp.concatenate([sa, sb], 0).astype(bf16)
        kf = kk.astype(f32)
        return mm, bias + kf[:R, :] + kf[R:, :]

    mm, bias = lax.fori_loop(0, tb // 2, body, (state[...], bias_out[...]), unroll=2)
    state[...] = mm
    bias_out[...] = bias

    @pl.when(block == 0)
    def _():
        span = edge_out.shape[0]
        edge_out[...] = (nt(dkz[0:span, :], wg[...]) + nt(dkh[0:span, :], wc[...])).astype(bf16)


def tail_kernel(x, dr1, dkz, dkh, pm, back_pm, edge, after, gain, convw, wg, wc, grad, sums, uext, dext, *, blocks):
    step = pl.program_id(0)
    tb = x.shape[1]
    m = tb * R
    halo = edge.shape[0]
    taps = convw.shape[0]
    width = gain.shape[1]

    @pl.when(step == 0)
    def _():
        uext[0:halo, :] = normed_edge(edge[...], gain[...])
        dext[blocks * m :, :] = after[...].astype(f32)
        sums[...] = jnp.zeros(sums.shape, f32)

    @pl.when(step < blocks)
    def _():
        rows = pl.ds(pl.multiple_of(step * m, m), m)
        dext[rows, :] = nt(dkz[...], wg[...]) + nt(dkh[...], wc[...])

    @pl.when(step >= blocks)
    def _():
        xp = position_major(pm[...], x[...])
        inv = lax.rsqrt(jnp.mean(xp * xp, -1, keepdims=True) + epsilon)
        xn = xp * inv
        uext[halo:, :] = (xn * gain[...]).astype(bf16).astype(f32)
        start = (step - blocks) * m
        here = dext[pl.ds(pl.multiple_of(start, R), m), :]
        du = convw[0:1, :] * here
        for k in range(taps):
            lo = halo - k * R
            part = (here * uext[lo : lo + m, :]).reshape(tb, R, width)
            sums[(k + 1) * R : (k + 2) * R, :] += jnp.sum(part, 0)
            if k:
                du = du + convw[k : k + 1, :] * dext[pl.ds(pl.multiple_of(start + k * R, R), m), :]
        uext[0:halo, :] = uext[m : m + halo, :]
        sums[0:R, :] += jnp.sum((du * xn).reshape(tb, R, width), 0)
        s1 = gain[...] * du
        mean = jnp.mean(s1 * xn, -1, keepdims=True)
        gin = dr1[...] + inv * (s1 - xn * mean)
        grad[...] = row_major(back_pm[...], gin.astype(bf16))


def output_kernel(r1, act, perm, wd, out):
    total = r1[...] + nn(act[...], wd[...])
    out[...] = row_major(perm[...], total.astype(bf16))


def spread_kernel(scal, src, *refs, piece, plan, mate):
    low = scal[2 + mate] & 7
    for a in range(8):
        base = (a ^ low) * piece
        at = 0
        for out, rows, columns in plan:
            ref = refs[len(refs) - len(plan) + out]
            for q in range(columns):
                width = src.shape[1]
                part = src[pl.ds(pl.multiple_of(base + at, 16), rows), :].astype(f32)
                ref[a * rows : (a + 1) * rows, q * width : (q + 1) * width] = part
                at += rows


def last_spread_kernel(scal, src, ride, rest, theirs, *refs, piece, plan, taps):
    norm, conv, mlp, bias = refs[-4:]
    spread_kernel(scal, src, *refs[:-4], piece=piece, plan=plan, mate=1)
    tail = src.shape[0] - 2 * R
    total = ride[...]
    for rows in (rest[...], theirs[...], src[tail:, :]):
        both = rows.astype(f32)
        total = total + (both[:R] + both[R:])
    norm[...] = total[0:1]
    conv[...] = total[1 : taps + 1]
    mlp[...] = total[taps + 1 : taps + 2]
    width = total.shape[1]
    for i in range(bias.shape[1] // width):
        bias[:, i * width : (i + 1) * width] = total[taps + 2 + i : taps + 3 + i]


def last_spread(scal, chunk, held, piece, plan, shapes, taps, hidden):
    src = chunk.their_rest
    width = src.shape[1]
    rows = 2 * R
    tail = pl.BlockSpec((rows, width), lambda g, s: (src.shape[0] // rows - 1, 0))
    small = ((1, width), (taps, width), (1, width), (1, hidden))

    def block(g, s):
        return ((s[1] ^ 1) * 2 + ((s[3] >> 3) ^ 1), 0)

    return pl.pallas_call(
        functools.partial(last_spread_kernel, piece=piece, plan=plan, taps=taps),
        grid_spec=pltpu.PrefetchScalarGridSpec(
            num_scalar_prefetch=1,
            grid=(1,),
            in_specs=[whole(src), whole(chunk.ride), tail, tail] + [ORDER] * len(held),
            out_specs=[pl.BlockSpec((dims[0] // 4, dims[1]), block) for dims in shapes]
            + [pl.BlockSpec(dims, lambda g, s: (0, 0)) for dims in small],
        ),
        out_shape=[pltpu.HBM(dims, f32) for dims in shapes] + [shape(dims) for dims in small],
        input_output_aliases={5 + k: k for k in range(len(held))},
        compiler_params=params(16),
        cost_estimate=MUCH,
        name="spread_last",
    )(scal, src, chunk.ride, chunk.rest, chunk.theirs, *held)


def spread(scal, src, held, mate, flip, piece, plan, shapes, name):
    def block(g, s):
        return ((s[1] ^ mate) * 2 + ((s[2 + mate] >> 3) ^ flip), 0)

    count = len(held)
    return pl.pallas_call(
        functools.partial(spread_kernel, piece=piece, plan=plan, mate=mate),
        grid_spec=pltpu.PrefetchScalarGridSpec(
            num_scalar_prefetch=1,
            grid=(1,),
            in_specs=[whole(src)] + [ORDER] * count,
            out_specs=[pl.BlockSpec((dims[0] // 4, dims[1]), block) for dims in shapes],
        ),
        out_shape=[pltpu.HBM(dims, f32) for dims in shapes],
        input_output_aliases={2 + k: k for k in range(count)},
        compiler_params=params(16),
        cost_estimate=MUCH,
        name=name,
    )(scal, src, *held)


def params(mib):
    return pltpu.CompilerParams(
        dimension_semantics=("arbitrary",), vmem_limit_bytes=mib * 1024 * 1024
    )


def shape(dims, kind=f32):
    return jax.ShapeDtypeStruct(dims, kind)


LITTLE = pl.CostEstimate(flops=1024, bytes_accessed=1024, transcendentals=0)
MUCH = pl.CostEstimate(flops=3 * 10**10, bytes_accessed=1024, transcendentals=0)
ORDER = pl.BlockSpec(memory_space=pl.ANY)


def far(array):
    return pltpu.with_memory_space_constraint(array, pltpu.HBM)


def whole(array):
    zeros = (0,) * array.ndim
    return pl.BlockSpec(array.shape, lambda *a: zeros, pipeline_mode=pl.Buffered(1))


def passed_along(value, axis, steps):
    count = lax.axis_size(axis)
    leading, last = (max(0, -steps), min(count, count - steps))
    return lax.ppermute(value, axis, [(source, source + steps) for source in range(leading, last)])


def flat_permute(value, pairs):
    return lax.ppermute(value, ("seq", "row"), pairs)


def stage_bits():
    row_bits = lax.axis_size("row").bit_length() - 1
    seq_bits = lax.axis_size("seq").bit_length() - 1
    plane = list(range(row_bits))
    line = [row_bits + 1 + z for z in range(seq_bits - 1)]
    cut = row_bits // 2
    return (plane + line, plane[cut:] + plane[:cut] + line[::-1])


def slot_of(flat, bits):
    slot = 0
    for k in range(4):
        slot = slot * 2 + ((flat >> bits[k]) & 1)
    return slot


def halving_pairs(stage):
    row_bits = lax.axis_size("row").bit_length() - 1
    orders = stage_bits()
    devices = lax.axis_size("row") * lax.axis_size("seq")
    return [(d, d ^ (1 << orders[(d >> row_bits) & 1][stage])) for d in range(devices)]


def core_pairs():
    row_bits = lax.axis_size("row").bit_length() - 1
    devices = lax.axis_size("row") * lax.axis_size("seq")
    return [(d, d ^ (1 << row_bits)) for d in range(devices)]


def added(a, b):
    return (a.astype(f32) + b.astype(f32)).astype(bf16)


class Sequence:
    def __init__(self, token):
        self.token = token

    def after(self, *arrays):
        *arrays, _ = lax.optimization_barrier((*arrays, self.token))
        return arrays[0] if len(arrays) == 1 else arrays

    def did(self, array):
        self.token = array
        return array


def split(value):
    high = lax.reduce_precision(value, 8, 7)
    return [high.astype(bf16), (value - high).astype(bf16)]


def join_kernel(mine, recv, ride, out, ride_out):
    rows = mine.shape[0] - 2 * R
    out[0:rows, :] = mine[0:rows, :]
    out[rows : 2 * rows, :] = recv[0:rows, :]
    parts = recv[rows:, :].astype(f32)
    total = ride[...] + (parts[:R] + parts[R:])
    ride_out[...] = total
    high = total.astype(bf16).astype(f32)
    out[2 * rows :, :] = jnp.concatenate([high, total - high], 0).astype(bf16)


def chain_kernel(mine, recv, out):
    rows = mine.shape[0]
    out[0:rows, :] = mine[...]
    out[rows:, :] = recv[...]


def chained(mine, recv):
    rows, width = mine.shape
    return pl.pallas_call(
        chain_kernel,
        in_specs=[pl.BlockSpec(memory_space=pltpu.VMEM)] * 2,
        out_specs=pl.BlockSpec(memory_space=pltpu.VMEM),
        out_shape=shape((2 * rows, width), bf16),
        compiler_params=pltpu.CompilerParams(vmem_limit_bytes=16 * 1024 * 1024),
        cost_estimate=MUCH,
        name="chain",
    )(mine, recv)


def joined(mine, recv, ride, estimate):
    rows, width = mine.shape
    return pl.pallas_call(
        join_kernel,
        in_specs=[pl.BlockSpec(memory_space=pltpu.VMEM)] * 3,
        out_specs=[pl.BlockSpec(memory_space=pltpu.VMEM)] * 2,
        out_shape=[shape((2 * rows - 2 * R, width), bf16), shape(ride.shape)],
        compiler_params=pltpu.CompilerParams(vmem_limit_bytes=16 * 1024 * 1024),
        cost_estimate=estimate,
        name="join",
    )(mine, recv, ride)


class Halving:
    def __init__(self, seq, send):
        self.seq = seq
        self.recv = flat_permute(send, core_pairs())
        self.stage = 0
        self.ride = None

    def riders(self):
        return [] if self.ride is None else split(self.ride)

    def step(self, *beside):
        k = self.stage
        self.stage += 1
        stages = len(stage_bits()[0])
        recv, *beside = self.seq.after(self.recv, *beside) if beside else (self.seq.after(self.recv),)
        if k < 4:
            half = self.keep.shape[0] // 2
            send = self.seq.did(added(self.keep[half:], recv[half:]))
            self.recv = flat_permute(send, halving_pairs(k))
            self.keep = added(self.keep[:half], recv[:half])
        elif k == 4:
            total = added(self.keep, recv)
            for extra in range(4, stages):
                total = added(total, flat_permute(total, halving_pairs(extra)))
                if self.ride is not None:
                    self.ride = self.ride + flat_permute(self.ride, halving_pairs(extra))
            self.rows = total.shape[0]
            self.total = self.seq.did(jnp.concatenate([total] + self.riders(), 0))
            self.recv = flat_permute(self.total, halving_pairs(3))
        elif k < 8:
            rows = self.rows
            self.rows = 2 * rows
            if self.ride is None:
                self.total = self.seq.did(chained(self.total, recv))
            else:
                self.total, self.ride = joined(
                    self.total, recv, self.ride, LITTLE if k == 5 else MUCH
                )
                self.seq.did(self.total)
            self.recv = flat_permute(self.total, halving_pairs(7 - k))
            if k == 7:
                self.theirs = flat_permute(self.total, core_pairs())
        else:
            self.rest = recv
            self.their_rest = flat_permute(recv, core_pairs())
        return beside


def chip_shift(value, steps):
    return passed_along(value, "seq", 2 * steps)


def per_device(
    inputs,
    lengths,
    norm_gain,
    conv_weight,
    gate_weight,
    gate_bias,
    cand_weight,
    out_weight,
    mlp_gain,
    up_weight,
    down_weight,
    cotangent,
):
    rows, span, width = inputs.shape
    hidden = gate_weight.shape[1]
    feed = up_weight.shape[1]
    taps = conv_weight.shape[0]
    margin = taps - 1
    tokens = rows * span
    tb = 32
    blocks = span // tb
    m = tb * R
    seq = lax.axis_index("seq")
    core = seq & 1
    chips = lax.axis_size("seq") // 2
    hops = chips - 1
    flat = seq * lax.axis_size("row") + lax.axis_index("row")
    slots = [slot_of(flat, bits) for bits in stage_bits()]
    here = jnp.where(core == 0, slots[0], slots[1])
    mate = jnp.where(core == 0, slots[1], slots[0])
    scal = jnp.concatenate([jnp.stack([seq * span, core, here, mate]).astype(jnp.int32), lengths])
    gain1 = norm_gain.reshape(1, width)
    gain2 = mlp_gain.reshape(1, width)
    bias = gate_bias.reshape(1, hidden)
    to_pm, to_rm = token_order()

    edge = inputs[:, span - margin :, :].swapaxes(0, 1).reshape(margin * rows, width)
    edge = passed_along(edge, "seq", 1)

    last = blocks - 1
    clamp = lambda i: jnp.minimum(i, last)
    late = lambda i: jnp.maximum(i - blocks, 0)
    later = lambda i: jnp.minimum(i + 1, last)
    before = lambda i: jnp.maximum(i - 1, 0)

    def rm(index):
        return pl.BlockSpec((rows, tb, width), lambda i, *s: (0, index(i), 0))

    def tok(w, index=clamp):
        return pl.BlockSpec((m, w), lambda i, *s: (index(i), 0))

    def rtok(w):
        return tok(w, lambda i: last - clamp(i))

    def fixed(dims):
        zeros = (0,) * len(dims)
        return pl.BlockSpec(dims, lambda i, *s: zeros)

    def call(kernel, name, grid, ins, outs, scratch, operands, scalars=True, much=False):
        spec = pltpu.PrefetchScalarGridSpec(
            num_scalar_prefetch=int(scalars),
            grid=(grid,),
            in_specs=ins,
            out_specs=[o[1] for o in outs],
            scratch_shapes=scratch,
        )
        return pl.pallas_call(
            kernel,
            grid_spec=spec,
            out_shape=[o[0] for o in outs],
            compiler_params=params(16),
            cost_estimate=MUCH if much else LITTLE,
            name=name,
        )(*operands)

    def rows_of(w, kind, spec=tok, kept=shape):
        return kept((tokens, w), kind), spec(w)

    (normed,) = call(
        norm_kernel, "norm", blocks,
        [rm(clamp), whole(to_pm), whole(gain1)],
        [rows_of(width, bf16)],
        [],
        (far(inputs), far(to_pm), far(gain1)),
        scalars=False,
    )
    edge, normed = lax.optimization_barrier((edge, normed))
    c, zl, kh, ends = call(
        front_kernel, "front", blocks,
        [
            tok(width), whole(edge), whole(gain1), whole(conv_weight),
            whole(gate_weight), whole(bias), whole(cand_weight),
        ],
        [
            rows_of(width, bf16), rows_of(hidden, bf16), rows_of(hidden, bf16),
            (shape((2 * R, hidden)), fixed((2 * R, hidden))),
        ],
        [
            pltpu.VMEM((margin * R + m, width), f32),
            pltpu.VMEM((2 * R, hidden), f32),
            pltpu.VMEM((R, hidden), jnp.int32),
        ],
        (
            scal, normed, edge, far(gain1), far(conv_weight), gate_weight, far(bias),
            cand_weight,
        ),
    )

    other = flat_permute(ends, core_pairs())
    first = jnp.where(core == 0, ends, other)
    second = jnp.where(core == 0, other, ends)
    decay = jnp.log(jnp.maximum(ends[:R] * other[:R], 1e-37))
    message = jnp.concatenate([decay, second[:R] * first[R:] + second[R:]], 0).astype(bf16)
    forward = [chip_shift(message, k) for k in range(1, chips)]

    gl, da = call(
        da_kernel, "da", blocks,
        [rm(clamp), whole(to_pm), whole(down_weight)],
        [rows_of(width, bf16), rows_of(feed, bf16)],
        [],
        (cotangent, to_pm, down_weight),
        scalars=False,
    )

    r1, y, hp, n2, act, dp, dm, dr1, dh, back, mg = call(
        functools.partial(core_kernel, fchunk=256, hops=hops, blocks=blocks), "core", blocks,
        [
            rm(clamp), whole(to_pm), tok(width), tok(feed), tok(hidden), tok(hidden, later), tok(hidden),
            tok(hidden, later), tok(hidden, before), whole(other),
            *[whole(f) for f in forward], whole(out_weight), whole(gain2), whole(up_weight),
        ],
        [
            rows_of(width, f32, kept=pltpu.HBM), rows_of(hidden, bf16), rows_of(hidden, bf16),
            rows_of(width, bf16), rows_of(feed, bf16), rows_of(feed, bf16), rows_of(width, bf16),
            rows_of(width, f32, kept=pltpu.HBM),
            rows_of(hidden, bf16),
            (shape((R, hidden)), fixed((R, hidden))), (shape((R, width)), fixed((R, width))),
        ],
        [
            pltpu.VMEM((R, hidden), f32),
            pltpu.VMEM((R, hidden), jnp.int32),
            pltpu.VMEM((R, hidden), f32),
            pltpu.VMEM((m, width), f32),
            pltpu.VMEM((m, hidden), bf16),
            pltpu.VMEM((m, hidden), bf16),
            pltpu.VMEM((m, hidden), bf16),
        ],
        (
            scal, inputs, to_pm, gl, da, zl, zl, kh, kh, zl, other, *forward, far(out_weight), gain2, up_weight,
        ),
    )

    order = Sequence(back)
    quarter = feed // 4

    def ffn_grads(pick, *beside):
        half = lambda s: s[1] if pick == 0 else 1 - s[1]
        a, d, *beside = order.after(act, dp, *beside)
        (piece,) = call(
            functools.partial(ffn_grad_kernel, pick=pick), "ffn_grad", 2,
            [
                pl.BlockSpec((tokens, quarter), lambda i, s: (0, half(s) * 2 + i)), whole(gl),
                pl.BlockSpec((tokens, width // 2), lambda i, s: (0, half(s))),
                pl.BlockSpec((tokens, feed // 2), lambda i, s: (0, i)),
            ],
            [(shape((SLOTS // 2 * PIECE1, width), bf16), fixed((SLOTS // 2 * PIECE1, width)))],
            [],
            (scal, a, gl, n2, d),
            much=pick == 0,
        )
        return order.did(piece), beside

    def gate_grads(pick):
        half = lambda s: s[1] if pick == 0 else 1 - s[1]
        z, h = order.after(dkz, dkh)
        (piece,) = call(
            functools.partial(gate_grad_kernel, pick=pick), "gate_grad", 1,
            [
                pl.BlockSpec((tokens, width // 2), lambda i, s: (0, half(s))),
                whole(z), whole(h),
                pl.BlockSpec((tokens, hidden // 2), lambda i, s: (0, half(s))), whole(dm),
            ],
            [(shape((SLOTS // 2 * PIECE2, width), bf16), fixed((SLOTS // 2 * PIECE2, width)))],
            [],
            (scal, c, z, h, y, dm),
            much=pick == 0,
        )
        return order.did(piece)

    fother = flat_permute(back, core_pairs())
    lower = jnp.where(core == 0, back, fother)
    upper = jnp.where(core == 0, fother, back)
    message = jnp.concatenate([decay, lower + first[:R] * upper], 0).astype(bf16)
    backward = [chip_shift(order.did(message), -k) for k in range(1, chips)]
    send1, _ = ffn_grads(1)
    chunk1 = Halving(order, send1)
    chunk1.keep, backward = ffn_grads(0, *backward)
    chunk1.step()

    dkz, dkh, edge_dc, bias_part = call(
        functools.partial(gate_kernel, blocks=blocks, hops=hops), "gates", blocks,
        [
            rtok(hidden), rtok(hidden), rtok(hidden), rtok(hidden),
            whole(other), whole(fother), *[whole(f) for f in backward],
            whole(gate_weight), whole(cand_weight), ORDER,
        ],
        [
            rows_of(hidden, bf16, rtok), rows_of(hidden, bf16, rtok),
            (shape((4 * R, width), bf16), fixed((4 * R, width))),
            (shape((R, hidden)), fixed((R, hidden))),
        ],
        [pltpu.VMEM((R, hidden), f32)],
        (
            scal, dh, zl, kh, hp, other, fother, *backward, gate_weight, cand_weight, order.token,
        ),
    )
    order.did(bias_part)
    after = passed_along(edge_dc[: margin * R], "seq", -1)
    send2 = gate_grads(1)
    chunk2 = Halving(order, send2)
    (output,) = call(
        output_kernel, "output", blocks,
        [tok(width), tok(feed), whole(to_rm), whole(down_weight)],
        [(shape((rows, span, width), bf16), rm(clamp))],
        [],
        (far(r1), order.after(act), to_rm, down_weight),
        scalars=False,
    )
    order.did(output)
    chunk1.step()
    chunk2.keep = gate_grads(0)
    (after,) = chunk2.step(after)
    input_grad, sums = call(
        functools.partial(tail_kernel, blocks=blocks), "tail", 2 * blocks,
        [
            rm(late), tok(width, late), tok(hidden), tok(hidden), whole(to_pm), whole(to_rm),
            whole(edge), whole(after), whole(gain1), whole(conv_weight), whole(gate_weight),
            whole(cand_weight),
        ],
        [
            (shape((rows, span, width), bf16), rm(late)),
            (shape(((taps + 1) * R, width)), fixed(((taps + 1) * R, width))),
        ],
        [
            pltpu.VMEM((margin * R + m, width), f32),
            pltpu.VMEM((margin * R + tokens, width), f32),
        ],
        (
            far(inputs), far(dr1), order.after(dkz), dkh, far(to_pm), far(to_rm), edge, after,
            far(gain1), far(conv_weight), far(gate_weight), far(cand_weight),
        ),
        scalars=False,
    )
    order.did(sums)
    small = jnp.concatenate(
        [
            sums.reshape(taps + 1, R, width).sum(1),
            mg.sum(0, keepdims=True),
            bias_part.sum(0).reshape(hidden // width, width),
        ],
        0,
    )

    plan1 = ((0, feed // SLOTS, 1), (1, width // SLOTS, feed // width))
    shapes1 = ((feed, width), (width, feed))
    plan2 = (
        (0, width // SLOTS, hidden // width),
        (1, width // SLOTS, hidden // width),
        (2, hidden // SLOTS, 1),
    )
    shapes2 = ((width, hidden), (width, hidden), (hidden, width))
    held1, held2 = (), ()

    def spread1(src, mate, flip):
        nonlocal held1
        src = order.after(src)
        held1 = spread(scal, src, held1, mate, flip, PIECE1, plan1, shapes1, "spread_ffn")
        order.did(held1[0])

    def spread2(src, mate, flip):
        nonlocal held2
        src = order.after(src)
        held2 = spread(scal, src, held2, mate, flip, PIECE2, plan2, shapes2, "spread_gates")
        order.did(held2[0])

    chunk2.ride = small
    for chunk in (chunk1, chunk2, chunk1, chunk2, chunk1, chunk2, chunk1, chunk2):
        chunk.step()
    chunk2.step()
    chunk1.step()
    chunk2.step()
    chunk1.step()
    chunk2.step()
    spread1(chunk1.total, 0, 0)
    spread1(chunk1.theirs, 1, 0)
    chunk1.step()
    spread1(chunk1.rest, 0, 1)
    spread2(chunk2.total, 0, 0)
    spread1(chunk1.their_rest, 1, 1)
    spread2(chunk2.theirs, 1, 0)
    chunk2.step()
    spread2(chunk2.rest, 0, 1)
    chunk2.their_rest = order.after(chunk2.their_rest)
    *held2, norm_sum, conv_sum, mlp_sum, bias_sum = last_spread(
        scal, chunk2, held2, PIECE2, plan2, shapes2, taps, hidden
    )
    return (
        output,
        input_grad,
        norm_sum.reshape(width),
        conv_sum,
        held2[0],
        bias_sum.reshape(hidden),
        held2[1],
        held2[2],
        mlp_sum.reshape(width),
        held1[1],
        held1[0],
    )


def solution(mesh):
    sharded = P("row", "seq", None)
    in_specs = (sharded, P("row")) + (P(),) * 9 + (sharded,)
    out_specs = (sharded, sharded) + (P(),) * 9
    return jax.shard_map(
        per_device, mesh=mesh, in_specs=in_specs, out_specs=out_specs, check_vma=False
    )
```

profile of v0, /device:TPU:0, one launch (start us, length us, event | category | flops | bytes accessed | tf_op | source)
XLA Modules:
  0.0 176.2 jit_solution(1949815540760902500)
XLA Ops:
  0.7 1.0 slice_bitcast_fusion
  1.7 2.4 %collective-permute-start = (bf16[24,512]{1,0:T(8,128)(2,1)S(1)}, bf16[24,512]{1,0:T(8,128)(2,1)S(1)}, u32[]{:S(2)}, u32[]{:S(2)}) collective-permute-start(bf16[24,512]{1,0:T(8,128)(2,1)S(1)} %bitcast.19), channel_id=1, source_target_pairs={{0,4},{4,8},{8,12},{12,16},{16,20},{20,24},{24,28},{1,5},{5,9},{9,... | collective-permute-start | bytes 73736 | tf_op jit(solution)/shard_map/ppermute | solution.py:483
  4.1 3.0 %norm.1.u = bf16[1024,512]{1,0:T(8,128)(2,1)S(1)} custom-call(bf16[8,128,512]{2,1,0:T(8,128)(2,1)} %x.5, bf16[256,256]{1,0:T(8,128)(2,1)} %constant.29.clone.perm.pm, f32[1,512]{1,0:T(1,128)} %bitcast.20), custom_call_target="tpu_custom_call" | custom-call | flops 1024 | bytes 1024 | tf_op jit(solution)/shard_map/norm/pallas_call | solution.py:703
  7.2 6.5 %front.1 = (bf16[1024,512]{1,0:T(8,128)(2,1)S(1)}, bf16[1024,1024]{1,0:T(8,128)(2,1)S(1)}, bf16[1024,1024]{1,0:T(8,128)(2,1)S(1)}, f32[16,1024]{1,0:T(8,128)S(1)}) custom-call(s32[12]{0:T(128)S(1)} %concatenate.17.scal, bf16[1024,512]{1,0:T(8,128)(2,1)S(1)} %norm.1.u, bf16[24,512]{1,0:T(8,128)(2,1)S(1)} %collective-permute-done.edge, f32[1,512]{1,0:T(1,128)} %bitcast.21, ...), custom_call_target="tpu_custom_call" | custom-call | flops 1024 | bytes 1024 | tf_op jit(solution)/shard_map/front/pallas_call | solution.py:703
  13.8 2.8 %collective-permute-start.1 = (f32[16,1024]{1,0:T(8,128)S(1)}, f32[16,1024]{1,0:T(8,128)S(1)}, u32[]{:S(2)}, u32[]{:S(2)}) collective-permute-start(f32[16,1024]{1,0:T(8,128)S(1)} %get-tuple-element.112), channel_id=1, source_target_pairs={{0,4},{1,5},{2,6},{3,7},{4,0},{5,1},{6,2},{7,3},{8,12},{9,13},{10,... | collective-permute-start | bytes 196616 | tf_op jit(solution)/shard_map/ppermute | solution.py:487
  16.6 0.9 collective-permute-done.1.other
  17.5 4.2 %collective-permute-start.4 = (bf16[16,1024]{1,0:T(8,128)(2,1)S(1)}, bf16[16,1024]{1,0:T(8,128)(2,1)S(1)}, u32[]{:S(2)}, u32[]{:S(2)}) collective-permute-start(bf16[16,1024]{1,0:T(8,128)(2,1)S(1)} %pad_maximum_fusion.2), channel_id=1, source_target_pairs={{0,24},{4,28},{1,25},{5,29},{2,26},{6,30},{3,27},{7,31}} | collective-permute-start | bytes 98312 | tf_op jit(solution)/shard_map/ppermute | solution.py:483
  21.8 1.3 collective-permute-start.3
  23.1 2.5 %collective-permute-start.2 = (bf16[16,1024]{1,0:T(8,128)(2,1)S(1)}, bf16[16,1024]{1,0:T(8,128)(2,1)S(1)}, u32[]{:S(2)}, u32[]{:S(2)}) collective-permute-start(bf16[16,1024]{1,0:T(8,128)(2,1)S(1)} %pad_maximum_fusion.2), channel_id=1, source_target_pairs={{0,8},{4,12},{8,16},{12,20},{16,24},{20,28},{1,9},{5,13},{9,17},{1... | collective-permute-start | bytes 98312 | tf_op jit(solution)/shard_map/ppermute | solution.py:483
  25.6 3.5 %da.1 = (bf16[1024,512]{1,0:T(8,128)(2,1)S(1)}, bf16[1024,2048]{1,0:T(8,128)(2,1)S(1)}) custom-call(bf16[8,128,512]{2,1,0:T(8,128)(2,1)S(1)} %copy-done.10, bf16[256,256]{1,0:T(8,128)(2,1)S(1)} %copy-done.8, bf16[2048,512]{1,0:T(8,128)(2,1)S(1)} %copy-done.7), custom_call_target="tpu_custom_call" | custom-call | flops 1024 | bytes 1024 | tf_op jit(solution)/shard_map/da/pallas_call | solution.py:703
  29.2 14.4 %core.1 = (f32[1024,512]{1,0:T(8,128)}, bf16[1024,1024]{1,0:T(8,128)(2,1)S(1)}, bf16[1024,1024]{1,0:T(8,128)(2,1)S(1)}, bf16[1024,512]{1,0:T(8,128)(2,1)S(1)}, b...) custom-call(s32[12]{0:T(128)S(1)} %concatenate.17.scal, ...), custom_call_target="tpu_custom_call" | custom-call | flops 1024 | bytes 1024 | tf_op jit(solution)/shard_map/core/pallas_call | solution.py:703
  43.6 1.2 collective-permute-done.5.fother
  44.8 1.3 collective-permute-start.8
  46.1 1.3 collective-permute-start.7
  47.4 1.3 collective-permute-start.6
  48.7 3.7 %ffn_grad.2 = bf16[2048,512]{1,0:T(8,128)(2,1)S(1)} custom-call(s32[12]{0:T(128)S(1)} %concatenate.17.scal, bf16[1024,2048]{1,0:T(8,128)(2,1)S(1)} %get-tuple-element.136.act, bf16[1024,512]{1,0:T(8,128)(2,1)S(1)} %get-tuple-element.106.gl, bf16[1024,512]{1,0:T(8,128)(2,1)S(1)} %get-tuple-element.121.n2, bf16[1024,2048]{1,0:T(8,128)(2,1)S(1)} %get-tuple-element.127.dp), custom_call_target="tpu_custom_call" | custom-call | flops 1024 | bytes 1024 | tf_op jit(solution)/shard_map/ffn_grad/pallas_call | solution.py:703
  52.7 0.6 collective-permute-done.7.refs_1_
  53.5 3.7 %ffn_grad.3 = bf16[2048,512]{1,0:T(8,128)(2,1)S(1)} custom-call(s32[12]{0:T(128)S(1)} %concatenate.17.scal, bf16[1024,2048]{1,0:T(8,128)(2,1)S(1)} %get-tuple-element.136.act, bf16[1024,512]{1,0:T(8,128)(2,1)S(1)} %get-tuple-element.106.gl, bf16[1024,512]{1,0:T(8,128)(2,1)S(1)} %get-tuple-element.121.n2, bf16[1024,2048]{1,0:T(8,128)(2,1)S(1)} %get-tuple-element.127.dp), custom_call_target="tpu_custom_call" | custom-call | flops 30000001024 | bytes 1024 | tf_op jit(solution)/shard_map/ffn_grad/pallas_call | solution.py:703
  57.2 0.6 add_convert_fusion
  57.8 1.6 collective-permute-start.10
  59.4 3.7 %gates.1 = (bf16[1024,1024]{1,0:T(8,128)(2,1)S(1)}, bf16[1024,1024]{1,0:T(8,128)(2,1)S(1)}, bf16[32,512]{1,0:T(8,128)(2,1)S(1)}, f32[8,1024]{1,0:T(8,128)S(1)}) custom-call(s32[12]{0:T(128)S(1)} %concatenate.17.scal, bf16[1024,1024]{1,0:T(8,128)(2,1)S(1)} %get-tuple-element.116.dh, bf16[1024,1024]{1,0:T(8,128)(2,1)S(1)} %get-tuple-element.110.zl.zl_next.zl_before, ...), custom_call_target="tpu_custom_call" | custom-call | flops 1024 | bytes 1024 | tf_op jit(solution)/shard_map/gates/pallas_call | solution.py:703
  63.1 2.4 %gate_grad.2 = bf16[1536,512]{1,0:T(8,128)(2,1)S(1)} custom-call(s32[12]{0:T(128)S(1)} %concatenate.17.scal, bf16[1024,512]{1,0:T(8,128)(2,1)S(1)} %get-tuple-element.115.c, bf16[1024,1024]{1,0:T(8,128)(2,1)S(1)} %get-tuple-element.143.dkz, bf16[1024,1024]{1,0:T(8,128)(2,1)S(1)} %get-tuple-element.140.dkh, bf16[1024,1024]{1,0:T(8,128)(2,1)S(1)} %get-tuple-element.134.y, ...), custom_call_target="tpu_custom_call" | custom-call | flops 1024 | bytes 1024 | tf_op jit(solution)/shard_map/gate_grad/pallas_call | solution.py:703
  65.6 1.5 collective-permute-start.12
  67.1 5.7 %output.1 = bf16[8,128,512]{2,1,0:T(8,128)(2,1)} custom-call(f32[1024,512]{1,0:T(8,128)} %get-tuple-element.113.r1, bf16[1024,2048]{1,0:T(8,128)(2,1)S(1)} %get-tuple-element.136.act, bf16[256,256]{1,0:T(8,128)(2,1)S(1)} %copy-done.11, bf16[2048,512]{1,0:T(8,128)(2,1)S(1)} %copy-done.7), custom_call_target="tpu_custom_call" | custom-call | flops 1024 | bytes 1024 | tf_op jit(solution)/shard_map/output/pallas_call | solution.py:703
  72.7 1.3 add_convert_fusion.4
  74.0 1.5 collective-permute-start.14
  75.5 2.4 %gate_grad.3 = bf16[1536,512]{1,0:T(8,128)(2,1)S(1)} custom-call(s32[12]{0:T(128)S(1)} %concatenate.17.scal, bf16[1024,512]{1,0:T(8,128)(2,1)S(1)} %get-tuple-element.115.c, bf16[1024,1024]{1,0:T(8,128)(2,1)S(1)} %get-tuple-element.143.dkz, bf16[1024,1024]{1,0:T(8,128)(2,1)S(1)} %get-tuple-element.140.dkh, bf16[1024,1024]{1,0:T(8,128)(2,1)S(1)} %get-tuple-element.134.y, ...), custom_call_target="tpu_custom_call" | custom-call | flops 30000001024 | bytes 1024 | tf_op jit(solution)/shard_map/gate_grad/pallas_call | solution.py:703
  78.0 1.3 add_convert_fusion.2
  79.3 1.4 collective-permute-start.13
  80.8 1.6 copy-done.6
  82.4 10.2 %tail.1 = (bf16[8,128,512]{2,1,0:T(8,128)(2,1)}, f32[40,512]{1,0:T(8,128)S(1)}) custom-call(bf16[8,128,512]{2,1,0:T(8,128)(2,1)} %x.5, f32[1024,512]{1,0:T(8,128)} %get-tuple-element.137.dr1, bf16[1024,1024]{1,0:T(8,128)(2,1)S(1)} %copy-done.4, bf16[1024,1024]{1,0:T(8,128)(2,1)S(1)} %copy-done.6, bf16[256,256]{1,0:T(8,128)(2,1)} %constant.29.clone.perm.pm, ...), custom_call_target="tpu_custom_call" | custom-call | flops 1024 | bytes 1024 | tf_op jit(solution)/shard_map/tail/pallas_call | solution.py:703
  92.6 1.2 add_convert_fusion.8
  93.8 2.2 %collective-permute-start.16 = (bf16[256,512]{1,0:T(8,128)(2,1)S(1)}, bf16[256,512]{1,0:T(8,128)(2,1)S(1)}, u32[]{:S(2)}, u32[]{:S(2)}) collective-permute-start(bf16[256,512]{1,0:T(8,128)(2,1)S(1)} %get-tuple-element.212), channel_id=1, source_target_pairs={{0,8},{1,9},{2,10},{3,11},{4,20},{5,21},{6,22},{7,23},{8,0},{9,1},... | collective-permute-start | bytes 786440 | tf_op jit(solution)/shard_map/ppermute | solution.py:487
  96.0 1.3 add_convert_fusion.6
  97.4 1.2 collective-permute-start.15
  98.6 4.4 %collective-permute-done.16 = bf16[256,512]{1,0:T(8,128)(2,1)S(1)} collective-permute-done((bf16[256,512]{1,0:T(8,128)(2,1)S(1)}, bf16[256,512]{1,0:T(8,128)(2,1)S(1)}, u32[]{:S(2)}, u32[]{:S(2)}) %collective-permute-start.16) | collective-permute-done | bytes 262176 | tf_op jit(solution)/shard_map/ppermute | solution.py:487
  103.0 3.1 %collective-permute-start.18 = (bf16[128,512]{1,0:T(8,128)(2,1)S(1)}, bf16[128,512]{1,0:T(8,128)(2,1)S(1)}, u32[]{:S(2)}, u32[]{:S(2)}) collective-permute-start(bf16[128,512]{1,0:T(8,128)(2,1)S(1)} %add_convert_fusion.14), channel_id=1, source_target_pairs={{0,16},{1,17},{2,18},{3,19},{4,12},{5,13},{6,14},{7,15},{8,24},{9,... | collective-permute-start | bytes 393224 | tf_op jit(solution)/shard_map/ppermute | solution.py:487
  106.3 2.5 %collective-permute-start.17 = (bf16[192,512]{1,0:T(8,128)(2,1)S(1)}, bf16[192,512]{1,0:T(8,128)(2,1)S(1)}, u32[]{:S(2)}, u32[]{:S(2)}) collective-permute-start(bf16[192,512]{1,0:T(8,128)(2,1)S(1)} %get-tuple-element.213), channel_id=1, source_target_pairs={{0,8},{1,9},{2,10},{3,11},{4,20},{5,21},{6,22},{7,23},{8,0},{9,1},... | collective-permute-start | bytes 589832 | tf_op jit(solution)/shard_map/ppermute | solution.py:487
  108.8 0.5 collective-permute-done.18
  109.4 3.5 %collective-permute-start.20 = (bf16[128,512]{1,0:T(8,128)(2,1)S(1)}, bf16[128,512]{1,0:T(8,128)(2,1)S(1)}, u32[]{:S(2)}, u32[]{:S(2)}) collective-permute-start(bf16[128,512]{1,0:T(8,128)(2,1)S(1)} %add_convert_fusion.12.mine), channel_id=1, source_target_pairs={{0,16},{1,17},{2,18},{3,19},{4,12},{5,13},{6,14},{7,15},{8,24},{9,... | collective-permute-start | bytes 393224 | tf_op jit(solution)/shard_map/ppermute | solution.py:487
  112.9 3.7 %collective-permute-done.17 = bf16[192,512]{1,0:T(8,128)(2,1)S(1)} collective-permute-done((bf16[192,512]{1,0:T(8,128)(2,1)S(1)}, bf16[192,512]{1,0:T(8,128)(2,1)S(1)}, u32[]{:S(2)}, u32[]{:S(2)}) %collective-permute-start.17) | collective-permute-done | bytes 196640 | tf_op jit(solution)/shard_map/ppermute | solution.py:487
  116.7 0.5 collective-permute-start.19
  117.2 9.4 %collective-permute-start.23 = (bf16[256,512]{1,0:T(8,128)(2,1)S(1)}, bf16[256,512]{1,0:T(8,128)(2,1)S(1)}, u32[]{:S(2)}, u32[]{:S(2)}) collective-permute-start(bf16[256,512]{1,0:T(8,128)(2,1)S(1)} %chain.3.mine), channel_id=1, source_target_pairs={{0,8},{1,9},{2,10},{3,11},{4,20},{5,21},{6,22},{7,23},{8,0},{9,1},... | collective-permute-start | bytes 786440 | tf_op jit(solution)/shard_map/ppermute | solution.py:487
  126.5 1.0 collective-permute-done.19
  127.6 2.4 %collective-permute-start.21 = (bf16[112,512]{1,0:T(8,128)(2,1)S(1)}, bf16[112,512]{1,0:T(8,128)(2,1)S(1)}, u32[]{:S(2)}, u32[]{:S(2)}) collective-permute-start(bf16[112,512]{1,0:T(8,128)(2,1)S(1)} %pad_maximum_fusion.mine), channel_id=1, source_target_pairs={{0,16},{1,17},{2,18},{3,19},{4,12},{5,13},{6,14},{7,15},{8,24},{9,... | collective-permute-start | bytes 344072 | tf_op jit(solution)/shard_map/ppermute | solution.py:487
  130.0 5.6 %collective-permute-done.21.recv = bf16[112,512]{1,0:T(8,128)(2,1)S(1)} collective-permute-done((bf16[112,512]{1,0:T(8,128)(2,1)S(1)}, bf16[112,512]{1,0:T(8,128)(2,1)S(1)}, u32[]{:S(2)}, u32[]{:S(2)}) %collective-permute-start.21) | collective-permute-done | bytes 114720 | tf_op jit(solution)/shard_map/ppermute | solution.py:487
  135.8 1.4 collective-permute-start.25
  137.2 4.4 %collective-permute-done.22.recv = bf16[208,512]{1,0:T(8,128)(2,1)S(1)} collective-permute-done((bf16[208,512]{1,0:T(8,128)(2,1)S(1)}, bf16[208,512]{1,0:T(8,128)(2,1)S(1)}, u32[]{:S(2)}, u32[]{:S(2)}) %collective-permute-start.22) | collective-permute-done | bytes 213024 | tf_op jit(solution)/shard_map/ppermute | solution.py:487
  141.6 1.3 collective-permute-start.24
  142.9 2.1 %collective-permute-done.25.recv = bf16[512,512]{1,0:T(8,128)(2,1)S(1)} collective-permute-done((bf16[512,512]{1,0:T(8,128)(2,1)S(1)}, bf16[512,512]{1,0:T(8,128)(2,1)S(1)}, u32[]{:S(2)}, u32[]{:S(2)}) %collective-permute-start.25) | collective-permute-done | bytes 524320 | tf_op jit(solution)/shard_map/ppermute | solution.py:487
  145.2 1.4 collective-permute-start.28
  146.7 4.3 %collective-permute-done.24.recv = bf16[400,512]{1,0:T(8,128)(2,1)S(1)} collective-permute-done((bf16[400,512]{1,0:T(8,128)(2,1)S(1)}, bf16[400,512]{1,0:T(8,128)(2,1)S(1)}, u32[]{:S(2)}, u32[]{:S(2)}) %collective-permute-start.24) | collective-permute-done | bytes 409632 | tf_op jit(solution)/shard_map/ppermute | solution.py:487
  150.9 1.0 join.5
  151.9 1.4 collective-permute-start.26
  153.3 2.0 %spread_ffn.4 = (f32[2048,512]{1,0:T(8,128)}, f32[512,2048]{1,0:T(8,128)}) custom-call(s32[12]{0:T(128)S(1)} %concatenate.17.scal, bf16[1024,512]{1,0:T(8,128)(2,1)S(1)} %chain.5.src), custom_call_target="tpu_custom_call" | custom-call | flops 30000001024 | bytes 1024 | tf_op jit(solution)/shard_map/spread_ffn/pallas_call | solution.py:440
  155.3 2.0 %spread_ffn.5 = (f32[2048,512]{1,0:T(8,128)}, f32[512,2048]{1,0:T(8,128)}) custom-call(s32[12]{0:T(128)S(1)} %concatenate.17.scal, bf16[1024,512]{1,0:T(8,128)(2,1)S(1)} %collective-permute-done.29.src, f32[2048,512]{1,0:T(8,128)} %get-tuple-element.167.refs_0_, f32[512,2048]{1,0:T(8,128)} %get-tuple-element.169.refs_1_), custom_call_target="tpu_custom_call", output_to_operand_aliasing={{0}: (2, {}), {1}: (3, {})} | custom-call | flops 30000001024 | bytes 1024 | tf_op jit(solution)/shard_map/spread_ffn/pallas_call | solution.py:440
  157.3 2.8 %collective-permute-done.28.src = bf16[1024,512]{1,0:T(8,128)(2,1)S(1)} collective-permute-done((bf16[1024,512]{1,0:T(8,128)(2,1)S(1)}, bf16[1024,512]{1,0:T(8,128)(2,1)S(1)}, u32[]{:S(2)}, u32[]{:S(2)}) %collective-permute-start.28) | collective-permute-done | bytes 1048608 | tf_op jit(solution)/shard_map/ppermute | solution.py:487
  160.1 1.0 collective-permute-start.30
  161.1 2.0 %spread_ffn.6 = (f32[2048,512]{1,0:T(8,128)}, f32[512,2048]{1,0:T(8,128)}) custom-call(s32[12]{0:T(128)S(1)} %concatenate.17.scal, bf16[1024,512]{1,0:T(8,128)(2,1)S(1)} %collective-permute-done.28.src, f32[2048,512]{1,0:T(8,128)} %get-tuple-element.170.refs_0_, f32[512,2048]{1,0:T(8,128)} %get-tuple-element.173.refs_1_), custom_call_target="tpu_custom_call", output_to_operand_aliasing={{0}: (2, {}), {1}: (3, {})} | custom-call | flops 30000001024 | bytes 1024 | tf_op jit(solution)/shard_map/spread_ffn/pallas_call | solution.py:440
  163.1 2.9 %spread_gates.3 = (f32[512,1024]{1,0:T(8,128)}, f32[512,1024]{1,0:T(8,128)}, f32[1024,512]{1,0:T(8,128)}) custom-call(s32[12]{0:T(128)S(1)} %concatenate.17.scal, bf16[784,512]{1,0:T(8,128)(2,1)} %get-tuple-element.175.src), custom_call_target="tpu_custom_call" | custom-call | flops 30000001024 | bytes 1024 | tf_op jit(solution)/shard_map/spread_gates/pallas_call | solution.py:440
  166.0 2.0 %spread_ffn.7 = (f32[2048,512]{1,0:T(8,128)}, f32[512,2048]{1,0:T(8,128)}) custom-call(s32[12]{0:T(128)S(1)} %concatenate.17.scal, bf16[1024,512]{1,0:T(8,128)(2,1)S(1)} %collective-permute-done.30.src, f32[2048,512]{1,0:T(8,128)} %get-tuple-element.174.refs_0_, f32[512,2048]{1,0:T(8,128)} %get-tuple-element.178.refs_1_), custom_call_target="tpu_custom_call", output_to_operand_aliasing={{0}: (2, {}), {1}: (3, {})} | custom-call | flops 30000001024 | bytes 1024 | tf_op jit(solution)/shard_map/spread_ffn/pallas_call | solution.py:440
  168.0 2.9 %spread_gates.4 = (f32[512,1024]{1,0:T(8,128)}, f32[512,1024]{1,0:T(8,128)}, f32[1024,512]{1,0:T(8,128)}) custom-call(s32[12]{0:T(128)S(1)} %concatenate.17.scal, bf16[784,512]{1,0:T(8,128)(2,1)} %collective-permute-done.27.src.theirs, f32[512,1024]{1,0:T(8,128)} %get-tuple-element.176.refs_0_, ...), custom_call_target="tpu_custom_call", output_to_operand_aliasing={{0}: (2, {}), {1}: (3, {}), {2}: (4, {})} | custom-call | flops 30000001024 | bytes 1024 | tf_op jit(solution)/shard_map/spread_gates/pallas_call | solution.py:440
  170.9 2.9 %spread_gates.5 = (f32[512,1024]{1,0:T(8,128)}, f32[512,1024]{1,0:T(8,128)}, f32[1024,512]{1,0:T(8,128)}) custom-call(s32[12]{0:T(128)S(1)} %concatenate.17.scal, bf16[784,512]{1,0:T(8,128)(2,1)} %collective-permute-done.26.src.rest, f32[512,1024]{1,0:T(8,128)} %get-tuple-element.183.refs_0_, ...), custom_call_target="tpu_custom_call", output_to_operand_aliasing={{0}: (2, {}), {1}: (3, {}), {2}: (4, {})} | custom-call | flops 30000001024 | bytes 1024 | tf_op jit(solution)/shard_map/spread_gates/pallas_call | solution.py:440
  173.7 2.5 %spread_last.1 = (f32[512,1024]{1,0:T(8,128)}, f32[512,1024]{1,0:T(8,128)}, f32[1024,512]{1,0:T(8,128)}, f32[1,512]{1,0:T(1,128)}, f32[4,512]{1,0:T(4,128)}, /*index=5*/f32[1,512]{1,0:T(1,128)}, f32[1,1024]{1,0:T(1,128)}) custom-call(s32[12]{0:T(128)S(1)} %concatenate.17.scal, ...), custom_call_target="tpu_custom_call", output_to_operand_aliasing={{0}: (5, {}), {1}: (6, {}), {2}: (7, {})} | custom-call | flops 30000001024 | bytes 1024 | tf_op jit(solution)/shard_map/spread_last/pallas_call | solution.py:418
  (81 shorter events, 1.6 us)
Async XLA Ops:
  0.6 6.5 %copy-start.14 = (s32[8]{0:T(128)S(1)}, s32[8]{0:T(128)}, u32[]{:S(2)}) copy-start(s32[8]{0:T(128)} %param.15) | copy-start | bytes 100
  0.7 6.6 %copy-start.2 = (bf16[512,1024]{1,0:T(8,128)(2,1)S(1)}, bf16[512,1024]{1,0:T(8,128)(2,1)}, u32[]{:S(2)}) copy-start(bf16[512,1024]{1,0:T(8,128)(2,1)} %wc.3) | copy-start | bytes 3145732
  0.7 6.6 %copy-start.1 = (bf16[512,1024]{1,0:T(8,128)(2,1)S(1)}, bf16[512,1024]{1,0:T(8,128)(2,1)}, u32[]{:S(2)}) copy-start(bf16[512,1024]{1,0:T(8,128)(2,1)} %wg.3) | copy-start | bytes 3145732
  1.7 5.5 %collective-permute-start = (bf16[24,512]{1,0:T(8,128)(2,1)S(1)}, bf16[24,512]{1,0:T(8,128)(2,1)S(1)}, u32[]{:S(2)}, u32[]{:S(2)}) collective-permute-start(bf16[24,512]{1,0:T(8,128)(2,1)S(1)} %bitcast.19), channel_id=1, source_target_pairs={{0,4},{4,8},{8,12},{12,16},{16,20},{20,24},{24,28},{1,5},{5,9},{9,... | collective-permute-start | bytes 73736 | tf_op jit(solution)/shard_map/ppermute | solution.py:483
  7.1 18.5 %copy-start.8 = (bf16[256,256]{1,0:T(8,128)(2,1)S(1)}, bf16[256,256]{1,0:T(8,128)(2,1)}, u32[]{:S(2)}) copy-start(bf16[256,256]{1,0:T(8,128)(2,1)} %constant.29.clone.perm.pm) | copy-start | bytes 393220
  7.2 18.4 %copy-start.7 = (bf16[2048,512]{1,0:T(8,128)(2,1)S(1)}, bf16[2048,512]{1,0:T(8,128)(2,1)}, u32[]{:S(2)}) copy-start(bf16[2048,512]{1,0:T(8,128)(2,1)} %wd.3) | copy-start | bytes 6291460
  7.2 18.4 %copy-start.10 = (bf16[8,128,512]{2,1,0:T(8,128)(2,1)S(1)}, bf16[8,128,512]{2,1,0:T(8,128)(2,1)}, u32[]{:S(2)}) copy-start(bf16[8,128,512]{2,1,0:T(8,128)(2,1)} %g.1) | copy-start | bytes 3145732
  13.8 15.4 %copy-start = (bf16[8,128,512]{2,1,0:T(8,128)(2,1)S(1)}, bf16[8,128,512]{2,1,0:T(8,128)(2,1)}, u32[]{:S(2)}) copy-start(bf16[8,128,512]{2,1,0:T(8,128)(2,1)} %x.5) | copy-start | bytes 3145732
  13.8 15.4 %copy-start.9 = (bf16[512,2048]{1,0:T(8,128)(2,1)S(1)}, bf16[512,2048]{1,0:T(8,128)(2,1)}, u32[]{:S(2)}) copy-start(bf16[512,2048]{1,0:T(8,128)(2,1)} %refs_5_.1) | copy-start | bytes 6291460
  13.8 15.4 %copy-start.12 = (f32[512]{0:T(512)S(1)}, f32[512]{0:T(512)}, u32[]{:S(2)}) copy-start(f32[512]{0:T(512)} %param.22) | copy-start | bytes 6148
  13.8 3.7 %collective-permute-start.1 = (f32[16,1024]{1,0:T(8,128)S(1)}, f32[16,1024]{1,0:T(8,128)S(1)}, u32[]{:S(2)}, u32[]{:S(2)}) collective-permute-start(f32[16,1024]{1,0:T(8,128)S(1)} %get-tuple-element.112), channel_id=1, source_target_pairs={{0,4},{1,5},{2,6},{3,7},{4,0},{5,1},{6,2},{7,3},{8,12},{9,13},{10,... | collective-permute-start | bytes 196616 | tf_op jit(solution)/shard_map/ppermute | solution.py:487
  17.5 11.6 %collective-permute-start.4 = (bf16[16,1024]{1,0:T(8,128)(2,1)S(1)}, bf16[16,1024]{1,0:T(8,128)(2,1)S(1)}, u32[]{:S(2)}, u32[]{:S(2)}) collective-permute-start(bf16[16,1024]{1,0:T(8,128)(2,1)S(1)} %pad_maximum_fusion.2), channel_id=1, source_target_pairs={{0,24},{4,28},{1,25},{5,29},{2,26},{6,30},{3,27},{7,31}} | collective-permute-start | bytes 98312 | tf_op jit(solution)/shard_map/ppermute | solution.py:483
  21.8 7.4 %collective-permute-start.3 = (bf16[16,1024]{1,0:T(8,128)(2,1)S(1)}, bf16[16,1024]{1,0:T(8,128)(2,1)S(1)}, u32[]{:S(2)}, u32[]{:S(2)}) collective-permute-start(bf16[16,1024]{1,0:T(8,128)(2,1)S(1)} %pad_maximum_fusion.2), channel_id=1, source_target_pairs={{0,16},{4,20},{8,24},{12,28},{1,17},{5,21},{9,25},{13,29},{2,18},{... | collective-permute-start | bytes 98312 | tf_op jit(solution)/shard_map/ppermute | solution.py:483
  23.1 6.1 %collective-permute-start.2 = (bf16[16,1024]{1,0:T(8,128)(2,1)S(1)}, bf16[16,1024]{1,0:T(8,128)(2,1)S(1)}, u32[]{:S(2)}, u32[]{:S(2)}) collective-permute-start(bf16[16,1024]{1,0:T(8,128)(2,1)S(1)} %pad_maximum_fusion.2), channel_id=1, source_target_pairs={{0,8},{4,12},{8,16},{12,20},{16,24},{20,28},{1,9},{5,13},{9,17},{1... | collective-permute-start | bytes 98312 | tf_op jit(solution)/shard_map/ppermute | solution.py:483
  43.6 1.2 collective-permute-start.5
  44.8 7.8 %collective-permute-start.8 = (bf16[16,1024]{1,0:T(8,128)(2,1)S(1)}, bf16[16,1024]{1,0:T(8,128)(2,1)S(1)}, u32[]{:S(2)}, u32[]{:S(2)}) collective-permute-start(bf16[16,1024]{1,0:T(8,128)(2,1)S(1)} %pad_maximum_fusion.1), channel_id=1, source_target_pairs={{24,0},{28,4},{25,1},{29,5},{26,2},{30,6},{27,3},{31,7}} | collective-permute-start | bytes 98312 | tf_op jit(solution)/shard_map/ppermute | solution.py:483
  46.1 7.1 %collective-permute-start.7 = (bf16[16,1024]{1,0:T(8,128)(2,1)S(1)}, bf16[16,1024]{1,0:T(8,128)(2,1)S(1)}, u32[]{:S(2)}, u32[]{:S(2)}) collective-permute-start(bf16[16,1024]{1,0:T(8,128)(2,1)S(1)} %pad_maximum_fusion.1), channel_id=1, source_target_pairs={{16,0},{20,4},{24,8},{28,12},{17,1},{21,5},{25,9},{29,13},{18,2},{... | collective-permute-start | bytes 98312 | tf_op jit(solution)/shard_map/ppermute | solution.py:483
  47.4 6.1 %collective-permute-start.6 = (bf16[16,1024]{1,0:T(8,128)(2,1)S(1)}, bf16[16,1024]{1,0:T(8,128)(2,1)S(1)}, u32[]{:S(2)}, u32[]{:S(2)}) collective-permute-start(bf16[16,1024]{1,0:T(8,128)(2,1)S(1)} %pad_maximum_fusion.1), channel_id=1, source_target_pairs={{8,0},{12,4},{16,8},{20,12},{24,16},{28,20},{9,1},{13,5},{17,9},{2... | collective-permute-start | bytes 98312 | tf_op jit(solution)/shard_map/ppermute | solution.py:483
  52.4 4.7 %collective-permute-start.9 = (bf16[2048,512]{1,0:T(8,128)(2,1)S(1)}, bf16[2048,512]{1,0:T(8,128)(2,1)S(1)}, u32[]{:S(2)}, u32[]{:S(2)}) collective-permute-start(bf16[2048,512]{1,0:T(8,128)(2,1)S(1)} %ffn_grad.2), channel_id=1, source_target_pairs={{0,4},{1,5},{2,6},{3,7},{4,0},{5,1},{6,2},{7,3},{8,12},{9,13},{10,... | collective-permute-start | bytes 6291464 | tf_op jit(solution)/shard_map/ppermute | solution.py:487
  57.8 14.9 %collective-permute-start.10 = (bf16[1024,512]{1,0:T(8,128)(2,1)S(1)}, bf16[1024,512]{1,0:T(8,128)(2,1)S(1)}, u32[]{:S(2)}, u32[]{:S(2)}) collective-permute-start(bf16[1024,512]{1,0:T(8,128)(2,1)S(1)} %get-tuple-element.204.refs_5_), channel_id=1, source_target_pairs={{0,1},{1,0},{2,3},{3,2},{4,6},{5,7},{6,4},{7,5},{8,9},{9,8},{10,11... | collective-permute-start | bytes 3145736 | tf_op jit(solution)/shard_map/ppermute | solution.py:487
  63.1 12.5 %copy-start.3 = (bf16[1024,1024]{1,0:T(8,128)(2,1)}, bf16[1024,1024]{1,0:T(8,128)(2,1)S(1)}, u32[]{:S(2)}) copy-start(bf16[1024,1024]{1,0:T(8,128)(2,1)S(1)} %get-tuple-element.143.dkz) | copy-start | bytes 6291460
  63.1 12.4 %copy-start.5 = (bf16[1024,1024]{1,0:T(8,128)(2,1)}, bf16[1024,1024]{1,0:T(8,128)(2,1)S(1)}, u32[]{:S(2)}) copy-start(bf16[1024,1024]{1,0:T(8,128)(2,1)S(1)} %get-tuple-element.140.dkh) | copy-start | bytes 6291460
  63.1 4.0 %copy-start.11 = (bf16[256,256]{1,0:T(8,128)(2,1)S(1)}, bf16[256,256]{1,0:T(8,128)(2,1)}, u32[]{:S(2)}) copy-start(bf16[256,256]{1,0:T(8,128)(2,1)} %constant.30.clone.perm.back_pm) | copy-start | bytes 393220
  65.5 12.5 %collective-permute-start.11 = (bf16[1536,512]{1,0:T(8,128)(2,1)S(1)}, bf16[1536,512]{1,0:T(8,128)(2,1)S(1)}, u32[]{:S(2)}, u32[]{:S(2)}) collective-permute-start(bf16[1536,512]{1,0:T(8,128)(2,1)S(1)} %gate_grad.2), channel_id=1, source_target_pairs={{0,4},{1,5},{2,6},{3,7},{4,0},{5,1},{6,2},{7,3},{8,12},{9,13},{10,... | collective-permute-start | bytes 4718600 | tf_op jit(solution)/shard_map/ppermute | solution.py:487
  65.6 12.4 %collective-permute-start.12 = (bf16[24,512]{1,0:T(8,128)(2,1)S(1)}, bf16[24,512]{1,0:T(8,128)(2,1)S(1)}, u32[]{:S(2)}, u32[]{:S(2)}) collective-permute-start(bf16[24,512]{1,0:T(8,128)(2,1)S(1)} %slice.134), channel_id=1, source_target_pairs={{4,0},{8,4},{12,8},{16,12},{20,16},{24,20},{28,24},{5,1},{9,5},{13... | collective-permute-start | bytes 73736 | tf_op jit(solution)/shard_map/ppermute | solution.py:483
  74.0 18.6 %collective-permute-start.14 = (bf16[512,512]{1,0:T(8,128)(2,1)}, bf16[512,512]{1,0:T(8,128)(2,1)}, u32[]{:S(2)}, u32[]{:S(2)}) collective-permute-start(bf16[512,512]{1,0:T(8,128)(2,1)} %get-tuple-element.208), channel_id=1, source_target_pairs={{0,2},{1,3},{2,0},{3,1},{4,5},{5,4},{6,7},{7,6},{8,10},{9,11},{10,... | collective-permute-start | bytes 1572872 | tf_op jit(solution)/shard_map/ppermute | solution.py:487
  77.9 2.8 %copy-start.4 = (bf16[1024,1024]{1,0:T(8,128)(2,1)S(1)}, bf16[1024,1024]{1,0:T(8,128)(2,1)}, u32[]{:S(2)}) copy-start(bf16[1024,1024]{1,0:T(8,128)(2,1)} %copy-done.3) | copy-start | bytes 6291460
  79.3 16.7 %collective-permute-start.13 = (bf16[768,512]{1,0:T(8,128)(2,1)}, bf16[768,512]{1,0:T(8,128)(2,1)}, u32[]{:S(2)}, u32[]{:S(2)}) collective-permute-start(bf16[768,512]{1,0:T(8,128)(2,1)} %get-tuple-element.206), channel_id=1, source_target_pairs={{0,1},{1,0},{2,3},{3,2},{4,6},{5,7},{6,4},{7,5},{8,9},{9,8},{10,11... | collective-permute-start | bytes 2359304 | tf_op jit(solution)/shard_map/ppermute | solution.py:487
  80.8 1.6 copy-start.6
  82.4 10.2 %copy-start.13 = (bf16[512,512]{1,0:T(8,128)(2,1)S(1)}, bf16[512,512]{1,0:T(8,128)(2,1)}, u32[]{:S(2)}) copy-start(bf16[512,512]{1,0:T(8,128)(2,1)} %get-tuple-element.207) | copy-start | bytes 1572868
  93.8 9.2 %collective-permute-start.16 = (bf16[256,512]{1,0:T(8,128)(2,1)S(1)}, bf16[256,512]{1,0:T(8,128)(2,1)S(1)}, u32[]{:S(2)}, u32[]{:S(2)}) collective-permute-start(bf16[256,512]{1,0:T(8,128)(2,1)S(1)} %get-tuple-element.212), channel_id=1, source_target_pairs={{0,8},{1,9},{2,10},{3,11},{4,20},{5,21},{6,22},{7,23},{8,0},{9,1},... | collective-permute-start | bytes 786440 | tf_op jit(solution)/shard_map/ppermute | solution.py:487
  97.4 8.8 %collective-permute-start.15 = (bf16[384,512]{1,0:T(8,128)(2,1)S(1)}, bf16[384,512]{1,0:T(8,128)(2,1)S(1)}, u32[]{:S(2)}, u32[]{:S(2)}) collective-permute-start(bf16[384,512]{1,0:T(8,128)(2,1)S(1)} %get-tuple-element.209), channel_id=1, source_target_pairs={{0,2},{1,3},{2,0},{3,1},{4,5},{5,4},{6,7},{7,6},{8,10},{9,11},{10,... | collective-permute-start | bytes 1179656 | tf_op jit(solution)/shard_map/ppermute | solution.py:487
  103.0 6.3 %collective-permute-start.18 = (bf16[128,512]{1,0:T(8,128)(2,1)S(1)}, bf16[128,512]{1,0:T(8,128)(2,1)S(1)}, u32[]{:S(2)}, u32[]{:S(2)}) collective-permute-start(bf16[128,512]{1,0:T(8,128)(2,1)S(1)} %add_convert_fusion.14), channel_id=1, source_target_pairs={{0,16},{1,17},{2,18},{3,19},{4,12},{5,13},{6,14},{7,15},{8,24},{9,... | collective-permute-start | bytes 393224 | tf_op jit(solution)/shard_map/ppermute | solution.py:487
  106.3 10.3 %collective-permute-start.17 = (bf16[192,512]{1,0:T(8,128)(2,1)S(1)}, bf16[192,512]{1,0:T(8,128)(2,1)S(1)}, u32[]{:S(2)}, u32[]{:S(2)}) collective-permute-start(bf16[192,512]{1,0:T(8,128)(2,1)S(1)} %get-tuple-element.213), channel_id=1, source_target_pairs={{0,8},{1,9},{2,10},{3,11},{4,20},{5,21},{6,22},{7,23},{8,0},{9,1},... | collective-permute-start | bytes 589832 | tf_op jit(solution)/shard_map/ppermute | solution.py:487
  109.4 7.8 %collective-permute-start.20 = (bf16[128,512]{1,0:T(8,128)(2,1)S(1)}, bf16[128,512]{1,0:T(8,128)(2,1)S(1)}, u32[]{:S(2)}, u32[]{:S(2)}) collective-permute-start(bf16[128,512]{1,0:T(8,128)(2,1)S(1)} %add_convert_fusion.12.mine), channel_id=1, source_target_pairs={{0,16},{1,17},{2,18},{3,19},{4,12},{5,13},{6,14},{7,15},{8,24},{9,... | collective-permute-start | bytes 393224 | tf_op jit(solution)/shard_map/ppermute | solution.py:487
  116.7 10.9 %collective-permute-start.19 = (bf16[96,512]{1,0:T(8,128)(2,1)S(1)}, bf16[96,512]{1,0:T(8,128)(2,1)S(1)}, u32[]{:S(2)}, u32[]{:S(2)}) collective-permute-start(bf16[96,512]{1,0:T(8,128)(2,1)S(1)} %add_convert_fusion.16), channel_id=1, source_target_pairs={{0,16},{1,17},{2,18},{3,19},{4,12},{5,13},{6,14},{7,15},{8,24},{9,... | collective-permute-start | bytes 294920 | tf_op jit(solution)/shard_map/ppermute | solution.py:487
  117.2 18.6 %collective-permute-start.23 = (bf16[256,512]{1,0:T(8,128)(2,1)S(1)}, bf16[256,512]{1,0:T(8,128)(2,1)S(1)}, u32[]{:S(2)}, u32[]{:S(2)}) collective-permute-start(bf16[256,512]{1,0:T(8,128)(2,1)S(1)} %chain.3.mine), channel_id=1, source_target_pairs={{0,8},{1,9},{2,10},{3,11},{4,20},{5,21},{6,22},{7,23},{8,0},{9,1},... | collective-permute-start | bytes 786440 | tf_op jit(solution)/shard_map/ppermute | solution.py:487
  127.6 8.0 %collective-permute-start.21 = (bf16[112,512]{1,0:T(8,128)(2,1)S(1)}, bf16[112,512]{1,0:T(8,128)(2,1)S(1)}, u32[]{:S(2)}, u32[]{:S(2)}) collective-permute-start(bf16[112,512]{1,0:T(8,128)(2,1)S(1)} %pad_maximum_fusion.mine), channel_id=1, source_target_pairs={{0,16},{1,17},{2,18},{3,19},{4,12},{5,13},{6,14},{7,15},{8,24},{9,... | collective-permute-start | bytes 344072 | tf_op jit(solution)/shard_map/ppermute | solution.py:487
  135.7 5.9 %collective-permute-start.22 = (bf16[208,512]{1,0:T(8,128)(2,1)S(1)}, bf16[208,512]{1,0:T(8,128)(2,1)S(1)}, u32[]{:S(2)}, u32[]{:S(2)}) collective-permute-start(bf16[208,512]{1,0:T(8,128)(2,1)S(1)} %get-tuple-element.157.mine), channel_id=1, source_target_pairs={{0,8},{1,9},{2,10},{3,11},{4,20},{5,21},{6,22},{7,23},{8,0},{9,1},... | collective-permute-start | bytes 638984 | tf_op jit(solution)/shard_map/ppermute | solution.py:487
  135.8 9.2 %collective-permute-start.25 = (bf16[512,512]{1,0:T(8,128)(2,1)S(1)}, bf16[512,512]{1,0:T(8,128)(2,1)S(1)}, u32[]{:S(2)}, u32[]{:S(2)}) collective-permute-start(bf16[512,512]{1,0:T(8,128)(2,1)S(1)} %chain.4.mine), channel_id=1, source_target_pairs={{0,2},{1,3},{2,0},{3,1},{4,5},{5,4},{6,7},{7,6},{8,10},{9,11},{10,... | collective-permute-start | bytes 1572872 | tf_op jit(solution)/shard_map/ppermute | solution.py:487
  141.6 9.3 %collective-permute-start.24 = (bf16[400,512]{1,0:T(8,128)(2,1)S(1)}, bf16[400,512]{1,0:T(8,128)(2,1)S(1)}, u32[]{:S(2)}, u32[]{:S(2)}) collective-permute-start(bf16[400,512]{1,0:T(8,128)(2,1)S(1)} %get-tuple-element.161.mine), channel_id=1, source_target_pairs={{0,2},{1,3},{2,0},{3,1},{4,5},{5,4},{6,7},{7,6},{8,10},{9,11},{10,... | collective-permute-start | bytes 1228808 | tf_op jit(solution)/shard_map/ppermute | solution.py:487
  145.2 10.1 %collective-permute-start.29 = (bf16[1024,512]{1,0:T(8,128)(2,1)S(1)}, bf16[1024,512]{1,0:T(8,128)(2,1)S(1)}, u32[]{:S(2)}, u32[]{:S(2)}) collective-permute-start(bf16[1024,512]{1,0:T(8,128)(2,1)S(1)} %chain.5.src), channel_id=1, source_target_pairs={{0,4},{1,5},{2,6},{3,7},{4,0},{5,1},{6,2},{7,3},{8,12},{9,13},{10,... | collective-permute-start | bytes 3145736 | tf_op jit(solution)/shard_map/ppermute | solution.py:487
  145.2 14.9 %collective-permute-start.28 = (bf16[1024,512]{1,0:T(8,128)(2,1)S(1)}, bf16[1024,512]{1,0:T(8,128)(2,1)S(1)}, u32[]{:S(2)}, u32[]{:S(2)}) collective-permute-start(bf16[1024,512]{1,0:T(8,128)(2,1)S(1)} %chain.5.src), channel_id=1, source_target_pairs={{0,1},{1,0},{2,3},{3,2},{4,6},{5,7},{6,4},{7,5},{8,9},{9,8},{10,11... | collective-permute-start | bytes 3145736 | tf_op jit(solution)/shard_map/ppermute | solution.py:487
  151.9 16.1 %collective-permute-start.27 = (bf16[784,512]{1,0:T(8,128)(2,1)}, bf16[784,512]{1,0:T(8,128)(2,1)}, u32[]{:S(2)}, u32[]{:S(2)}) collective-permute-start(bf16[784,512]{1,0:T(8,128)(2,1)} %get-tuple-element.175.src), channel_id=1, source_target_pairs={{0,4},{1,5},{2,6},{3,7},{4,0},{5,1},{6,2},{7,3},{8,12},{9,13},{10,... | collective-permute-start | bytes 2408456 | tf_op jit(solution)/shard_map/ppermute | solution.py:487
  151.9 18.9 %collective-permute-start.26 = (bf16[784,512]{1,0:T(8,128)(2,1)}, bf16[784,512]{1,0:T(8,128)(2,1)}, u32[]{:S(2)}, u32[]{:S(2)}) collective-permute-start(bf16[784,512]{1,0:T(8,128)(2,1)} %get-tuple-element.175.src), channel_id=1, source_target_pairs={{0,1},{1,0},{2,3},{3,2},{4,6},{5,7},{6,4},{7,5},{8,9},{9,8},{10,11... | collective-permute-start | bytes 2408456 | tf_op jit(solution)/shard_map/ppermute | solution.py:487
  160.1 5.9 %collective-permute-start.30 = (bf16[1024,512]{1,0:T(8,128)(2,1)S(1)}, bf16[1024,512]{1,0:T(8,128)(2,1)S(1)}, u32[]{:S(2)}, u32[]{:S(2)}) collective-permute-start(bf16[1024,512]{1,0:T(8,128)(2,1)S(1)} %collective-permute-done.28.src), channel_id=1, source_target_pairs={{0,4},{1,5},{2,6},{3,7},{4,0},{5,1},{6,2},{7,3},{8,12},{9,13},{10,... | collective-permute-start | bytes 3145736 | tf_op jit(solution)/shard_map/ppermute | solution.py:487
  170.8 2.9 %collective-permute-start.31 = (bf16[784,512]{1,0:T(8,128)(2,1)}, bf16[784,512]{1,0:T(8,128)(2,1)S(1)}, u32[]{:S(2)}, u32[]{:S(2)}) collective-permute-start(bf16[784,512]{1,0:T(8,128)(2,1)} %collective-permute-done.26.src.rest), channel_id=1, source_target_pairs={{0,4},{1,5},{2,6},{3,7},{4,0},{5,1},{6,2},{7,3},{8,12},{9,13},{10,... | collective-permute-start | bytes 2408456 | tf_op jit(solution)/shard_map/ppermute | solution.py:487
where the time goes:
time: 177 us; the launch traced here: 176 us
  Pallas kernels  79.4 us (45%)
  starting transfers between devices  54.8 us (31%)
  waiting for transfers between devices  31.9 us (18%)
  other arithmetic  6.12 us (3%)
  local copies, waits for them, and re-layouts  2.79 us (2%)
    pallas_call x11, Pallas kernels, call(): pl.pallas_call(kernel, grid_spec=spec, out_shape=[o[0] for o in outs], co...  59.2 us
    ppermute x24, starting transfers between devices, flat_permute(): return lax.ppermute(value, ('seq', 'row'), pairs)  39 us
    ppermute x24, waiting for transfers between devices, flat_permute(): return lax.ppermute(value, ('seq', 'row'), pairs)  31.1 us
    pallas_call x7, Pallas kernels, spread(): pl.pallas_call(functools.partial(spread_kernel, piece=piece, plan=plan, m...  16.6 us
    ppermute x8, starting transfers between devices, passed_along(): lax.ppermute(value, axis, [(source, source + steps) for source in range(l...  15.7 us
    convert_element_type x10, other arithmetic, added(): return (a.astype(f32) + b.astype(f32)).astype(bf16)  5.98 us
  transfers between devices with their start and end apart: 32, of which 13 were waited for; matrix products, arithmetic and copies ran while one was open for 3% of the time, Pallas kernels for 32%

commit v1 on v0

--- a/solution.py
+++ b/solution.py
@@ -427,7 +427,7 @@
         out_shape=[pltpu.HBM(dims, f32) for dims in shapes] + [shape(dims) for dims in small],
         input_output_aliases={5 + k: k for k in range(len(held))},
         compiler_params=params(16),
-        cost_estimate=MUCH,
+        cost_estimate=SOME,
         name="spread_last",
     )(scal, src, chunk.ride, chunk.rest, chunk.theirs, *held)
 
@@ -448,7 +448,7 @@
         out_shape=[pltpu.HBM(dims, f32) for dims in shapes],
         input_output_aliases={2 + k: k for k in range(count)},
         compiler_params=params(16),
-        cost_estimate=MUCH,
+        cost_estimate=SOME,
         name=name,
     )(scal, src, *held)
 
@@ -465,6 +465,7 @@
 
 LITTLE = pl.CostEstimate(flops=1024, bytes_accessed=1024, transcendentals=0)
 MUCH = pl.CostEstimate(flops=3 * 10**10, bytes_accessed=1024, transcendentals=0)
+SOME = pl.CostEstimate(flops=10**10, bytes_accessed=1024, transcendentals=0)
 ORDER = pl.BlockSpec(memory_space=pl.ANY)
 
 
@@ -563,7 +564,7 @@
         out_specs=pl.BlockSpec(memory_space=pltpu.VMEM),
         out_shape=shape((2 * rows, width), bf16),
         compiler_params=pltpu.CompilerParams(vmem_limit_bytes=16 * 1024 * 1024),
-        cost_estimate=MUCH,
+        cost_estimate=SOME,
         name="chain",
     )(mine, recv)
 
@@ -617,7 +618,7 @@
                 self.total = self.seq.did(chained(self.total, recv))
             else:
                 self.total, self.ride = joined(
-                    self.total, recv, self.ride, LITTLE if k == 5 else MUCH
+                    self.total, recv, self.ride, LITTLE if k == 5 else SOME
                 )
                 self.seq.did(self.total)
             self.recv = flat_permute(self.total, halving_pairs(7 - k))

time: 177 us -> 174 us (0.983)
  Pallas kernels: 79.4 us -> 74.4 us
    pallas_call x7, Pallas kernels: 16.6 us -> 13.2 us  [spread(): pl.pallas_call(functools.partial(spread_kernel, piece=piece, plan=plan, m...]
  transfers between devices with their start and end apart: 32 -> 32, of which waited for: 13 -> 15; matrix products, arithmetic and copies ran while one was open for 3% -> 3% of each run, Pallas kernels for 32% -> 30%
where the time goes in v1:
time: 174 us; the launch traced here: 173 us
  Pallas kernels  74.4 us (43%)
  starting transfers between devices  55.4 us (32%)
  waiting for transfers between devices  33.1 us (19%)
  other arithmetic  6.12 us (4%)
  local copies, waits for them, and re-layouts  2.79 us (2%)
    pallas_call x11, Pallas kernels, call(): pl.pallas_call(kernel, grid_spec=spec, out_shape=[o[0] for o in outs], co...  59.2 us
    ppermute x24, starting transfers between devices, flat_permute(): return lax.ppermute(value, ('seq', 'row'), pairs)  39.7 us
    ppermute x24, waiting for transfers between devices, flat_permute(): return lax.ppermute(value, ('seq', 'row'), pairs)  32.3 us
    ppermute x8, starting transfers between devices, passed_along(): lax.ppermute(value, axis, [(source, source + steps) for source in range(l...  15.7 us
    pallas_call x7, Pallas kernels, spread(): pl.pallas_call(functools.partial(spread_kernel, piece=piece, plan=plan, m...  13.2 us
    convert_element_type x10, other arithmetic, added(): return (a.astype(f32) + b.astype(f32)).astype(bf16)  5.98 us
  transfers between devices with their start and end apart: 32, of which 15 were waited for; matrix products, arithmetic and copies ran while one was open for 3% of the time, Pallas kernels for 30%

profile of v1, /device:TPU:0, one launch (start us, length us, event | category | flops | bytes accessed | tf_op | source)
XLA Modules:
  0.0 173.0 jit_solution(10358967849547725545)
XLA Ops:
  0.7 1.0 slice_bitcast_fusion
  1.7 2.4 %collective-permute-start = (bf16[24,512]{1,0:T(8,128)(2,1)S(1)}, bf16[24,512]{1,0:T(8,128)(2,1)S(1)}, u32[]{:S(2)}, u32[]{:S(2)}) collective-permute-start(bf16[24,512]{1,0:T(8,128)(2,1)S(1)} %bitcast.19), channel_id=1, source_target_pairs={{0,4},{4,8},{8,12},{12,16},{16,20},{20,24},{24,28},{1,5},{5,9},{9,... | collective-permute-start | bytes 73736 | tf_op jit(solution)/shard_map/ppermute | solution.py:484
  4.1 3.0 %norm.1.u = bf16[1024,512]{1,0:T(8,128)(2,1)S(1)} custom-call(bf16[8,128,512]{2,1,0:T(8,128)(2,1)} %x.5, bf16[256,256]{1,0:T(8,128)(2,1)} %constant.29.clone.perm.pm, f32[1,512]{1,0:T(1,128)} %bitcast.20), custom_call_target="tpu_custom_call" | custom-call | flops 1024 | bytes 1024 | tf_op jit(solution)/shard_map/norm/pallas_call | solution.py:704
  7.2 6.5 %front.1 = (bf16[1024,512]{1,0:T(8,128)(2,1)S(1)}, bf16[1024,1024]{1,0:T(8,128)(2,1)S(1)}, bf16[1024,1024]{1,0:T(8,128)(2,1)S(1)}, f32[16,1024]{1,0:T(8,128)S(1)}) custom-call(s32[12]{0:T(128)S(1)} %concatenate.17.scal, bf16[1024,512]{1,0:T(8,128)(2,1)S(1)} %norm.1.u, bf16[24,512]{1,0:T(8,128)(2,1)S(1)} %collective-permute-done.edge, f32[1,512]{1,0:T(1,128)} %bitcast.21, ...), custom_call_target="tpu_custom_call" | custom-call | flops 1024 | bytes 1024 | tf_op jit(solution)/shard_map/front/pallas_call | solution.py:704
  13.8 2.8 %collective-permute-start.1 = (f32[16,1024]{1,0:T(8,128)S(1)}, f32[16,1024]{1,0:T(8,128)S(1)}, u32[]{:S(2)}, u32[]{:S(2)}) collective-permute-start(f32[16,1024]{1,0:T(8,128)S(1)} %get-tuple-element.112), channel_id=1, source_target_pairs={{0,4},{1,5},{2,6},{3,7},{4,0},{5,1},{6,2},{7,3},{8,12},{9,13},{10,... | collective-permute-start | bytes 196616 | tf_op jit(solution)/shard_map/ppermute | solution.py:488
  16.6 0.9 collective-permute-done.1.other
  17.5 4.2 %collective-permute-start.4 = (bf16[16,1024]{1,0:T(8,128)(2,1)S(1)}, bf16[16,1024]{1,0:T(8,128)(2,1)S(1)}, u32[]{:S(2)}, u32[]{:S(2)}) collective-permute-start(bf16[16,1024]{1,0:T(8,128)(2,1)S(1)} %pad_maximum_fusion.2), channel_id=1, source_target_pairs={{0,24},{4,28},{1,25},{5,29},{2,26},{6,30},{3,27},{7,31}} | collective-permute-start | bytes 98312 | tf_op jit(solution)/shard_map/ppermute | solution.py:484
  21.8 1.3 collective-permute-start.3
  23.1 2.5 %collective-permute-start.2 = (bf16[16,1024]{1,0:T(8,128)(2,1)S(1)}, bf16[16,1024]{1,0:T(8,128)(2,1)S(1)}, u32[]{:S(2)}, u32[]{:S(2)}) collective-permute-start(bf16[16,1024]{1,0:T(8,128)(2,1)S(1)} %pad_maximum_fusion.2), channel_id=1, source_target_pairs={{0,8},{4,12},{8,16},{12,20},{16,24},{20,28},{1,9},{5,13},{9,17},{1... | collective-permute-start | bytes 98312 | tf_op jit(solution)/shard_map/ppermute | solution.py:484
  25.6 3.5 %da.1 = (bf16[1024,512]{1,0:T(8,128)(2,1)S(1)}, bf16[1024,2048]{1,0:T(8,128)(2,1)S(1)}) custom-call(bf16[8,128,512]{2,1,0:T(8,128)(2,1)S(1)} %copy-done.10, bf16[256,256]{1,0:T(8,128)(2,1)S(1)} %copy-done.8, bf16[2048,512]{1,0:T(8,128)(2,1)S(1)} %copy-done.7), custom_call_target="tpu_custom_call" | custom-call | flops 1024 | bytes 1024 | tf_op jit(solution)/shard_map/da/pallas_call | solution.py:704
  29.2 14.4 %core.1 = (f32[1024,512]{1,0:T(8,128)}, bf16[1024,1024]{1,0:T(8,128)(2,1)S(1)}, bf16[1024,1024]{1,0:T(8,128)(2,1)S(1)}, bf16[1024,512]{1,0:T(8,128)(2,1)S(1)}, b...) custom-call(s32[12]{0:T(128)S(1)} %concatenate.17.scal, ...), custom_call_target="tpu_custom_call" | custom-call | flops 1024 | bytes 1024 | tf_op jit(solution)/shard_map/core/pallas_call | solution.py:704
  43.6 1.2 collective-permute-done.5.fother
  44.8 1.3 collective-permute-start.8
  46.1 1.3 collective-permute-start.7
  47.4 1.3 collective-permute-start.6
  48.7 3.7 %ffn_grad.2 = bf16[2048,512]{1,0:T(8,128)(2,1)S(1)} custom-call(s32[12]{0:T(128)S(1)} %concatenate.17.scal, bf16[1024,2048]{1,0:T(8,128)(2,1)S(1)} %get-tuple-element.136.act, bf16[1024,512]{1,0:T(8,128)(2,1)S(1)} %get-tuple-element.106.gl, bf16[1024,512]{1,0:T(8,128)(2,1)S(1)} %get-tuple-element.121.n2, bf16[1024,2048]{1,0:T(8,128)(2,1)S(1)} %get-tuple-element.127.dp), custom_call_target="tpu_custom_call" | custom-call | flops 1024 | bytes 1024 | tf_op jit(solution)/shard_map/ffn_grad/pallas_call | solution.py:704
  52.7 0.6 collective-permute-done.7.refs_1_
  53.5 3.7 %ffn_grad.3 = bf16[2048,512]{1,0:T(8,128)(2,1)S(1)} custom-call(s32[12]{0:T(128)S(1)} %concatenate.17.scal, bf16[1024,2048]{1,0:T(8,128)(2,1)S(1)} %get-tuple-element.136.act, bf16[1024,512]{1,0:T(8,128)(2,1)S(1)} %get-tuple-element.106.gl, bf16[1024,512]{1,0:T(8,128)(2,1)S(1)} %get-tuple-element.121.n2, bf16[1024,2048]{1,0:T(8,128)(2,1)S(1)} %get-tuple-element.127.dp), custom_call_target="tpu_custom_call" | custom-call | flops 30000001024 | bytes 1024 | tf_op jit(solution)/shard_map/ffn_grad/pallas_call | solution.py:704
  57.2 0.6 add_convert_fusion
  57.8 1.6 collective-permute-start.10
  59.4 3.7 %gates.1 = (bf16[1024,1024]{1,0:T(8,128)(2,1)S(1)}, bf16[1024,1024]{1,0:T(8,128)(2,1)S(1)}, bf16[32,512]{1,0:T(8,128)(2,1)S(1)}, f32[8,1024]{1,0:T(8,128)S(1)}) custom-call(s32[12]{0:T(128)S(1)} %concatenate.17.scal, bf16[1024,1024]{1,0:T(8,128)(2,1)S(1)} %get-tuple-element.116.dh, bf16[1024,1024]{1,0:T(8,128)(2,1)S(1)} %get-tuple-element.110.zl.zl_next.zl_before, ...), custom_call_target="tpu_custom_call" | custom-call | flops 1024 | bytes 1024 | tf_op jit(solution)/shard_map/gates/pallas_call | solution.py:704
  63.1 2.4 %gate_grad.2 = bf16[1536,512]{1,0:T(8,128)(2,1)S(1)} custom-call(s32[12]{0:T(128)S(1)} %concatenate.17.scal, bf16[1024,512]{1,0:T(8,128)(2,1)S(1)} %get-tuple-element.115.c, bf16[1024,1024]{1,0:T(8,128)(2,1)S(1)} %get-tuple-element.143.dkz, bf16[1024,1024]{1,0:T(8,128)(2,1)S(1)} %get-tuple-element.140.dkh, bf16[1024,1024]{1,0:T(8,128)(2,1)S(1)} %get-tuple-element.134.y, ...), custom_call_target="tpu_custom_call" | custom-call | flops 1024 | bytes 1024 | tf_op jit(solution)/shard_map/gate_grad/pallas_call | solution.py:704
  65.6 1.5 collective-permute-start.12
  67.1 5.7 %output.1 = bf16[8,128,512]{2,1,0:T(8,128)(2,1)} custom-call(f32[1024,512]{1,0:T(8,128)} %get-tuple-element.113.r1, bf16[1024,2048]{1,0:T(8,128)(2,1)S(1)} %get-tuple-element.136.act, bf16[256,256]{1,0:T(8,128)(2,1)S(1)} %copy-done.11, bf16[2048,512]{1,0:T(8,128)(2,1)S(1)} %copy-done.7), custom_call_target="tpu_custom_call" | custom-call | flops 1024 | bytes 1024 | tf_op jit(solution)/shard_map/output/pallas_call | solution.py:704
  72.7 1.3 add_convert_fusion.4
  74.0 1.5 collective-permute-start.14
  75.5 2.4 %gate_grad.3 = bf16[1536,512]{1,0:T(8,128)(2,1)S(1)} custom-call(s32[12]{0:T(128)S(1)} %concatenate.17.scal, bf16[1024,512]{1,0:T(8,128)(2,1)S(1)} %get-tuple-element.115.c, bf16[1024,1024]{1,0:T(8,128)(2,1)S(1)} %get-tuple-element.143.dkz, bf16[1024,1024]{1,0:T(8,128)(2,1)S(1)} %get-tuple-element.140.dkh, bf16[1024,1024]{1,0:T(8,128)(2,1)S(1)} %get-tuple-element.134.y, ...), custom_call_target="tpu_custom_call" | custom-call | flops 30000001024 | bytes 1024 | tf_op jit(solution)/shard_map/gate_grad/pallas_call | solution.py:704
  78.0 1.3 add_convert_fusion.2
  79.3 1.4 collective-permute-start.13
  80.8 1.6 copy-done.6
  82.4 10.2 %tail.1 = (bf16[8,128,512]{2,1,0:T(8,128)(2,1)}, f32[40,512]{1,0:T(8,128)S(1)}) custom-call(bf16[8,128,512]{2,1,0:T(8,128)(2,1)} %x.5, f32[1024,512]{1,0:T(8,128)} %get-tuple-element.137.dr1, bf16[1024,1024]{1,0:T(8,128)(2,1)S(1)} %copy-done.4, bf16[1024,1024]{1,0:T(8,128)(2,1)S(1)} %copy-done.6, bf16[256,256]{1,0:T(8,128)(2,1)} %constant.29.clone.perm.pm, ...), custom_call_target="tpu_custom_call" | custom-call | flops 1024 | bytes 1024 | tf_op jit(solution)/shard_map/tail/pallas_call | solution.py:704
  92.6 1.2 add_convert_fusion.8
  93.8 2.2 %collective-permute-start.16 = (bf16[256,512]{1,0:T(8,128)(2,1)S(1)}, bf16[256,512]{1,0:T(8,128)(2,1)S(1)}, u32[]{:S(2)}, u32[]{:S(2)}) collective-permute-start(bf16[256,512]{1,0:T(8,128)(2,1)S(1)} %get-tuple-element.212), channel_id=1, source_target_pairs={{0,8},{1,9},{2,10},{3,11},{4,20},{5,21},{6,22},{7,23},{8,0},{9,1},... | collective-permute-start | bytes 786440 | tf_op jit(solution)/shard_map/ppermute | solution.py:488
  96.0 1.3 add_convert_fusion.6
  97.4 1.2 collective-permute-start.15
  98.6 4.4 %collective-permute-done.16 = bf16[256,512]{1,0:T(8,128)(2,1)S(1)} collective-permute-done((bf16[256,512]{1,0:T(8,128)(2,1)S(1)}, bf16[256,512]{1,0:T(8,128)(2,1)S(1)}, u32[]{:S(2)}, u32[]{:S(2)}) %collective-permute-start.16) | collective-permute-done | bytes 262176 | tf_op jit(solution)/shard_map/ppermute | solution.py:488
  103.0 3.1 %collective-permute-start.18 = (bf16[128,512]{1,0:T(8,128)(2,1)S(1)}, bf16[128,512]{1,0:T(8,128)(2,1)S(1)}, u32[]{:S(2)}, u32[]{:S(2)}) collective-permute-start(bf16[128,512]{1,0:T(8,128)(2,1)S(1)} %add_convert_fusion.14), channel_id=1, source_target_pairs={{0,16},{1,17},{2,18},{3,19},{4,12},{5,13},{6,14},{7,15},{8,24},{9,... | collective-permute-start | bytes 393224 | tf_op jit(solution)/shard_map/ppermute | solution.py:488
  106.3 2.5 %collective-permute-start.17 = (bf16[192,512]{1,0:T(8,128)(2,1)S(1)}, bf16[192,512]{1,0:T(8,128)(2,1)S(1)}, u32[]{:S(2)}, u32[]{:S(2)}) collective-permute-start(bf16[192,512]{1,0:T(8,128)(2,1)S(1)} %get-tuple-element.213), channel_id=1, source_target_pairs={{0,8},{1,9},{2,10},{3,11},{4,20},{5,21},{6,22},{7,23},{8,0},{9,1},... | collective-permute-start | bytes 589832 | tf_op jit(solution)/shard_map/ppermute | solution.py:488
  108.8 0.5 collective-permute-done.18
  109.4 3.5 %collective-permute-start.20 = (bf16[128,512]{1,0:T(8,128)(2,1)S(1)}, bf16[128,512]{1,0:T(8,128)(2,1)S(1)}, u32[]{:S(2)}, u32[]{:S(2)}) collective-permute-start(bf16[128,512]{1,0:T(8,128)(2,1)S(1)} %add_convert_fusion.12.mine), channel_id=1, source_target_pairs={{0,16},{1,17},{2,18},{3,19},{4,12},{5,13},{6,14},{7,15},{8,24},{9,... | collective-permute-start | bytes 393224 | tf_op jit(solution)/shard_map/ppermute | solution.py:488
  112.9 3.7 %collective-permute-done.17 = bf16[192,512]{1,0:T(8,128)(2,1)S(1)} collective-permute-done((bf16[192,512]{1,0:T(8,128)(2,1)S(1)}, bf16[192,512]{1,0:T(8,128)(2,1)S(1)}, u32[]{:S(2)}, u32[]{:S(2)}) %collective-permute-start.17) | collective-permute-done | bytes 196640 | tf_op jit(solution)/shard_map/ppermute | solution.py:488
  116.7 0.5 collective-permute-start.19
  117.2 9.4 %collective-permute-start.23 = (bf16[256,512]{1,0:T(8,128)(2,1)S(1)}, bf16[256,512]{1,0:T(8,128)(2,1)S(1)}, u32[]{:S(2)}, u32[]{:S(2)}) collective-permute-start(bf16[256,512]{1,0:T(8,128)(2,1)S(1)} %chain.3.mine), channel_id=1, source_target_pairs={{0,8},{1,9},{2,10},{3,11},{4,20},{5,21},{6,22},{7,23},{8,0},{9,1},... | collective-permute-start | bytes 786440 | tf_op jit(solution)/shard_map/ppermute | solution.py:488
  126.5 1.0 collective-permute-done.19
  127.6 2.4 %collective-permute-start.21 = (bf16[112,512]{1,0:T(8,128)(2,1)S(1)}, bf16[112,512]{1,0:T(8,128)(2,1)S(1)}, u32[]{:S(2)}, u32[]{:S(2)}) collective-permute-start(bf16[112,512]{1,0:T(8,128)(2,1)S(1)} %pad_maximum_fusion.mine), channel_id=1, source_target_pairs={{0,16},{1,17},{2,18},{3,19},{4,12},{5,13},{6,14},{7,15},{8,24},{9,... | collective-permute-start | bytes 344072 | tf_op jit(solution)/shard_map/ppermute | solution.py:488
  130.0 5.6 %collective-permute-done.21.recv = bf16[112,512]{1,0:T(8,128)(2,1)S(1)} collective-permute-done((bf16[112,512]{1,0:T(8,128)(2,1)S(1)}, bf16[112,512]{1,0:T(8,128)(2,1)S(1)}, u32[]{:S(2)}, u32[]{:S(2)}) %collective-permute-start.21) | collective-permute-done | bytes 114720 | tf_op jit(solution)/shard_map/ppermute | solution.py:488
  135.8 1.4 collective-permute-start.25
  137.2 4.4 %collective-permute-done.22.recv = bf16[208,512]{1,0:T(8,128)(2,1)S(1)} collective-permute-done((bf16[208,512]{1,0:T(8,128)(2,1)S(1)}, bf16[208,512]{1,0:T(8,128)(2,1)S(1)}, u32[]{:S(2)}, u32[]{:S(2)}) %collective-permute-start.22) | collective-permute-done | bytes 213024 | tf_op jit(solution)/shard_map/ppermute | solution.py:488
  141.6 1.3 collective-permute-start.24
  142.9 2.1 %collective-permute-done.25.recv = bf16[512,512]{1,0:T(8,128)(2,1)S(1)} collective-permute-done((bf16[512,512]{1,0:T(8,128)(2,1)S(1)}, bf16[512,512]{1,0:T(8,128)(2,1)S(1)}, u32[]{:S(2)}, u32[]{:S(2)}) %collective-permute-start.25) | collective-permute-done | bytes 524320 | tf_op jit(solution)/shard_map/ppermute | solution.py:488
  145.2 1.4 collective-permute-start.28
  146.7 4.3 %collective-permute-done.24.recv = bf16[400,512]{1,0:T(8,128)(2,1)S(1)} collective-permute-done((bf16[400,512]{1,0:T(8,128)(2,1)S(1)}, bf16[400,512]{1,0:T(8,128)(2,1)S(1)}, u32[]{:S(2)}, u32[]{:S(2)}) %collective-permute-start.24) | collective-permute-done | bytes 409632 | tf_op jit(solution)/shard_map/ppermute | solution.py:488
  151.1 1.5 collective-permute-start.26
  152.5 2.0 %spread_ffn.4 = (f32[2048,512]{1,0:T(8,128)}, f32[512,2048]{1,0:T(8,128)}) custom-call(s32[12]{0:T(128)S(1)} %concatenate.17.scal, bf16[1024,512]{1,0:T(8,128)(2,1)S(1)} %chain.5.src), custom_call_target="tpu_custom_call" | custom-call | flops 10000000000 | bytes 1024 | tf_op jit(solution)/shard_map/spread_ffn/pallas_call | solution.py:440
  154.5 2.0 %spread_ffn.5 = (f32[2048,512]{1,0:T(8,128)}, f32[512,2048]{1,0:T(8,128)}) custom-call(s32[12]{0:T(128)S(1)} %concatenate.17.scal, bf16[1024,512]{1,0:T(8,128)(2,1)S(1)} %collective-permute-done.29.src, f32[2048,512]{1,0:T(8,128)} %get-tuple-element.167.refs_0_, f32[512,2048]{1,0:T(8,128)} %get-tuple-element.169.refs_1_), custom_call_target="tpu_custom_call", output_to_operand_aliasing={{0}: (2, {}), {1}: (3, {})} | custom-call | flops 10000000000 | bytes 1024 | tf_op jit(solution)/shard_map/spread_ffn/pallas_call | solution.py:440
  156.5 3.6 %collective-permute-done.28.src = bf16[1024,512]{1,0:T(8,128)(2,1)S(1)} collective-permute-done((bf16[1024,512]{1,0:T(8,128)(2,1)S(1)}, bf16[1024,512]{1,0:T(8,128)(2,1)S(1)}, u32[]{:S(2)}, u32[]{:S(2)}) %collective-permute-start.28) | collective-permute-done | bytes 1048608 | tf_op jit(solution)/shard_map/ppermute | solution.py:488
  160.1 0.9 collective-permute-start.30
  161.0 2.0 %spread_ffn.6 = (f32[2048,512]{1,0:T(8,128)}, f32[512,2048]{1,0:T(8,128)}) custom-call(s32[12]{0:T(128)S(1)} %concatenate.17.scal, bf16[1024,512]{1,0:T(8,128)(2,1)S(1)} %collective-permute-done.28.src, f32[2048,512]{1,0:T(8,128)} %get-tuple-element.170.refs_0_, f32[512,2048]{1,0:T(8,128)} %get-tuple-element.173.refs_1_), custom_call_target="tpu_custom_call", output_to_operand_aliasing={{0}: (2, {}), {1}: (3, {})} | custom-call | flops 10000000000 | bytes 1024 | tf_op jit(solution)/shard_map/spread_ffn/pallas_call | solution.py:440
  163.0 1.7 %spread_gates.3 = (f32[512,1024]{1,0:T(8,128)}, f32[512,1024]{1,0:T(8,128)}, f32[1024,512]{1,0:T(8,128)}) custom-call(s32[12]{0:T(128)S(1)} %concatenate.17.scal, bf16[784,512]{1,0:T(8,128)(2,1)S(1)} %get-tuple-element.175.src), custom_call_target="tpu_custom_call" | custom-call | flops 10000000000 | bytes 1024 | tf_op jit(solution)/shard_map/spread_gates/pallas_call | solution.py:440
  164.7 2.0 %spread_ffn.7 = (f32[2048,512]{1,0:T(8,128)}, f32[512,2048]{1,0:T(8,128)}) custom-call(s32[12]{0:T(128)S(1)} %concatenate.17.scal, bf16[1024,512]{1,0:T(8,128)(2,1)S(1)} %collective-permute-done.30.src, f32[2048,512]{1,0:T(8,128)} %get-tuple-element.174.refs_0_, f32[512,2048]{1,0:T(8,128)} %get-tuple-element.178.refs_1_), custom_call_target="tpu_custom_call", output_to_operand_aliasing={{0}: (2, {}), {1}: (3, {})} | custom-call | flops 10000000000 | bytes 1024 | tf_op jit(solution)/shard_map/spread_ffn/pallas_call | solution.py:440
  166.7 1.7 %spread_gates.4 = (f32[512,1024]{1,0:T(8,128)}, f32[512,1024]{1,0:T(8,128)}, f32[1024,512]{1,0:T(8,128)}) custom-call(s32[12]{0:T(128)S(1)} %concatenate.17.scal, bf16[784,512]{1,0:T(8,128)(2,1)S(1)} %collective-permute-done.27.src.theirs, f32[512,1024]{1,0:T(8,128)} %get-tuple-element.176.refs_0_, ...), custom_call_target="tpu_custom_call", output_to_operand_aliasing={{0}: (2, {}), {1}: (3, {}), {2}: (4, {})} | custom-call | flops 10000000000 | bytes 1024 | tf_op jit(solution)/shard_map/spread_gates/pallas_call | solution.py:440
  168.7 0.6 collective-permute-start.31
  169.3 1.7 %spread_gates.5 = (f32[512,1024]{1,0:T(8,128)}, f32[512,1024]{1,0:T(8,128)}, f32[1024,512]{1,0:T(8,128)}) custom-call(s32[12]{0:T(128)S(1)} %concatenate.17.scal, bf16[784,512]{1,0:T(8,128)(2,1)S(1)} %collective-permute-done.26.src.rest, f32[512,1024]{1,0:T(8,128)} %get-tuple-element.183.refs_0_, ...), custom_call_target="tpu_custom_call", output_to_operand_aliasing={{0}: (2, {}), {1}: (3, {}), {2}: (4, {})} | custom-call | flops 10000000000 | bytes 1024 | tf_op jit(solution)/shard_map/spread_gates/pallas_call | solution.py:440
  171.3 1.8 %spread_last.1 = (f32[512,1024]{1,0:T(8,128)}, f32[512,1024]{1,0:T(8,128)}, f32[1024,512]{1,0:T(8,128)}, f32[1,512]{1,0:T(1,128)}, f32[4,512]{1,0:T(4,128)}, /*index=5*/f32[1,512]{1,0:T(1,128)}, f32[1,1024]{1,0:T(1,128)}) custom-call(s32[12]{0:T(128)S(1)} %concatenate.17.scal, ...), custom_call_target="tpu_custom_call", output_to_operand_aliasing={{0}: (5, {}), {1}: (6, {}), {2}: (7, {})} | custom-call | flops 10000000000 | bytes 1024 | tf_op jit(solution)/shard_map/spread_last/pallas_call | solution.py:418
  (81 shorter events, 2.1 us)
Async XLA Ops:
  0.6 6.5 %copy-start.14 = (s32[8]{0:T(128)S(1)}, s32[8]{0:T(128)}, u32[]{:S(2)}) copy-start(s32[8]{0:T(128)} %param.15) | copy-start | bytes 100
  0.7 6.6 %copy-start.2 = (bf16[512,1024]{1,0:T(8,128)(2,1)S(1)}, bf16[512,1024]{1,0:T(8,128)(2,1)}, u32[]{:S(2)}) copy-start(bf16[512,1024]{1,0:T(8,128)(2,1)} %wc.3) | copy-start | bytes 3145732
  0.7 6.6 %copy-start.1 = (bf16[512,1024]{1,0:T(8,128)(2,1)S(1)}, bf16[512,1024]{1,0:T(8,128)(2,1)}, u32[]{:S(2)}) copy-start(bf16[512,1024]{1,0:T(8,128)(2,1)} %wg.3) | copy-start | bytes 3145732
  1.7 5.5 %collective-permute-start = (bf16[24,512]{1,0:T(8,128)(2,1)S(1)}, bf16[24,512]{1,0:T(8,128)(2,1)S(1)}, u32[]{:S(2)}, u32[]{:S(2)}) collective-permute-start(bf16[24,512]{1,0:T(8,128)(2,1)S(1)} %bitcast.19), channel_id=1, source_target_pairs={{0,4},{4,8},{8,12},{12,16},{16,20},{20,24},{24,28},{1,5},{5,9},{9,... | collective-permute-start | bytes 73736 | tf_op jit(solution)/shard_map/ppermute | solution.py:484
  7.1 18.5 %copy-start.8 = (bf16[256,256]{1,0:T(8,128)(2,1)S(1)}, bf16[256,256]{1,0:T(8,128)(2,1)}, u32[]{:S(2)}) copy-start(bf16[256,256]{1,0:T(8,128)(2,1)} %constant.29.clone.perm.pm) | copy-start | bytes 393220
  7.2 18.4 %copy-start.7 = (bf16[2048,512]{1,0:T(8,128)(2,1)S(1)}, bf16[2048,512]{1,0:T(8,128)(2,1)}, u32[]{:S(2)}) copy-start(bf16[2048,512]{1,0:T(8,128)(2,1)} %wd.3) | copy-start | bytes 6291460
  7.2 18.4 %copy-start.10 = (bf16[8,128,512]{2,1,0:T(8,128)(2,1)S(1)}, bf16[8,128,512]{2,1,0:T(8,128)(2,1)}, u32[]{:S(2)}) copy-start(bf16[8,128,512]{2,1,0:T(8,128)(2,1)} %g.1) | copy-start | bytes 3145732
  13.8 15.4 %copy-start = (bf16[8,128,512]{2,1,0:T(8,128)(2,1)S(1)}, bf16[8,128,512]{2,1,0:T(8,128)(2,1)}, u32[]{:S(2)}) copy-start(bf16[8,128,512]{2,1,0:T(8,128)(2,1)} %x.5) | copy-start | bytes 3145732
  13.8 15.4 %copy-start.9 = (bf16[512,2048]{1,0:T(8,128)(2,1)S(1)}, bf16[512,2048]{1,0:T(8,128)(2,1)}, u32[]{:S(2)}) copy-start(bf16[512,2048]{1,0:T(8,128)(2,1)} %refs_5_.1) | copy-start | bytes 6291460
  13.8 15.4 %copy-start.12 = (f32[512]{0:T(512)S(1)}, f32[512]{0:T(512)}, u32[]{:S(2)}) copy-start(f32[512]{0:T(512)} %param.22) | copy-start | bytes 6148
  13.8 3.7 %collective-permute-start.1 = (f32[16,1024]{1,0:T(8,128)S(1)}, f32[16,1024]{1,0:T(8,128)S(1)}, u32[]{:S(2)}, u32[]{:S(2)}) collective-permute-start(f32[16,1024]{1,0:T(8,128)S(1)} %get-tuple-element.112), channel_id=1, source_target_pairs={{0,4},{1,5},{2,6},{3,7},{4,0},{5,1},{6,2},{7,3},{8,12},{9,13},{10,... | collective-permute-start | bytes 196616 | tf_op jit(solution)/shard_map/ppermute | solution.py:488
  17.5 11.6 %collective-permute-start.4 = (bf16[16,1024]{1,0:T(8,128)(2,1)S(1)}, bf16[16,1024]{1,0:T(8,128)(2,1)S(1)}, u32[]{:S(2)}, u32[]{:S(2)}) collective-permute-start(bf16[16,1024]{1,0:T(8,128)(2,1)S(1)} %pad_maximum_fusion.2), channel_id=1, source_target_pairs={{0,24},{4,28},{1,25},{5,29},{2,26},{6,30},{3,27},{7,31}} | collective-permute-start | bytes 98312 | tf_op jit(solution)/shard_map/ppermute | solution.py:484
  21.8 7.4 %collective-permute-start.3 = (bf16[16,1024]{1,0:T(8,128)(2,1)S(1)}, bf16[16,1024]{1,0:T(8,128)(2,1)S(1)}, u32[]{:S(2)}, u32[]{:S(2)}) collective-permute-start(bf16[16,1024]{1,0:T(8,128)(2,1)S(1)} %pad_maximum_fusion.2), channel_id=1, source_target_pairs={{0,16},{4,20},{8,24},{12,28},{1,17},{5,21},{9,25},{13,29},{2,18},{... | collective-permute-start | bytes 98312 | tf_op jit(solution)/shard_map/ppermute | solution.py:484
  23.1 6.1 %collective-permute-start.2 = (bf16[16,1024]{1,0:T(8,128)(2,1)S(1)}, bf16[16,1024]{1,0:T(8,128)(2,1)S(1)}, u32[]{:S(2)}, u32[]{:S(2)}) collective-permute-start(bf16[16,1024]{1,0:T(8,128)(2,1)S(1)} %pad_maximum_fusion.2), channel_id=1, source_target_pairs={{0,8},{4,12},{8,16},{12,20},{16,24},{20,28},{1,9},{5,13},{9,17},{1... | collective-permute-start | bytes 98312 | tf_op jit(solution)/shard_map/ppermute | solution.py:484
  43.6 1.2 collective-permute-start.5
  44.8 7.8 %collective-permute-start.8 = (bf16[16,1024]{1,0:T(8,128)(2,1)S(1)}, bf16[16,1024]{1,0:T(8,128)(2,1)S(1)}, u32[]{:S(2)}, u32[]{:S(2)}) collective-permute-start(bf16[16,1024]{1,0:T(8,128)(2,1)S(1)} %pad_maximum_fusion.1), channel_id=1, source_target_pairs={{24,0},{28,4},{25,1},{29,5},{26,2},{30,6},{27,3},{31,7}} | collective-permute-start | bytes 98312 | tf_op jit(solution)/shard_map/ppermute | solution.py:484
  46.1 7.1 %collective-permute-start.7 = (bf16[16,1024]{1,0:T(8,128)(2,1)S(1)}, bf16[16,1024]{1,0:T(8,128)(2,1)S(1)}, u32[]{:S(2)}, u32[]{:S(2)}) collective-permute-start(bf16[16,1024]{1,0:T(8,128)(2,1)S(1)} %pad_maximum_fusion.1), channel_id=1, source_target_pairs={{16,0},{20,4},{24,8},{28,12},{17,1},{21,5},{25,9},{29,13},{18,2},{... | collective-permute-start | bytes 98312 | tf_op jit(solution)/shard_map/ppermute | solution.py:484
  47.4 6.1 %collective-permute-start.6 = (bf16[16,1024]{1,0:T(8,128)(2,1)S(1)}, bf16[16,1024]{1,0:T(8,128)(2,1)S(1)}, u32[]{:S(2)}, u32[]{:S(2)}) collective-permute-start(bf16[16,1024]{1,0:T(8,128)(2,1)S(1)} %pad_maximum_fusion.1), channel_id=1, source_target_pairs={{8,0},{12,4},{16,8},{20,12},{24,16},{28,20},{9,1},{13,5},{17,9},{2... | collective-permute-start | bytes 98312 | tf_op jit(solution)/shard_map/ppermute | solution.py:484
  52.4 4.7 %collective-permute-start.9 = (bf16[2048,512]{1,0:T(8,128)(2,1)S(1)}, bf16[2048,512]{1,0:T(8,128)(2,1)S(1)}, u32[]{:S(2)}, u32[]{:S(2)}) collective-permute-start(bf16[2048,512]{1,0:T(8,128)(2,1)S(1)} %ffn_grad.2), channel_id=1, source_target_pairs={{0,4},{1,5},{2,6},{3,7},{4,0},{5,1},{6,2},{7,3},{8,12},{9,13},{10,... | collective-permute-start | bytes 6291464 | tf_op jit(solution)/shard_map/ppermute | solution.py:488
  57.8 14.9 %collective-permute-start.10 = (bf16[1024,512]{1,0:T(8,128)(2,1)S(1)}, bf16[1024,512]{1,0:T(8,128)(2,1)S(1)}, u32[]{:S(2)}, u32[]{:S(2)}) collective-permute-start(bf16[1024,512]{1,0:T(8,128)(2,1)S(1)} %get-tuple-element.204.refs_5_), channel_id=1, source_target_pairs={{0,1},{1,0},{2,3},{3,2},{4,6},{5,7},{6,4},{7,5},{8,9},{9,8},{10,11... | collective-permute-start | bytes 3145736 | tf_op jit(solution)/shard_map/ppermute | solution.py:488
  63.1 12.5 %copy-start.3 = (bf16[1024,1024]{1,0:T(8,128)(2,1)}, bf16[1024,1024]{1,0:T(8,128)(2,1)S(1)}, u32[]{:S(2)}) copy-start(bf16[1024,1024]{1,0:T(8,128)(2,1)S(1)} %get-tuple-element.143.dkz) | copy-start | bytes 6291460
  63.1 12.4 %copy-start.5 = (bf16[1024,1024]{1,0:T(8,128)(2,1)}, bf16[1024,1024]{1,0:T(8,128)(2,1)S(1)}, u32[]{:S(2)}) copy-start(bf16[1024,1024]{1,0:T(8,128)(2,1)S(1)} %get-tuple-element.140.dkh) | copy-start | bytes 6291460
  63.1 4.0 %copy-start.11 = (bf16[256,256]{1,0:T(8,128)(2,1)S(1)}, bf16[256,256]{1,0:T(8,128)(2,1)}, u32[]{:S(2)}) copy-start(bf16[256,256]{1,0:T(8,128)(2,1)} %constant.30.clone.perm.back_pm) | copy-start | bytes 393220
  65.5 12.5 %collective-permute-start.11 = (bf16[1536,512]{1,0:T(8,128)(2,1)S(1)}, bf16[1536,512]{1,0:T(8,128)(2,1)S(1)}, u32[]{:S(2)}, u32[]{:S(2)}) collective-permute-start(bf16[1536,512]{1,0:T(8,128)(2,1)S(1)} %gate_grad.2), channel_id=1, source_target_pairs={{0,4},{1,5},{2,6},{3,7},{4,0},{5,1},{6,2},{7,3},{8,12},{9,13},{10,... | collective-permute-start | bytes 4718600 | tf_op jit(solution)/shard_map/ppermute | solution.py:488
  65.6 12.4 %collective-permute-start.12 = (bf16[24,512]{1,0:T(8,128)(2,1)S(1)}, bf16[24,512]{1,0:T(8,128)(2,1)S(1)}, u32[]{:S(2)}, u32[]{:S(2)}) collective-permute-start(bf16[24,512]{1,0:T(8,128)(2,1)S(1)} %slice.134), channel_id=1, source_target_pairs={{4,0},{8,4},{12,8},{16,12},{20,16},{24,20},{28,24},{5,1},{9,5},{13... | collective-permute-start | bytes 73736 | tf_op jit(solution)/shard_map/ppermute | solution.py:484
  74.0 18.6 %collective-permute-start.14 = (bf16[512,512]{1,0:T(8,128)(2,1)}, bf16[512,512]{1,0:T(8,128)(2,1)}, u32[]{:S(2)}, u32[]{:S(2)}) collective-permute-start(bf16[512,512]{1,0:T(8,128)(2,1)} %get-tuple-element.208), channel_id=1, source_target_pairs={{0,2},{1,3},{2,0},{3,1},{4,5},{5,4},{6,7},{7,6},{8,10},{9,11},{10,... | collective-permute-start | bytes 1572872 | tf_op jit(solution)/shard_map/ppermute | solution.py:488
  77.9 2.8 %copy-start.4 = (bf16[1024,1024]{1,0:T(8,128)(2,1)S(1)}, bf16[1024,1024]{1,0:T(8,128)(2,1)}, u32[]{:S(2)}) copy-start(bf16[1024,1024]{1,0:T(8,128)(2,1)} %copy-done.3) | copy-start | bytes 6291460
  79.3 16.7 %collective-permute-start.13 = (bf16[768,512]{1,0:T(8,128)(2,1)}, bf16[768,512]{1,0:T(8,128)(2,1)}, u32[]{:S(2)}, u32[]{:S(2)}) collective-permute-start(bf16[768,512]{1,0:T(8,128)(2,1)} %get-tuple-element.206), channel_id=1, source_target_pairs={{0,1},{1,0},{2,3},{3,2},{4,6},{5,7},{6,4},{7,5},{8,9},{9,8},{10,11... | collective-permute-start | bytes 2359304 | tf_op jit(solution)/shard_map/ppermute | solution.py:488
  80.8 1.6 copy-start.6
  82.4 10.2 %copy-start.13 = (bf16[512,512]{1,0:T(8,128)(2,1)S(1)}, bf16[512,512]{1,0:T(8,128)(2,1)}, u32[]{:S(2)}) copy-start(bf16[512,512]{1,0:T(8,128)(2,1)} %get-tuple-element.207) | copy-start | bytes 1572868
  93.8 9.2 %collective-permute-start.16 = (bf16[256,512]{1,0:T(8,128)(2,1)S(1)}, bf16[256,512]{1,0:T(8,128)(2,1)S(1)}, u32[]{:S(2)}, u32[]{:S(2)}) collective-permute-start(bf16[256,512]{1,0:T(8,128)(2,1)S(1)} %get-tuple-element.212), channel_id=1, source_target_pairs={{0,8},{1,9},{2,10},{3,11},{4,20},{5,21},{6,22},{7,23},{8,0},{9,1},... | collective-permute-start | bytes 786440 | tf_op jit(solution)/shard_map/ppermute | solution.py:488
  97.4 8.8 %collective-permute-start.15 = (bf16[384,512]{1,0:T(8,128)(2,1)S(1)}, bf16[384,512]{1,0:T(8,128)(2,1)S(1)}, u32[]{:S(2)}, u32[]{:S(2)}) collective-permute-start(bf16[384,512]{1,0:T(8,128)(2,1)S(1)} %get-tuple-element.209), channel_id=1, source_target_pairs={{0,2},{1,3},{2,0},{3,1},{4,5},{5,4},{6,7},{7,6},{8,10},{9,11},{10,... | collective-permute-start | bytes 1179656 | tf_op jit(solution)/shard_map/ppermute | solution.py:488
  103.0 6.3 %collective-permute-start.18 = (bf16[128,512]{1,0:T(8,128)(2,1)S(1)}, bf16[128,512]{1,0:T(8,128)(2,1)S(1)}, u32[]{:S(2)}, u32[]{:S(2)}) collective-permute-start(bf16[128,512]{1,0:T(8,128)(2,1)S(1)} %add_convert_fusion.14), channel_id=1, source_target_pairs={{0,16},{1,17},{2,18},{3,19},{4,12},{5,13},{6,14},{7,15},{8,24},{9,... | collective-permute-start | bytes 393224 | tf_op jit(solution)/shard_map/ppermute | solution.py:488
  106.3 10.3 %collective-permute-start.17 = (bf16[192,512]{1,0:T(8,128)(2,1)S(1)}, bf16[192,512]{1,0:T(8,128)(2,1)S(1)}, u32[]{:S(2)}, u32[]{:S(2)}) collective-permute-start(bf16[192,512]{1,0:T(8,128)(2,1)S(1)} %get-tuple-element.213), channel_id=1, source_target_pairs={{0,8},{1,9},{2,10},{3,11},{4,20},{5,21},{6,22},{7,23},{8,0},{9,1},... | collective-permute-start | bytes 589832 | tf_op jit(solution)/shard_map/ppermute | solution.py:488
  109.4 7.8 %collective-permute-start.20 = (bf16[128,512]{1,0:T(8,128)(2,1)S(1)}, bf16[128,512]{1,0:T(8,128)(2,1)S(1)}, u32[]{:S(2)}, u32[]{:S(2)}) collective-permute-start(bf16[128,512]{1,0:T(8,128)(2,1)S(1)} %add_convert_fusion.12.mine), channel_id=1, source_target_pairs={{0,16},{1,17},{2,18},{3,19},{4,12},{5,13},{6,14},{7,15},{8,24},{9,... | collective-permute-start | bytes 393224 | tf_op jit(solution)/shard_map/ppermute | solution.py:488
  116.7 10.9 %collective-permute-start.19 = (bf16[96,512]{1,0:T(8,128)(2,1)S(1)}, bf16[96,512]{1,0:T(8,128)(2,1)S(1)}, u32[]{:S(2)}, u32[]{:S(2)}) collective-permute-start(bf16[96,512]{1,0:T(8,128)(2,1)S(1)} %add_convert_fusion.16), channel_id=1, source_target_pairs={{0,16},{1,17},{2,18},{3,19},{4,12},{5,13},{6,14},{7,15},{8,24},{9,... | collective-permute-start | bytes 294920 | tf_op jit(solution)/shard_map/ppermute | solution.py:488
  117.2 18.6 %collective-permute-start.23 = (bf16[256,512]{1,0:T(8,128)(2,1)S(1)}, bf16[256,512]{1,0:T(8,128)(2,1)S(1)}, u32[]{:S(2)}, u32[]{:S(2)}) collective-permute-start(bf16[256,512]{1,0:T(8,128)(2,1)S(1)} %chain.3.mine), channel_id=1, source_target_pairs={{0,8},{1,9},{2,10},{3,11},{4,20},{5,21},{6,22},{7,23},{8,0},{9,1},... | collective-permute-start | bytes 786440 | tf_op jit(solution)/shard_map/ppermute | solution.py:488
  127.6 8.0 %collective-permute-start.21 = (bf16[112,512]{1,0:T(8,128)(2,1)S(1)}, bf16[112,512]{1,0:T(8,128)(2,1)S(1)}, u32[]{:S(2)}, u32[]{:S(2)}) collective-permute-start(bf16[112,512]{1,0:T(8,128)(2,1)S(1)} %pad_maximum_fusion.mine), channel_id=1, source_target_pairs={{0,16},{1,17},{2,18},{3,19},{4,12},{5,13},{6,14},{7,15},{8,24},{9,... | collective-permute-start | bytes 344072 | tf_op jit(solution)/shard_map/ppermute | solution.py:488
  135.7 5.9 %collective-permute-start.22 = (bf16[208,512]{1,0:T(8,128)(2,1)S(1)}, bf16[208,512]{1,0:T(8,128)(2,1)S(1)}, u32[]{:S(2)}, u32[]{:S(2)}) collective-permute-start(bf16[208,512]{1,0:T(8,128)(2,1)S(1)} %get-tuple-element.157.mine), channel_id=1, source_target_pairs={{0,8},{1,9},{2,10},{3,11},{4,20},{5,21},{6,22},{7,23},{8,0},{9,1},... | collective-permute-start | bytes 638984 | tf_op jit(solution)/shard_map/ppermute | solution.py:488
  135.8 9.2 %collective-permute-start.25 = (bf16[512,512]{1,0:T(8,128)(2,1)S(1)}, bf16[512,512]{1,0:T(8,128)(2,1)S(1)}, u32[]{:S(2)}, u32[]{:S(2)}) collective-permute-start(bf16[512,512]{1,0:T(8,128)(2,1)S(1)} %chain.4.mine), channel_id=1, source_target_pairs={{0,2},{1,3},{2,0},{3,1},{4,5},{5,4},{6,7},{7,6},{8,10},{9,11},{10,... | collective-permute-start | bytes 1572872 | tf_op jit(solution)/shard_map/ppermute | solution.py:488
  141.6 9.3 %collective-permute-start.24 = (bf16[400,512]{1,0:T(8,128)(2,1)S(1)}, bf16[400,512]{1,0:T(8,128)(2,1)S(1)}, u32[]{:S(2)}, u32[]{:S(2)}) collective-permute-start(bf16[400,512]{1,0:T(8,128)(2,1)S(1)} %get-tuple-element.161.mine), channel_id=1, source_target_pairs={{0,2},{1,3},{2,0},{3,1},{4,5},{5,4},{6,7},{7,6},{8,10},{9,11},{10,... | collective-permute-start | bytes 1228808 | tf_op jit(solution)/shard_map/ppermute | solution.py:488
  145.2 9.3 %collective-permute-start.29 = (bf16[1024,512]{1,0:T(8,128)(2,1)S(1)}, bf16[1024,512]{1,0:T(8,128)(2,1)S(1)}, u32[]{:S(2)}, u32[]{:S(2)}) collective-permute-start(bf16[1024,512]{1,0:T(8,128)(2,1)S(1)} %chain.5.src), channel_id=1, source_target_pairs={{0,4},{1,5},{2,6},{3,7},{4,0},{5,1},{6,2},{7,3},{8,12},{9,13},{10,... | collective-permute-start | bytes 3145736 | tf_op jit(solution)/shard_map/ppermute | solution.py:488
  145.2 14.9 %collective-permute-start.28 = (bf16[1024,512]{1,0:T(8,128)(2,1)S(1)}, bf16[1024,512]{1,0:T(8,128)(2,1)S(1)}, u32[]{:S(2)}, u32[]{:S(2)}) collective-permute-start(bf16[1024,512]{1,0:T(8,128)(2,1)S(1)} %chain.5.src), channel_id=1, source_target_pairs={{0,1},{1,0},{2,3},{3,2},{4,6},{5,7},{6,4},{7,5},{8,9},{9,8},{10,11... | collective-permute-start | bytes 3145736 | tf_op jit(solution)/shard_map/ppermute | solution.py:488
  151.0 15.7 %collective-permute-start.27 = (bf16[784,512]{1,0:T(8,128)(2,1)S(1)}, bf16[784,512]{1,0:T(8,128)(2,1)S(1)}, u32[]{:S(2)}, u32[]{:S(2)}) collective-permute-start(bf16[784,512]{1,0:T(8,128)(2,1)S(1)} %get-tuple-element.175.src), channel_id=1, source_target_pairs={{0,4},{1,5},{2,6},{3,7},{4,0},{5,1},{6,2},{7,3},{8,12},{9,13},{10,... | collective-permute-start | bytes 2408456 | tf_op jit(solution)/shard_map/ppermute | solution.py:488
  151.1 17.6 %collective-permute-start.26 = (bf16[784,512]{1,0:T(8,128)(2,1)S(1)}, bf16[784,512]{1,0:T(8,128)(2,1)S(1)}, u32[]{:S(2)}, u32[]{:S(2)}) collective-permute-start(bf16[784,512]{1,0:T(8,128)(2,1)S(1)} %get-tuple-element.175.src), channel_id=1, source_target_pairs={{0,1},{1,0},{2,3},{3,2},{4,6},{5,7},{6,4},{7,5},{8,9},{9,8},{10,11... | collective-permute-start | bytes 2408456 | tf_op jit(solution)/shard_map/ppermute | solution.py:488
  160.1 4.6 %collective-permute-start.30 = (bf16[1024,512]{1,0:T(8,128)(2,1)S(1)}, bf16[1024,512]{1,0:T(8,128)(2,1)S(1)}, u32[]{:S(2)}, u32[]{:S(2)}) collective-permute-start(bf16[1024,512]{1,0:T(8,128)(2,1)S(1)} %collective-permute-done.28.src), channel_id=1, source_target_pairs={{0,4},{1,5},{2,6},{3,7},{4,0},{5,1},{6,2},{7,3},{8,12},{9,13},{10,... | collective-permute-start | bytes 3145736 | tf_op jit(solution)/shard_map/ppermute | solution.py:488
  168.7 2.5 %collective-permute-start.31 = (bf16[784,512]{1,0:T(8,128)(2,1)S(1)}, bf16[784,512]{1,0:T(8,128)(2,1)S(1)}, u32[]{:S(2)}, u32[]{:S(2)}) collective-permute-start(bf16[784,512]{1,0:T(8,128)(2,1)S(1)} %collective-permute-done.26.src.rest), channel_id=1, source_target_pairs={{0,4},{1,5},{2,6},{3,7},{4,0},{5,1},{6,2},{7,3},{8,12},{9,13},{10,... | collective-permute-start | bytes 2408456 | tf_op jit(solution)/shard_map/ppermute | solution.py:488

commit v2 on v1

--- a/solution.py
+++ b/solution.py
@@ -465,7 +465,7 @@
 
 LITTLE = pl.CostEstimate(flops=1024, bytes_accessed=1024, transcendentals=0)
 MUCH = pl.CostEstimate(flops=3 * 10**10, bytes_accessed=1024, transcendentals=0)
-SOME = pl.CostEstimate(flops=10**10, bytes_accessed=1024, transcendentals=0)
+SOME = pl.CostEstimate(flops=8 * 10**9, bytes_accessed=1024, transcendentals=0)
 ORDER = pl.BlockSpec(memory_space=pl.ANY)
 
 
@@ -693,7 +693,8 @@
         zeros = (0,) * len(dims)
         return pl.BlockSpec(dims, lambda i, *s: zeros)
 
-    def call(kernel, name, grid, ins, outs, scratch, operands, scalars=True, much=False):
+    def call(kernel, name, grid, ins, outs, scratch, operands, scalars=True, estimate=None):
+        estimate = LITTLE if estimate is None else estimate
         spec = pltpu.PrefetchScalarGridSpec(
             num_scalar_prefetch=int(scalars),
             grid=(grid,),
@@ -706,7 +707,7 @@
             grid_spec=spec,
             out_shape=[o[0] for o in outs],
             compiler_params=params(16),
-            cost_estimate=MUCH if much else LITTLE,
+            cost_estimate=estimate,
             name=name,
         )(*operands)
 
@@ -803,7 +804,7 @@
             [(shape((SLOTS // 2 * PIECE1, width), bf16), fixed((SLOTS // 2 * PIECE1, width)))],
             [],
             (scal, a, gl, n2, d),
-            much=pick == 0,
+            estimate=MUCH if pick == 0 else LITTLE,
         )
         return order.did(piece), beside
 
@@ -820,7 +821,7 @@
             [(shape((SLOTS // 2 * PIECE2, width), bf16), fixed((SLOTS // 2 * PIECE2, width)))],
             [],
             (scal, c, z, h, y, dm),
-            much=pick == 0,
+            estimate=SOME if pick == 0 else LITTLE,
         )
         return order.did(piece)
 

time: 174 us -> 174 us (level)
  no operation moved by 1% of the time
where the time goes in v2:
time: 174 us; the launch traced here: 173 us
  Pallas kernels  74.4 us (43%)
  starting transfers between devices  55.4 us (32%)
  waiting for transfers between devices  33.1 us (19%)
  other arithmetic  6.12 us (4%)
  local copies, waits for them, and re-layouts  2.79 us (2%)
    pallas_call x11, Pallas kernels, call(): pl.pallas_call(kernel, grid_spec=spec, out_shape=[o[0] for o in outs], co...  59.2 us
    ppermute x24, starting transfers between devices, flat_permute(): return lax.ppermute(value, ('seq', 'row'), pairs)  39.7 us
    ppermute x24, waiting for transfers between devices, flat_permute(): return lax.ppermute(value, ('seq', 'row'), pairs)  32.3 us
    ppermute x8, starting transfers between devices, passed_along(): lax.ppermute(value, axis, [(source, source + steps) for source in range(l...  15.7 us
    pallas_call x7, Pallas kernels, spread(): pl.pallas_call(functools.partial(spread_kernel, piece=piece, plan=plan, m...  13.2 us
    convert_element_type x10, other arithmetic, added(): return (a.astype(f32) + b.astype(f32)).astype(bf16)  5.98 us
  transfers between devices with their start and end apart: 32, of which 15 were waited for; matrix products, arithmetic and copies ran while one was open for 3% of the time, Pallas kernels for 30%

profile of v2, /device:TPU:0, one launch (start us, length us, event | category | flops | bytes accessed | tf_op | source)
XLA Modules:
  0.0 173.0 jit_solution(10358967849547725545)
XLA Ops:
  0.7 1.0 slice_bitcast_fusion
  1.7 2.4 %collective-permute-start = (bf16[24,512]{1,0:T(8,128)(2,1)S(1)}, bf16[24,512]{1,0:T(8,128)(2,1)S(1)}, u32[]{:S(2)}, u32[]{:S(2)}) collective-permute-start(bf16[24,512]{1,0:T(8,128)(2,1)S(1)} %bitcast.19), channel_id=1, source_target_pairs={{0,4},{4,8},{8,12},{12,16},{16,20},{20,24},{24,28},{1,5},{5,9},{9,... | collective-permute-start | bytes 73736 | tf_op jit(solution)/shard_map/ppermute | solution.py:484
  4.1 3.0 %norm.1.u = bf16[1024,512]{1,0:T(8,128)(2,1)S(1)} custom-call(bf16[8,128,512]{2,1,0:T(8,128)(2,1)} %x.5, bf16[256,256]{1,0:T(8,128)(2,1)} %constant.29.clone.perm.pm, f32[1,512]{1,0:T(1,128)} %bitcast.20), custom_call_target="tpu_custom_call" | custom-call | flops 1024 | bytes 1024 | tf_op jit(solution)/shard_map/norm/pallas_call | solution.py:705
  7.2 6.5 %front.1 = (bf16[1024,512]{1,0:T(8,128)(2,1)S(1)}, bf16[1024,1024]{1,0:T(8,128)(2,1)S(1)}, bf16[1024,1024]{1,0:T(8,128)(2,1)S(1)}, f32[16,1024]{1,0:T(8,128)S(1)}) custom-call(s32[12]{0:T(128)S(1)} %concatenate.17.scal, bf16[1024,512]{1,0:T(8,128)(2,1)S(1)} %norm.1.u, bf16[24,512]{1,0:T(8,128)(2,1)S(1)} %collective-permute-done.edge, f32[1,512]{1,0:T(1,128)} %bitcast.21, ...), custom_call_target="tpu_custom_call" | custom-call | flops 1024 | bytes 1024 | tf_op jit(solution)/shard_map/front/pallas_call | solution.py:705
  13.8 2.8 %collective-permute-start.1 = (f32[16,1024]{1,0:T(8,128)S(1)}, f32[16,1024]{1,0:T(8,128)S(1)}, u32[]{:S(2)}, u32[]{:S(2)}) collective-permute-start(f32[16,1024]{1,0:T(8,128)S(1)} %get-tuple-element.112), channel_id=1, source_target_pairs={{0,4},{1,5},{2,6},{3,7},{4,0},{5,1},{6,2},{7,3},{8,12},{9,13},{10,... | collective-permute-start | bytes 196616 | tf_op jit(solution)/shard_map/ppermute | solution.py:488
  16.6 0.9 collective-permute-done.1.other
  17.5 4.2 %collective-permute-start.4 = (bf16[16,1024]{1,0:T(8,128)(2,1)S(1)}, bf16[16,1024]{1,0:T(8,128)(2,1)S(1)}, u32[]{:S(2)}, u32[]{:S(2)}) collective-permute-start(bf16[16,1024]{1,0:T(8,128)(2,1)S(1)} %pad_maximum_fusion.2), channel_id=1, source_target_pairs={{0,24},{4,28},{1,25},{5,29},{2,26},{6,30},{3,27},{7,31}} | collective-permute-start | bytes 98312 | tf_op jit(solution)/shard_map/ppermute | solution.py:484
  21.8 1.3 collective-permute-start.3
  23.1 2.5 %collective-permute-start.2 = (bf16[16,1024]{1,0:T(8,128)(2,1)S(1)}, bf16[16,1024]{1,0:T(8,128)(2,1)S(1)}, u32[]{:S(2)}, u32[]{:S(2)}) collective-permute-start(bf16[16,1024]{1,0:T(8,128)(2,1)S(1)} %pad_maximum_fusion.2), channel_id=1, source_target_pairs={{0,8},{4,12},{8,16},{12,20},{16,24},{20,28},{1,9},{5,13},{9,17},{1... | collective-permute-start | bytes 98312 | tf_op jit(solution)/shard_map/ppermute | solution.py:484
  25.6 3.5 %da.1 = (bf16[1024,512]{1,0:T(8,128)(2,1)S(1)}, bf16[1024,2048]{1,0:T(8,128)(2,1)S(1)}) custom-call(bf16[8,128,512]{2,1,0:T(8,128)(2,1)S(1)} %copy-done.10, bf16[256,256]{1,0:T(8,128)(2,1)S(1)} %copy-done.8, bf16[2048,512]{1,0:T(8,128)(2,1)S(1)} %copy-done.7), custom_call_target="tpu_custom_call" | custom-call | flops 1024 | bytes 1024 | tf_op jit(solution)/shard_map/da/pallas_call | solution.py:705
  29.2 14.4 %core.1 = (f32[1024,512]{1,0:T(8,128)}, bf16[1024,1024]{1,0:T(8,128)(2,1)S(1)}, bf16[1024,1024]{1,0:T(8,128)(2,1)S(1)}, bf16[1024,512]{1,0:T(8,128)(2,1)S(1)}, b...) custom-call(s32[12]{0:T(128)S(1)} %concatenate.17.scal, ...), custom_call_target="tpu_custom_call" | custom-call | flops 1024 | bytes 1024 | tf_op jit(solution)/shard_map/core/pallas_call | solution.py:705
  43.6 1.2 collective-permute-done.5.fother
  44.8 1.3 collective-permute-start.8
  46.1 1.3 collective-permute-start.7
  47.4 1.3 collective-permute-start.6
  48.7 3.7 %ffn_grad.2 = bf16[2048,512]{1,0:T(8,128)(2,1)S(1)} custom-call(s32[12]{0:T(128)S(1)} %concatenate.17.scal, bf16[1024,2048]{1,0:T(8,128)(2,1)S(1)} %get-tuple-element.136.act, bf16[1024,512]{1,0:T(8,128)(2,1)S(1)} %get-tuple-element.106.gl, bf16[1024,512]{1,0:T(8,128)(2,1)S(1)} %get-tuple-element.121.n2, bf16[1024,2048]{1,0:T(8,128)(2,1)S(1)} %get-tuple-element.127.dp), custom_call_target="tpu_custom_call" | custom-call | flops 1024 | bytes 1024 | tf_op jit(solution)/shard_map/ffn_grad/pallas_call | solution.py:705
  52.7 0.6 collective-permute-done.7.refs_1_
  53.5 3.7 %ffn_grad.3 = bf16[2048,512]{1,0:T(8,128)(2,1)S(1)} custom-call(s32[12]{0:T(128)S(1)} %concatenate.17.scal, bf16[1024,2048]{1,0:T(8,128)(2,1)S(1)} %get-tuple-element.136.act, bf16[1024,512]{1,0:T(8,128)(2,1)S(1)} %get-tuple-element.106.gl, bf16[1024,512]{1,0:T(8,128)(2,1)S(1)} %get-tuple-element.121.n2, bf16[1024,2048]{1,0:T(8,128)(2,1)S(1)} %get-tuple-element.127.dp), custom_call_target="tpu_custom_call" | custom-call | flops 30000001024 | bytes 1024 | tf_op jit(solution)/shard_map/ffn_grad/pallas_call | solution.py:705
  57.2 0.6 add_convert_fusion
  57.8 1.6 collective-permute-start.10
  59.4 3.7 %gates.1 = (bf16[1024,1024]{1,0:T(8,128)(2,1)S(1)}, bf16[1024,1024]{1,0:T(8,128)(2,1)S(1)}, bf16[32,512]{1,0:T(8,128)(2,1)S(1)}, f32[8,1024]{1,0:T(8,128)S(1)}) custom-call(s32[12]{0:T(128)S(1)} %concatenate.17.scal, bf16[1024,1024]{1,0:T(8,128)(2,1)S(1)} %get-tuple-element.116.dh, bf16[1024,1024]{1,0:T(8,128)(2,1)S(1)} %get-tuple-element.110.zl.zl_next.zl_before, ...), custom_call_target="tpu_custom_call" | custom-call | flops 1024 | bytes 1024 | tf_op jit(solution)/shard_map/gates/pallas_call | solution.py:705
  63.1 2.4 %gate_grad.2 = bf16[1536,512]{1,0:T(8,128)(2,1)S(1)} custom-call(s32[12]{0:T(128)S(1)} %concatenate.17.scal, bf16[1024,512]{1,0:T(8,128)(2,1)S(1)} %get-tuple-element.115.c, bf16[1024,1024]{1,0:T(8,128)(2,1)S(1)} %get-tuple-element.143.dkz, bf16[1024,1024]{1,0:T(8,128)(2,1)S(1)} %get-tuple-element.140.dkh, bf16[1024,1024]{1,0:T(8,128)(2,1)S(1)} %get-tuple-element.134.y, ...), custom_call_target="tpu_custom_call" | custom-call | flops 1024 | bytes 1024 | tf_op jit(solution)/shard_map/gate_grad/pallas_call | solution.py:705
  65.6 1.5 collective-permute-start.12
  67.1 5.7 %output.1 = bf16[8,128,512]{2,1,0:T(8,128)(2,1)} custom-call(f32[1024,512]{1,0:T(8,128)} %get-tuple-element.113.r1, bf16[1024,2048]{1,0:T(8,128)(2,1)S(1)} %get-tuple-element.136.act, bf16[256,256]{1,0:T(8,128)(2,1)S(1)} %copy-done.11, bf16[2048,512]{1,0:T(8,128)(2,1)S(1)} %copy-done.7), custom_call_target="tpu_custom_call" | custom-call | flops 1024 | bytes 1024 | tf_op jit(solution)/shard_map/output/pallas_call | solution.py:705
  72.7 1.3 add_convert_fusion.4
  74.0 1.5 collective-permute-start.14
  75.5 2.4 %gate_grad.3 = bf16[1536,512]{1,0:T(8,128)(2,1)S(1)} custom-call(s32[12]{0:T(128)S(1)} %concatenate.17.scal, bf16[1024,512]{1,0:T(8,128)(2,1)S(1)} %get-tuple-element.115.c, bf16[1024,1024]{1,0:T(8,128)(2,1)S(1)} %get-tuple-element.143.dkz, bf16[1024,1024]{1,0:T(8,128)(2,1)S(1)} %get-tuple-element.140.dkh, bf16[1024,1024]{1,0:T(8,128)(2,1)S(1)} %get-tuple-element.134.y, ...), custom_call_target="tpu_custom_call" | custom-call | flops 8000000000 | bytes 1024 | tf_op jit(solution)/shard_map/gate_grad/pallas_call | solution.py:705
  78.0 1.3 add_convert_fusion.2
  79.3 1.4 collective-permute-start.13
  80.8 1.6 copy-done.6
  82.4 10.2 %tail.1 = (bf16[8,128,512]{2,1,0:T(8,128)(2,1)}, f32[40,512]{1,0:T(8,128)S(1)}) custom-call(bf16[8,128,512]{2,1,0:T(8,128)(2,1)} %x.5, f32[1024,512]{1,0:T(8,128)} %get-tuple-element.137.dr1, bf16[1024,1024]{1,0:T(8,128)(2,1)S(1)} %copy-done.4, bf16[1024,1024]{1,0:T(8,128)(2,1)S(1)} %copy-done.6, bf16[256,256]{1,0:T(8,128)(2,1)} %constant.29.clone.perm.pm, ...), custom_call_target="tpu_custom_call" | custom-call | flops 1024 | bytes 1024 | tf_op jit(solution)/shard_map/tail/pallas_call | solution.py:705
  92.6 1.2 add_convert_fusion.8
  93.8 2.2 %collective-permute-start.16 = (bf16[256,512]{1,0:T(8,128)(2,1)S(1)}, bf16[256,512]{1,0:T(8,128)(2,1)S(1)}, u32[]{:S(2)}, u32[]{:S(2)}) collective-permute-start(bf16[256,512]{1,0:T(8,128)(2,1)S(1)} %get-tuple-element.212), channel_id=1, source_target_pairs={{0,8},{1,9},{2,10},{3,11},{4,20},{5,21},{6,22},{7,23},{8,0},{9,1},... | collective-permute-start | bytes 786440 | tf_op jit(solution)/shard_map/ppermute | solution.py:488
  96.0 1.3 add_convert_fusion.6
  97.4 1.2 collective-permute-start.15
  98.6 4.4 %collective-permute-done.16 = bf16[256,512]{1,0:T(8,128)(2,1)S(1)} collective-permute-done((bf16[256,512]{1,0:T(8,128)(2,1)S(1)}, bf16[256,512]{1,0:T(8,128)(2,1)S(1)}, u32[]{:S(2)}, u32[]{:S(2)}) %collective-permute-start.16) | collective-permute-done | bytes 262176 | tf_op jit(solution)/shard_map/ppermute | solution.py:488
  103.0 3.1 %collective-permute-start.18 = (bf16[128,512]{1,0:T(8,128)(2,1)S(1)}, bf16[128,512]{1,0:T(8,128)(2,1)S(1)}, u32[]{:S(2)}, u32[]{:S(2)}) collective-permute-start(bf16[128,512]{1,0:T(8,128)(2,1)S(1)} %add_convert_fusion.14), channel_id=1, source_target_pairs={{0,16},{1,17},{2,18},{3,19},{4,12},{5,13},{6,14},{7,15},{8,24},{9,... | collective-permute-start | bytes 393224 | tf_op jit(solution)/shard_map/ppermute | solution.py:488
  106.3 2.5 %collective-permute-start.17 = (bf16[192,512]{1,0:T(8,128)(2,1)S(1)}, bf16[192,512]{1,0:T(8,128)(2,1)S(1)}, u32[]{:S(2)}, u32[]{:S(2)}) collective-permute-start(bf16[192,512]{1,0:T(8,128)(2,1)S(1)} %get-tuple-element.213), channel_id=1, source_target_pairs={{0,8},{1,9},{2,10},{3,11},{4,20},{5,21},{6,22},{7,23},{8,0},{9,1},... | collective-permute-start | bytes 589832 | tf_op jit(solution)/shard_map/ppermute | solution.py:488
  108.8 0.5 collective-permute-done.18
  109.4 3.5 %collective-permute-start.20 = (bf16[128,512]{1,0:T(8,128)(2,1)S(1)}, bf16[128,512]{1,0:T(8,128)(2,1)S(1)}, u32[]{:S(2)}, u32[]{:S(2)}) collective-permute-start(bf16[128,512]{1,0:T(8,128)(2,1)S(1)} %add_convert_fusion.12.mine), channel_id=1, source_target_pairs={{0,16},{1,17},{2,18},{3,19},{4,12},{5,13},{6,14},{7,15},{8,24},{9,... | collective-permute-start | bytes 393224 | tf_op jit(solution)/shard_map/ppermute | solution.py:488
  112.9 3.7 %collective-permute-done.17 = bf16[192,512]{1,0:T(8,128)(2,1)S(1)} collective-permute-done((bf16[192,512]{1,0:T(8,128)(2,1)S(1)}, bf16[192,512]{1,0:T(8,128)(2,1)S(1)}, u32[]{:S(2)}, u32[]{:S(2)}) %collective-permute-start.17) | collective-permute-done | bytes 196640 | tf_op jit(solution)/shard_map/ppermute | solution.py:488
  116.7 0.5 collective-permute-start.19
  117.2 9.4 %collective-permute-start.23 = (bf16[256,512]{1,0:T(8,128)(2,1)S(1)}, bf16[256,512]{1,0:T(8,128)(2,1)S(1)}, u32[]{:S(2)}, u32[]{:S(2)}) collective-permute-start(bf16[256,512]{1,0:T(8,128)(2,1)S(1)} %chain.3.mine), channel_id=1, source_target_pairs={{0,8},{1,9},{2,10},{3,11},{4,20},{5,21},{6,22},{7,23},{8,0},{9,1},... | collective-permute-start | bytes 786440 | tf_op jit(solution)/shard_map/ppermute | solution.py:488
  126.5 1.0 collective-permute-done.19
  127.6 2.4 %collective-permute-start.21 = (bf16[112,512]{1,0:T(8,128)(2,1)S(1)}, bf16[112,512]{1,0:T(8,128)(2,1)S(1)}, u32[]{:S(2)}, u32[]{:S(2)}) collective-permute-start(bf16[112,512]{1,0:T(8,128)(2,1)S(1)} %pad_maximum_fusion.mine), channel_id=1, source_target_pairs={{0,16},{1,17},{2,18},{3,19},{4,12},{5,13},{6,14},{7,15},{8,24},{9,... | collective-permute-start | bytes 344072 | tf_op jit(solution)/shard_map/ppermute | solution.py:488
  130.0 5.6 %collective-permute-done.21.recv = bf16[112,512]{1,0:T(8,128)(2,1)S(1)} collective-permute-done((bf16[112,512]{1,0:T(8,128)(2,1)S(1)}, bf16[112,512]{1,0:T(8,128)(2,1)S(1)}, u32[]{:S(2)}, u32[]{:S(2)}) %collective-permute-start.21) | collective-permute-done | bytes 114720 | tf_op jit(solution)/shard_map/ppermute | solution.py:488
  135.8 1.4 collective-permute-start.25
  137.2 4.4 %collective-permute-done.22.recv = bf16[208,512]{1,0:T(8,128)(2,1)S(1)} collective-permute-done((bf16[208,512]{1,0:T(8,128)(2,1)S(1)}, bf16[208,512]{1,0:T(8,128)(2,1)S(1)}, u32[]{:S(2)}, u32[]{:S(2)}) %collective-permute-start.22) | collective-permute-done | bytes 213024 | tf_op jit(solution)/shard_map/ppermute | solution.py:488
  141.6 1.3 collective-permute-start.24
  142.9 2.1 %collective-permute-done.25.recv = bf16[512,512]{1,0:T(8,128)(2,1)S(1)} collective-permute-done((bf16[512,512]{1,0:T(8,128)(2,1)S(1)}, bf16[512,512]{1,0:T(8,128)(2,1)S(1)}, u32[]{:S(2)}, u32[]{:S(2)}) %collective-permute-start.25) | collective-permute-done | bytes 524320 | tf_op jit(solution)/shard_map/ppermute | solution.py:488
  145.2 1.4 collective-permute-start.28
  146.7 4.3 %collective-permute-done.24.recv = bf16[400,512]{1,0:T(8,128)(2,1)S(1)} collective-permute-done((bf16[400,512]{1,0:T(8,128)(2,1)S(1)}, bf16[400,512]{1,0:T(8,128)(2,1)S(1)}, u32[]{:S(2)}, u32[]{:S(2)}) %collective-permute-start.24) | collective-permute-done | bytes 409632 | tf_op jit(solution)/shard_map/ppermute | solution.py:488
  151.1 1.5 collective-permute-start.26
  152.5 2.0 %spread_ffn.4 = (f32[2048,512]{1,0:T(8,128)}, f32[512,2048]{1,0:T(8,128)}) custom-call(s32[12]{0:T(128)S(1)} %concatenate.17.scal, bf16[1024,512]{1,0:T(8,128)(2,1)S(1)} %chain.5.src), custom_call_target="tpu_custom_call" | custom-call | flops 8000000000 | bytes 1024 | tf_op jit(solution)/shard_map/spread_ffn/pallas_call | solution.py:440
  154.5 2.0 %spread_ffn.5 = (f32[2048,512]{1,0:T(8,128)}, f32[512,2048]{1,0:T(8,128)}) custom-call(s32[12]{0:T(128)S(1)} %concatenate.17.scal, bf16[1024,512]{1,0:T(8,128)(2,1)S(1)} %collective-permute-done.29.src, f32[2048,512]{1,0:T(8,128)} %get-tuple-element.167.refs_0_, f32[512,2048]{1,0:T(8,128)} %get-tuple-element.169.refs_1_), custom_call_target="tpu_custom_call", output_to_operand_aliasing={{0}: (2, {}), {1}: (3, {})} | custom-call | flops 8000000000 | bytes 1024 | tf_op jit(solution)/shard_map/spread_ffn/pallas_call | solution.py:440
  156.5 3.6 %collective-permute-done.28.src = bf16[1024,512]{1,0:T(8,128)(2,1)S(1)} collective-permute-done((bf16[1024,512]{1,0:T(8,128)(2,1)S(1)}, bf16[1024,512]{1,0:T(8,128)(2,1)S(1)}, u32[]{:S(2)}, u32[]{:S(2)}) %collective-permute-start.28) | collective-permute-done | bytes 1048608 | tf_op jit(solution)/shard_map/ppermute | solution.py:488
  160.1 0.9 collective-permute-start.30
  161.0 2.0 %spread_ffn.6 = (f32[2048,512]{1,0:T(8,128)}, f32[512,2048]{1,0:T(8,128)}) custom-call(s32[12]{0:T(128)S(1)} %concatenate.17.scal, bf16[1024,512]{1,0:T(8,128)(2,1)S(1)} %collective-permute-done.28.src, f32[2048,512]{1,0:T(8,128)} %get-tuple-element.170.refs_0_, f32[512,2048]{1,0:T(8,128)} %get-tuple-element.173.refs_1_), custom_call_target="tpu_custom_call", output_to_operand_aliasing={{0}: (2, {}), {1}: (3, {})} | custom-call | flops 8000000000 | bytes 1024 | tf_op jit(solution)/shard_map/spread_ffn/pallas_call | solution.py:440
  163.0 1.7 %spread_gates.3 = (f32[512,1024]{1,0:T(8,128)}, f32[512,1024]{1,0:T(8,128)}, f32[1024,512]{1,0:T(8,128)}) custom-call(s32[12]{0:T(128)S(1)} %concatenate.17.scal, bf16[784,512]{1,0:T(8,128)(2,1)S(1)} %get-tuple-element.175.src), custom_call_target="tpu_custom_call" | custom-call | flops 8000000000 | bytes 1024 | tf_op jit(solution)/shard_map/spread_gates/pallas_call | solution.py:440
  164.7 2.0 %spread_ffn.7 = (f32[2048,512]{1,0:T(8,128)}, f32[512,2048]{1,0:T(8,128)}) custom-call(s32[12]{0:T(128)S(1)} %concatenate.17.scal, bf16[1024,512]{1,0:T(8,128)(2,1)S(1)} %collective-permute-done.30.src, f32[2048,512]{1,0:T(8,128)} %get-tuple-element.174.refs_0_, f32[512,2048]{1,0:T(8,128)} %get-tuple-element.178.refs_1_), custom_call_target="tpu_custom_call", output_to_operand_aliasing={{0}: (2, {}), {1}: (3, {})} | custom-call | flops 8000000000 | bytes 1024 | tf_op jit(solution)/shard_map/spread_ffn/pallas_call | solution.py:440
  166.7 1.7 %spread_gates.4 = (f32[512,1024]{1,0:T(8,128)}, f32[512,1024]{1,0:T(8,128)}, f32[1024,512]{1,0:T(8,128)}) custom-call(s32[12]{0:T(128)S(1)} %concatenate.17.scal, bf16[784,512]{1,0:T(8,128)(2,1)S(1)} %collective-permute-done.27.src.theirs, f32[512,1024]{1,0:T(8,128)} %get-tuple-element.176.refs_0_, ...), custom_call_target="tpu_custom_call", output_to_operand_aliasing={{0}: (2, {}), {1}: (3, {}), {2}: (4, {})} | custom-call | flops 8000000000 | bytes 1024 | tf_op jit(solution)/shard_map/spread_gates/pallas_call | solution.py:440
  168.7 0.6 collective-permute-start.31
  169.3 1.7 %spread_gates.5 = (f32[512,1024]{1,0:T(8,128)}, f32[512,1024]{1,0:T(8,128)}, f32[1024,512]{1,0:T(8,128)}) custom-call(s32[12]{0:T(128)S(1)} %concatenate.17.scal, bf16[784,512]{1,0:T(8,128)(2,1)S(1)} %collective-permute-done.26.src.rest, f32[512,1024]{1,0:T(8,128)} %get-tuple-element.183.refs_0_, ...), custom_call_target="tpu_custom_call", output_to_operand_aliasing={{0}: (2, {}), {1}: (3, {}), {2}: (4, {})} | custom-call | flops 8000000000 | bytes 1024 | tf_op jit(solution)/shard_map/spread_gates/pallas_call | solution.py:440
  171.3 1.8 %spread_last.1 = (f32[512,1024]{1,0:T(8,128)}, f32[512,1024]{1,0:T(8,128)}, f32[1024,512]{1,0:T(8,128)}, f32[1,512]{1,0:T(1,128)}, f32[4,512]{1,0:T(4,128)}, /*index=5*/f32[1,512]{1,0:T(1,128)}, f32[1,1024]{1,0:T(1,128)}) custom-call(s32[12]{0:T(128)S(1)} %concatenate.17.scal, ...), custom_call_target="tpu_custom_call", output_to_operand_aliasing={{0}: (5, {}), {1}: (6, {}), {2}: (7, {})} | custom-call | flops 8000000000 | bytes 1024 | tf_op jit(solution)/shard_map/spread_last/pallas_call | solution.py:418
  (81 shorter events, 2.1 us)
Async XLA Ops:
  0.6 6.5 %copy-start.14 = (s32[8]{0:T(128)S(1)}, s32[8]{0:T(128)}, u32[]{:S(2)}) copy-start(s32[8]{0:T(128)} %param.15) | copy-start | bytes 100
  0.7 6.6 %copy-start.2 = (bf16[512,1024]{1,0:T(8,128)(2,1)S(1)}, bf16[512,1024]{1,0:T(8,128)(2,1)}, u32[]{:S(2)}) copy-start(bf16[512,1024]{1,0:T(8,128)(2,1)} %wc.3) | copy-start | bytes 3145732
  0.7 6.6 %copy-start.1 = (bf16[512,1024]{1,0:T(8,128)(2,1)S(1)}, bf16[512,1024]{1,0:T(8,128)(2,1)}, u32[]{:S(2)}) copy-start(bf16[512,1024]{1,0:T(8,128)(2,1)} %wg.3) | copy-start | bytes 3145732
  1.7 5.5 %collective-permute-start = (bf16[24,512]{1,0:T(8,128)(2,1)S(1)}, bf16[24,512]{1,0:T(8,128)(2,1)S(1)}, u32[]{:S(2)}, u32[]{:S(2)}) collective-permute-start(bf16[24,512]{1,0:T(8,128)(2,1)S(1)} %bitcast.19), channel_id=1, source_target_pairs={{0,4},{4,8},{8,12},{12,16},{16,20},{20,24},{24,28},{1,5},{5,9},{9,... | collective-permute-start | bytes 73736 | tf_op jit(solution)/shard_map/ppermute | solution.py:484
  7.1 18.5 %copy-start.8 = (bf16[256,256]{1,0:T(8,128)(2,1)S(1)}, bf16[256,256]{1,0:T(8,128)(2,1)}, u32[]{:S(2)}) copy-start(bf16[256,256]{1,0:T(8,128)(2,1)} %constant.29.clone.perm.pm) | copy-start | bytes 393220
  7.2 18.4 %copy-start.7 = (bf16[2048,512]{1,0:T(8,128)(2,1)S(1)}, bf16[2048,512]{1,0:T(8,128)(2,1)}, u32[]{:S(2)}) copy-start(bf16[2048,512]{1,0:T(8,128)(2,1)} %wd.3) | copy-start | bytes 6291460
  7.2 18.4 %copy-start.10 = (bf16[8,128,512]{2,1,0:T(8,128)(2,1)S(1)}, bf16[8,128,512]{2,1,0:T(8,128)(2,1)}, u32[]{:S(2)}) copy-start(bf16[8,128,512]{2,1,0:T(8,128)(2,1)} %g.1) | copy-start | bytes 3145732
  13.8 15.4 %copy-start = (bf16[8,128,512]{2,1,0:T(8,128)(2,1)S(1)}, bf16[8,128,512]{2,1,0:T(8,128)(2,1)}, u32[]{:S(2)}) copy-start(bf16[8,128,512]{2,1,0:T(8,128)(2,1)} %x.5) | copy-start | bytes 3145732
  13.8 15.4 %copy-start.9 = (bf16[512,2048]{1,0:T(8,128)(2,1)S(1)}, bf16[512,2048]{1,0:T(8,128)(2,1)}, u32[]{:S(2)}) copy-start(bf16[512,2048]{1,0:T(8,128)(2,1)} %refs_5_.1) | copy-start | bytes 6291460
  13.8 15.4 %copy-start.12 = (f32[512]{0:T(512)S(1)}, f32[512]{0:T(512)}, u32[]{:S(2)}) copy-start(f32[512]{0:T(512)} %param.22) | copy-start | bytes 6148
  13.8 3.7 %collective-permute-start.1 = (f32[16,1024]{1,0:T(8,128)S(1)}, f32[16,1024]{1,0:T(8,128)S(1)}, u32[]{:S(2)}, u32[]{:S(2)}) collective-permute-start(f32[16,1024]{1,0:T(8,128)S(1)} %get-tuple-element.112), channel_id=1, source_target_pairs={{0,4},{1,5},{2,6},{3,7},{4,0},{5,1},{6,2},{7,3},{8,12},{9,13},{10,... | collective-permute-start | bytes 196616 | tf_op jit(solution)/shard_map/ppermute | solution.py:488
  17.5 11.6 %collective-permute-start.4 = (bf16[16,1024]{1,0:T(8,128)(2,1)S(1)}, bf16[16,1024]{1,0:T(8,128)(2,1)S(1)}, u32[]{:S(2)}, u32[]{:S(2)}) collective-permute-start(bf16[16,1024]{1,0:T(8,128)(2,1)S(1)} %pad_maximum_fusion.2), channel_id=1, source_target_pairs={{0,24},{4,28},{1,25},{5,29},{2,26},{6,30},{3,27},{7,31}} | collective-permute-start | bytes 98312 | tf_op jit(solution)/shard_map/ppermute | solution.py:484
  21.8 7.4 %collective-permute-start.3 = (bf16[16,1024]{1,0:T(8,128)(2,1)S(1)}, bf16[16,1024]{1,0:T(8,128)(2,1)S(1)}, u32[]{:S(2)}, u32[]{:S(2)}) collective-permute-start(bf16[16,1024]{1,0:T(8,128)(2,1)S(1)} %pad_maximum_fusion.2), channel_id=1, source_target_pairs={{0,16},{4,20},{8,24},{12,28},{1,17},{5,21},{9,25},{13,29},{2,18},{... | collective-permute-start | bytes 98312 | tf_op jit(solution)/shard_map/ppermute | solution.py:484
  23.1 6.1 %collective-permute-start.2 = (bf16[16,1024]{1,0:T(8,128)(2,1)S(1)}, bf16[16,1024]{1,0:T(8,128)(2,1)S(1)}, u32[]{:S(2)}, u32[]{:S(2)}) collective-permute-start(bf16[16,1024]{1,0:T(8,128)(2,1)S(1)} %pad_maximum_fusion.2), channel_id=1, source_target_pairs={{0,8},{4,12},{8,16},{12,20},{16,24},{20,28},{1,9},{5,13},{9,17},{1... | collective-permute-start | bytes 98312 | tf_op jit(solution)/shard_map/ppermute | solution.py:484
  43.6 1.2 collective-permute-start.5
  44.8 7.8 %collective-permute-start.8 = (bf16[16,1024]{1,0:T(8,128)(2,1)S(1)}, bf16[16,1024]{1,0:T(8,128)(2,1)S(1)}, u32[]{:S(2)}, u32[]{:S(2)}) collective-permute-start(bf16[16,1024]{1,0:T(8,128)(2,1)S(1)} %pad_maximum_fusion.1), channel_id=1, source_target_pairs={{24,0},{28,4},{25,1},{29,5},{26,2},{30,6},{27,3},{31,7}} | collective-permute-start | bytes 98312 | tf_op jit(solution)/shard_map/ppermute | solution.py:484
  46.1 7.1 %collective-permute-start.7 = (bf16[16,1024]{1,0:T(8,128)(2,1)S(1)}, bf16[16,1024]{1,0:T(8,128)(2,1)S(1)}, u32[]{:S(2)}, u32[]{:S(2)}) collective-permute-start(bf16[16,1024]{1,0:T(8,128)(2,1)S(1)} %pad_maximum_fusion.1), channel_id=1, source_target_pairs={{16,0},{20,4},{24,8},{28,12},{17,1},{21,5},{25,9},{29,13},{18,2},{... | collective-permute-start | bytes 98312 | tf_op jit(solution)/shard_map/ppermute | solution.py:484
  47.4 6.1 %collective-permute-start.6 = (bf16[16,1024]{1,0:T(8,128)(2,1)S(1)}, bf16[16,1024]{1,0:T(8,128)(2,1)S(1)}, u32[]{:S(2)}, u32[]{:S(2)}) collective-permute-start(bf16[16,1024]{1,0:T(8,128)(2,1)S(1)} %pad_maximum_fusion.1), channel_id=1, source_target_pairs={{8,0},{12,4},{16,8},{20,12},{24,16},{28,20},{9,1},{13,5},{17,9},{2... | collective-permute-start | bytes 98312 | tf_op jit(solution)/shard_map/ppermute | solution.py:484
  52.4 4.7 %collective-permute-start.9 = (bf16[2048,512]{1,0:T(8,128)(2,1)S(1)}, bf16[2048,512]{1,0:T(8,128)(2,1)S(1)}, u32[]{:S(2)}, u32[]{:S(2)}) collective-permute-start(bf16[2048,512]{1,0:T(8,128)(2,1)S(1)} %ffn_grad.2), channel_id=1, source_target_pairs={{0,4},{1,5},{2,6},{3,7},{4,0},{5,1},{6,2},{7,3},{8,12},{9,13},{10,... | collective-permute-start | bytes 6291464 | tf_op jit(solution)/shard_map/ppermute | solution.py:488
  57.8 14.9 %collective-permute-start.10 = (bf16[1024,512]{1,0:T(8,128)(2,1)S(1)}, bf16[1024,512]{1,0:T(8,128)(2,1)S(1)}, u32[]{:S(2)}, u32[]{:S(2)}) collective-permute-start(bf16[1024,512]{1,0:T(8,128)(2,1)S(1)} %get-tuple-element.204.refs_5_), channel_id=1, source_target_pairs={{0,1},{1,0},{2,3},{3,2},{4,6},{5,7},{6,4},{7,5},{8,9},{9,8},{10,11... | collective-permute-start | bytes 3145736 | tf_op jit(solution)/shard_map/ppermute | solution.py:488
  63.1 12.5 %copy-start.3 = (bf16[1024,1024]{1,0:T(8,128)(2,1)}, bf16[1024,1024]{1,0:T(8,128)(2,1)S(1)}, u32[]{:S(2)}) copy-start(bf16[1024,1024]{1,0:T(8,128)(2,1)S(1)} %get-tuple-element.143.dkz) | copy-start | bytes 6291460
  63.1 12.4 %copy-start.5 = (bf16[1024,1024]{1,0:T(8,128)(2,1)}, bf16[1024,1024]{1,0:T(8,128)(2,1)S(1)}, u32[]{:S(2)}) copy-start(bf16[1024,1024]{1,0:T(8,128)(2,1)S(1)} %get-tuple-element.140.dkh) | copy-start | bytes 6291460
  63.1 4.0 %copy-start.11 = (bf16[256,256]{1,0:T(8,128)(2,1)S(1)}, bf16[256,256]{1,0:T(8,128)(2,1)}, u32[]{:S(2)}) copy-start(bf16[256,256]{1,0:T(8,128)(2,1)} %constant.30.clone.perm.back_pm) | copy-start | bytes 393220
  65.5 12.5 %collective-permute-start.11 = (bf16[1536,512]{1,0:T(8,128)(2,1)S(1)}, bf16[1536,512]{1,0:T(8,128)(2,1)S(1)}, u32[]{:S(2)}, u32[]{:S(2)}) collective-permute-start(bf16[1536,512]{1,0:T(8,128)(2,1)S(1)} %gate_grad.2), channel_id=1, source_target_pairs={{0,4},{1,5},{2,6},{3,7},{4,0},{5,1},{6,2},{7,3},{8,12},{9,13},{10,... | collective-permute-start | bytes 4718600 | tf_op jit(solution)/shard_map/ppermute | solution.py:488
  65.6 12.4 %collective-permute-start.12 = (bf16[24,512]{1,0:T(8,128)(2,1)S(1)}, bf16[24,512]{1,0:T(8,128)(2,1)S(1)}, u32[]{:S(2)}, u32[]{:S(2)}) collective-permute-start(bf16[24,512]{1,0:T(8,128)(2,1)S(1)} %slice.134), channel_id=1, source_target_pairs={{4,0},{8,4},{12,8},{16,12},{20,16},{24,20},{28,24},{5,1},{9,5},{13... | collective-permute-start | bytes 73736 | tf_op jit(solution)/shard_map/ppermute | solution.py:484
  74.0 18.6 %collective-permute-start.14 = (bf16[512,512]{1,0:T(8,128)(2,1)}, bf16[512,512]{1,0:T(8,128)(2,1)}, u32[]{:S(2)}, u32[]{:S(2)}) collective-permute-start(bf16[512,512]{1,0:T(8,128)(2,1)} %get-tuple-element.208), channel_id=1, source_target_pairs={{0,2},{1,3},{2,0},{3,1},{4,5},{5,4},{6,7},{7,6},{8,10},{9,11},{10,... | collective-permute-start | bytes 1572872 | tf_op jit(solution)/shard_map/ppermute | solution.py:488
  77.9 2.8 %copy-start.4 = (bf16[1024,1024]{1,0:T(8,128)(2,1)S(1)}, bf16[1024,1024]{1,0:T(8,128)(2,1)}, u32[]{:S(2)}) copy-start(bf16[1024,1024]{1,0:T(8,128)(2,1)} %copy-done.3) | copy-start | bytes 6291460
  79.3 16.7 %collective-permute-start.13 = (bf16[768,512]{1,0:T(8,128)(2,1)}, bf16[768,512]{1,0:T(8,128)(2,1)}, u32[]{:S(2)}, u32[]{:S(2)}) collective-permute-start(bf16[768,512]{1,0:T(8,128)(2,1)} %get-tuple-element.206), channel_id=1, source_target_pairs={{0,1},{1,0},{2,3},{3,2},{4,6},{5,7},{6,4},{7,5},{8,9},{9,8},{10,11... | collective-permute-start | bytes 2359304 | tf_op jit(solution)/shard_map/ppermute | solution.py:488
  80.8 1.6 copy-start.6
  82.4 10.2 %copy-start.13 = (bf16[512,512]{1,0:T(8,128)(2,1)S(1)}, bf16[512,512]{1,0:T(8,128)(2,1)}, u32[]{:S(2)}) copy-start(bf16[512,512]{1,0:T(8,128)(2,1)} %get-tuple-element.207) | copy-start | bytes 1572868
  93.8 9.2 %collective-permute-start.16 = (bf16[256,512]{1,0:T(8,128)(2,1)S(1)}, bf16[256,512]{1,0:T(8,128)(2,1)S(1)}, u32[]{:S(2)}, u32[]{:S(2)}) collective-permute-start(bf16[256,512]{1,0:T(8,128)(2,1)S(1)} %get-tuple-element.212), channel_id=1, source_target_pairs={{0,8},{1,9},{2,10},{3,11},{4,20},{5,21},{6,22},{7,23},{8,0},{9,1},... | collective-permute-start | bytes 786440 | tf_op jit(solution)/shard_map/ppermute | solution.py:488
  97.4 8.8 %collective-permute-start.15 = (bf16[384,512]{1,0:T(8,128)(2,1)S(1)}, bf16[384,512]{1,0:T(8,128)(2,1)S(1)}, u32[]{:S(2)}, u32[]{:S(2)}) collective-permute-start(bf16[384,512]{1,0:T(8,128)(2,1)S(1)} %get-tuple-element.209), channel_id=1, source_target_pairs={{0,2},{1,3},{2,0},{3,1},{4,5},{5,4},{6,7},{7,6},{8,10},{9,11},{10,... | collective-permute-start | bytes 1179656 | tf_op jit(solution)/shard_map/ppermute | solution.py:488
  103.0 6.3 %collective-permute-start.18 = (bf16[128,512]{1,0:T(8,128)(2,1)S(1)}, bf16[128,512]{1,0:T(8,128)(2,1)S(1)}, u32[]{:S(2)}, u32[]{:S(2)}) collective-permute-start(bf16[128,512]{1,0:T(8,128)(2,1)S(1)} %add_convert_fusion.14), channel_id=1, source_target_pairs={{0,16},{1,17},{2,18},{3,19},{4,12},{5,13},{6,14},{7,15},{8,24},{9,... | collective-permute-start | bytes 393224 | tf_op jit(solution)/shard_map/ppermute | solution.py:488
  106.3 10.3 %collective-permute-start.17 = (bf16[192,512]{1,0:T(8,128)(2,1)S(1)}, bf16[192,512]{1,0:T(8,128)(2,1)S(1)}, u32[]{:S(2)}, u32[]{:S(2)}) collective-permute-start(bf16[192,512]{1,0:T(8,128)(2,1)S(1)} %get-tuple-element.213), channel_id=1, source_target_pairs={{0,8},{1,9},{2,10},{3,11},{4,20},{5,21},{6,22},{7,23},{8,0},{9,1},... | collective-permute-start | bytes 589832 | tf_op jit(solution)/shard_map/ppermute | solution.py:488
  109.4 7.8 %collective-permute-start.20 = (bf16[128,512]{1,0:T(8,128)(2,1)S(1)}, bf16[128,512]{1,0:T(8,128)(2,1)S(1)}, u32[]{:S(2)}, u32[]{:S(2)}) collective-permute-start(bf16[128,512]{1,0:T(8,128)(2,1)S(1)} %add_convert_fusion.12.mine), channel_id=1, source_target_pairs={{0,16},{1,17},{2,18},{3,19},{4,12},{5,13},{6,14},{7,15},{8,24},{9,... | collective-permute-start | bytes 393224 | tf_op jit(solution)/shard_map/ppermute | solution.py:488
  116.7 10.9 %collective-permute-start.19 = (bf16[96,512]{1,0:T(8,128)(2,1)S(1)}, bf16[96,512]{1,0:T(8,128)(2,1)S(1)}, u32[]{:S(2)}, u32[]{:S(2)}) collective-permute-start(bf16[96,512]{1,0:T(8,128)(2,1)S(1)} %add_convert_fusion.16), channel_id=1, source_target_pairs={{0,16},{1,17},{2,18},{3,19},{4,12},{5,13},{6,14},{7,15},{8,24},{9,... | collective-permute-start | bytes 294920 | tf_op jit(solution)/shard_map/ppermute | solution.py:488
  117.2 18.6 %collective-permute-start.23 = (bf16[256,512]{1,0:T(8,128)(2,1)S(1)}, bf16[256,512]{1,0:T(8,128)(2,1)S(1)}, u32[]{:S(2)}, u32[]{:S(2)}) collective-permute-start(bf16[256,512]{1,0:T(8,128)(2,1)S(1)} %chain.3.mine), channel_id=1, source_target_pairs={{0,8},{1,9},{2,10},{3,11},{4,20},{5,21},{6,22},{7,23},{8,0},{9,1},... | collective-permute-start | bytes 786440 | tf_op jit(solution)/shard_map/ppermute | solution.py:488
  127.6 8.0 %collective-permute-start.21 = (bf16[112,512]{1,0:T(8,128)(2,1)S(1)}, bf16[112,512]{1,0:T(8,128)(2,1)S(1)}, u32[]{:S(2)}, u32[]{:S(2)}) collective-permute-start(bf16[112,512]{1,0:T(8,128)(2,1)S(1)} %pad_maximum_fusion.mine), channel_id=1, source_target_pairs={{0,16},{1,17},{2,18},{3,19},{4,12},{5,13},{6,14},{7,15},{8,24},{9,... | collective-permute-start | bytes 344072 | tf_op jit(solution)/shard_map/ppermute | solution.py:488
  135.7 5.9 %collective-permute-start.22 = (bf16[208,512]{1,0:T(8,128)(2,1)S(1)}, bf16[208,512]{1,0:T(8,128)(2,1)S(1)}, u32[]{:S(2)}, u32[]{:S(2)}) collective-permute-start(bf16[208,512]{1,0:T(8,128)(2,1)S(1)} %get-tuple-element.157.mine), channel_id=1, source_target_pairs={{0,8},{1,9},{2,10},{3,11},{4,20},{5,21},{6,22},{7,23},{8,0},{9,1},... | collective-permute-start | bytes 638984 | tf_op jit(solution)/shard_map/ppermute | solution.py:488
  135.8 9.2 %collective-permute-start.25 = (bf16[512,512]{1,0:T(8,128)(2,1)S(1)}, bf16[512,512]{1,0:T(8,128)(2,1)S(1)}, u32[]{:S(2)}, u32[]{:S(2)}) collective-permute-start(bf16[512,512]{1,0:T(8,128)(2,1)S(1)} %chain.4.mine), channel_id=1, source_target_pairs={{0,2},{1,3},{2,0},{3,1},{4,5},{5,4},{6,7},{7,6},{8,10},{9,11},{10,... | collective-permute-start | bytes 1572872 | tf_op jit(solution)/shard_map/ppermute | solution.py:488
  141.6 9.3 %collective-permute-start.24 = (bf16[400,512]{1,0:T(8,128)(2,1)S(1)}, bf16[400,512]{1,0:T(8,128)(2,1)S(1)}, u32[]{:S(2)}, u32[]{:S(2)}) collective-permute-start(bf16[400,512]{1,0:T(8,128)(2,1)S(1)} %get-tuple-element.161.mine), channel_id=1, source_target_pairs={{0,2},{1,3},{2,0},{3,1},{4,5},{5,4},{6,7},{7,6},{8,10},{9,11},{10,... | collective-permute-start | bytes 1228808 | tf_op jit(solution)/shard_map/ppermute | solution.py:488
  145.2 9.3 %collective-permute-start.29 = (bf16[1024,512]{1,0:T(8,128)(2,1)S(1)}, bf16[1024,512]{1,0:T(8,128)(2,1)S(1)}, u32[]{:S(2)}, u32[]{:S(2)}) collective-permute-start(bf16[1024,512]{1,0:T(8,128)(2,1)S(1)} %chain.5.src), channel_id=1, source_target_pairs={{0,4},{1,5},{2,6},{3,7},{4,0},{5,1},{6,2},{7,3},{8,12},{9,13},{10,... | collective-permute-start | bytes 3145736 | tf_op jit(solution)/shard_map/ppermute | solution.py:488
  145.2 14.9 %collective-permute-start.28 = (bf16[1024,512]{1,0:T(8,128)(2,1)S(1)}, bf16[1024,512]{1,0:T(8,128)(2,1)S(1)}, u32[]{:S(2)}, u32[]{:S(2)}) collective-permute-start(bf16[1024,512]{1,0:T(8,128)(2,1)S(1)} %chain.5.src), channel_id=1, source_target_pairs={{0,1},{1,0},{2,3},{3,2},{4,6},{5,7},{6,4},{7,5},{8,9},{9,8},{10,11... | collective-permute-start | bytes 3145736 | tf_op jit(solution)/shard_map/ppermute | solution.py:488
  151.0 15.7 %collective-permute-start.27 = (bf16[784,512]{1,0:T(8,128)(2,1)S(1)}, bf16[784,512]{1,0:T(8,128)(2,1)S(1)}, u32[]{:S(2)}, u32[]{:S(2)}) collective-permute-start(bf16[784,512]{1,0:T(8,128)(2,1)S(1)} %get-tuple-element.175.src), channel_id=1, source_target_pairs={{0,4},{1,5},{2,6},{3,7},{4,0},{5,1},{6,2},{7,3},{8,12},{9,13},{10,... | collective-permute-start | bytes 2408456 | tf_op jit(solution)/shard_map/ppermute | solution.py:488
  151.1 17.6 %collective-permute-start.26 = (bf16[784,512]{1,0:T(8,128)(2,1)S(1)}, bf16[784,512]{1,0:T(8,128)(2,1)S(1)}, u32[]{:S(2)}, u32[]{:S(2)}) collective-permute-start(bf16[784,512]{1,0:T(8,128)(2,1)S(1)} %get-tuple-element.175.src), channel_id=1, source_target_pairs={{0,1},{1,0},{2,3},{3,2},{4,6},{5,7},{6,4},{7,5},{8,9},{9,8},{10,11... | collective-permute-start | bytes 2408456 | tf_op jit(solution)/shard_map/ppermute | solution.py:488
  160.1 4.6 %collective-permute-start.30 = (bf16[1024,512]{1,0:T(8,128)(2,1)S(1)}, bf16[1024,512]{1,0:T(8,128)(2,1)S(1)}, u32[]{:S(2)}, u32[]{:S(2)}) collective-permute-start(bf16[1024,512]{1,0:T(8,128)(2,1)S(1)} %collective-permute-done.28.src), channel_id=1, source_target_pairs={{0,4},{1,5},{2,6},{3,7},{4,0},{5,1},{6,2},{7,3},{8,12},{9,13},{10,... | collective-permute-start | bytes 3145736 | tf_op jit(solution)/shard_map/ppermute | solution.py:488
  168.7 2.5 %collective-permute-start.31 = (bf16[784,512]{1,0:T(8,128)(2,1)S(1)}, bf16[784,512]{1,0:T(8,128)(2,1)S(1)}, u32[]{:S(2)}, u32[]{:S(2)}) collective-permute-start(bf16[784,512]{1,0:T(8,128)(2,1)S(1)} %collective-permute-done.26.src.rest), channel_id=1, source_target_pairs={{0,4},{1,5},{2,6},{3,7},{4,0},{5,1},{6,2},{7,3},{8,12},{9,13},{10,... | collective-permute-start | bytes 2408456 | tf_op jit(solution)/shard_map/ppermute | solution.py:488

commit v3 on v1

--- a/solution.py
+++ b/solution.py
@@ -693,7 +693,7 @@
         zeros = (0,) * len(dims)
         return pl.BlockSpec(dims, lambda i, *s: zeros)
 
-    def call(kernel, name, grid, ins, outs, scratch, operands, scalars=True, much=False):
+    def call(kernel, name, grid, ins, outs, scratch, operands, scalars=True, much=False, mib=16):
         spec = pltpu.PrefetchScalarGridSpec(
             num_scalar_prefetch=int(scalars),
             grid=(grid,),
@@ -705,7 +705,7 @@
             kernel,
             grid_spec=spec,
             out_shape=[o[0] for o in outs],
-            compiler_params=params(16),
+            compiler_params=params(mib),
             cost_estimate=MUCH if much else LITTLE,
             name=name,
         )(*operands)
@@ -821,6 +821,7 @@
             [],
             (scal, c, z, h, y, dm),
             much=pick == 0,
+            mib=12,
         )
         return order.did(piece)
 
@@ -862,6 +863,7 @@
         [],
         (far(r1), order.after(act), to_rm, down_weight),
         scalars=False,
+        mib=12,
     )
     order.did(output)
     chunk1.step()
@@ -887,6 +889,7 @@
             far(gain1), far(conv_weight), far(gate_weight), far(cand_weight),
         ),
         scalars=False,
+        mib=12,
     )
     order.did(sums)
     small = jnp.concatenate(

time: 174 us -> 174 us (level)
  no operation moved by 1% of the time
where the time goes in v3:
time: 174 us; the launch traced here: 173 us
  Pallas kernels  74.4 us (43%)
  starting transfers between devices  55.3 us (32%)
  waiting for transfers between devices  33.2 us (19%)
  other arithmetic  6.12 us (4%)
  local copies, waits for them, and re-layouts  2.79 us (2%)
    pallas_call x11, Pallas kernels, call(): pl.pallas_call(kernel, grid_spec=spec, out_shape=[o[0] for o in outs], co...  59.2 us
    ppermute x24, starting transfers between devices, flat_permute(): return lax.ppermute(value, ('seq', 'row'), pairs)  39.6 us
    ppermute x24, waiting for transfers between devices, flat_permute(): return lax.ppermute(value, ('seq', 'row'), pairs)  32.4 us
    ppermute x8, starting transfers between devices, passed_along(): lax.ppermute(value, axis, [(source, source + steps) for source in range(l...  15.7 us
    pallas_call x7, Pallas kernels, spread(): pl.pallas_call(functools.partial(spread_kernel, piece=piece, plan=plan, m...  13.2 us
    convert_element_type x10, other arithmetic, added(): return (a.astype(f32) + b.astype(f32)).astype(bf16)  5.98 us
  transfers between devices with their start and end apart: 32, of which 15 were waited for; matrix products, arithmetic and copies ran while one was open for 3% of the time, Pallas kernels for 30%

profile of v3, /device:TPU:0, one launch (start us, length us, event | category | flops | bytes accessed | tf_op | source)
XLA Modules:
  0.0 173.0 jit_solution(10032829462866026868)
XLA Ops:
  0.7 1.0 slice_bitcast_fusion
  1.7 2.4 %collective-permute-start = (bf16[24,512]{1,0:T(8,128)(2,1)S(1)}, bf16[24,512]{1,0:T(8,128)(2,1)S(1)}, u32[]{:S(2)}, u32[]{:S(2)}) collective-permute-start(bf16[24,512]{1,0:T(8,128)(2,1)S(1)} %bitcast.19), channel_id=1, source_target_pairs={{0,4},{4,8},{8,12},{12,16},{16,20},{20,24},{24,28},{1,5},{5,9},{9,... | collective-permute-start | bytes 73736 | tf_op jit(solution)/shard_map/ppermute | solution.py:484
  4.1 3.0 %norm.1.u = bf16[1024,512]{1,0:T(8,128)(2,1)S(1)} custom-call(bf16[8,128,512]{2,1,0:T(8,128)(2,1)} %x.5, bf16[256,256]{1,0:T(8,128)(2,1)} %constant.29.clone.perm.pm, f32[1,512]{1,0:T(1,128)} %bitcast.20), custom_call_target="tpu_custom_call" | custom-call | flops 1024 | bytes 1024 | tf_op jit(solution)/shard_map/norm/pallas_call | solution.py:704
  7.2 6.5 %front.1 = (bf16[1024,512]{1,0:T(8,128)(2,1)S(1)}, bf16[1024,1024]{1,0:T(8,128)(2,1)S(1)}, bf16[1024,1024]{1,0:T(8,128)(2,1)S(1)}, f32[16,1024]{1,0:T(8,128)S(1)}) custom-call(s32[12]{0:T(128)S(1)} %concatenate.17.scal, bf16[1024,512]{1,0:T(8,128)(2,1)S(1)} %norm.1.u, bf16[24,512]{1,0:T(8,128)(2,1)S(1)} %collective-permute-done.edge, f32[1,512]{1,0:T(1,128)} %bitcast.21, ...), custom_call_target="tpu_custom_call" | custom-call | flops 1024 | bytes 1024 | tf_op jit(solution)/shard_map/front/pallas_call | solution.py:704
  13.8 2.8 %collective-permute-start.1 = (f32[16,1024]{1,0:T(8,128)S(1)}, f32[16,1024]{1,0:T(8,128)S(1)}, u32[]{:S(2)}, u32[]{:S(2)}) collective-permute-start(f32[16,1024]{1,0:T(8,128)S(1)} %get-tuple-element.112), channel_id=1, source_target_pairs={{0,4},{1,5},{2,6},{3,7},{4,0},{5,1},{6,2},{7,3},{8,12},{9,13},{10,... | collective-permute-start | bytes 196616 | tf_op jit(solution)/shard_map/ppermute | solution.py:488
  16.6 0.9 collective-permute-done.1.other
  17.5 4.2 %collective-permute-start.4 = (bf16[16,1024]{1,0:T(8,128)(2,1)S(1)}, bf16[16,1024]{1,0:T(8,128)(2,1)S(1)}, u32[]{:S(2)}, u32[]{:S(2)}) collective-permute-start(bf16[16,1024]{1,0:T(8,128)(2,1)S(1)} %pad_maximum_fusion.2), channel_id=1, source_target_pairs={{0,24},{4,28},{1,25},{5,29},{2,26},{6,30},{3,27},{7,31}} | collective-permute-start | bytes 98312 | tf_op jit(solution)/shard_map/ppermute | solution.py:484
  21.8 1.3 collective-permute-start.3
  23.1 2.5 %collective-permute-start.2 = (bf16[16,1024]{1,0:T(8,128)(2,1)S(1)}, bf16[16,1024]{1,0:T(8,128)(2,1)S(1)}, u32[]{:S(2)}, u32[]{:S(2)}) collective-permute-start(bf16[16,1024]{1,0:T(8,128)(2,1)S(1)} %pad_maximum_fusion.2), channel_id=1, source_target_pairs={{0,8},{4,12},{8,16},{12,20},{16,24},{20,28},{1,9},{5,13},{9,17},{1... | collective-permute-start | bytes 98312 | tf_op jit(solution)/shard_map/ppermute | solution.py:484
  25.6 3.5 %da.1 = (bf16[1024,512]{1,0:T(8,128)(2,1)S(1)}, bf16[1024,2048]{1,0:T(8,128)(2,1)S(1)}) custom-call(bf16[8,128,512]{2,1,0:T(8,128)(2,1)S(1)} %copy-done.10, bf16[256,256]{1,0:T(8,128)(2,1)S(1)} %copy-done.8, bf16[2048,512]{1,0:T(8,128)(2,1)S(1)} %copy-done.7), custom_call_target="tpu_custom_call" | custom-call | flops 1024 | bytes 1024 | tf_op jit(solution)/shard_map/da/pallas_call | solution.py:704
  29.2 14.4 %core.1 = (f32[1024,512]{1,0:T(8,128)}, bf16[1024,1024]{1,0:T(8,128)(2,1)S(1)}, bf16[1024,1024]{1,0:T(8,128)(2,1)S(1)}, bf16[1024,512]{1,0:T(8,128)(2,1)S(1)}, b...) custom-call(s32[12]{0:T(128)S(1)} %concatenate.17.scal, ...), custom_call_target="tpu_custom_call" | custom-call | flops 1024 | bytes 1024 | tf_op jit(solution)/shard_map/core/pallas_call | solution.py:704
  43.6 1.2 collective-permute-done.5.fother
  44.8 1.3 collective-permute-start.8
  46.1 1.3 collective-permute-start.7
  47.4 1.3 collective-permute-start.6
  48.7 3.7 %ffn_grad.2 = bf16[2048,512]{1,0:T(8,128)(2,1)S(1)} custom-call(s32[12]{0:T(128)S(1)} %concatenate.17.scal, bf16[1024,2048]{1,0:T(8,128)(2,1)S(1)} %get-tuple-element.136.act, bf16[1024,512]{1,0:T(8,128)(2,1)S(1)} %get-tuple-element.106.gl, bf16[1024,512]{1,0:T(8,128)(2,1)S(1)} %get-tuple-element.121.n2, bf16[1024,2048]{1,0:T(8,128)(2,1)S(1)} %get-tuple-element.127.dp), custom_call_target="tpu_custom_call" | custom-call | flops 1024 | bytes 1024 | tf_op jit(solution)/shard_map/ffn_grad/pallas_call | solution.py:704
  52.7 0.6 collective-permute-done.7.refs_1_
  53.5 3.7 %ffn_grad.3 = bf16[2048,512]{1,0:T(8,128)(2,1)S(1)} custom-call(s32[12]{0:T(128)S(1)} %concatenate.17.scal, bf16[1024,2048]{1,0:T(8,128)(2,1)S(1)} %get-tuple-element.136.act, bf16[1024,512]{1,0:T(8,128)(2,1)S(1)} %get-tuple-element.106.gl, bf16[1024,512]{1,0:T(8,128)(2,1)S(1)} %get-tuple-element.121.n2, bf16[1024,2048]{1,0:T(8,128)(2,1)S(1)} %get-tuple-element.127.dp), custom_call_target="tpu_custom_call" | custom-call | flops 30000001024 | bytes 1024 | tf_op jit(solution)/shard_map/ffn_grad/pallas_call | solution.py:704
  57.2 0.6 add_convert_fusion
  57.8 1.6 collective-permute-start.10
  59.4 3.7 %gates.1 = (bf16[1024,1024]{1,0:T(8,128)(2,1)S(1)}, bf16[1024,1024]{1,0:T(8,128)(2,1)S(1)}, bf16[32,512]{1,0:T(8,128)(2,1)S(1)}, f32[8,1024]{1,0:T(8,128)S(1)}) custom-call(s32[12]{0:T(128)S(1)} %concatenate.17.scal, bf16[1024,1024]{1,0:T(8,128)(2,1)S(1)} %get-tuple-element.116.dh, bf16[1024,1024]{1,0:T(8,128)(2,1)S(1)} %get-tuple-element.110.zl.zl_next.zl_before, ...), custom_call_target="tpu_custom_call" | custom-call | flops 1024 | bytes 1024 | tf_op jit(solution)/shard_map/gates/pallas_call | solution.py:704
  63.1 2.4 %gate_grad.2 = bf16[1536,512]{1,0:T(8,128)(2,1)S(1)} custom-call(s32[12]{0:T(128)S(1)} %concatenate.17.scal, bf16[1024,512]{1,0:T(8,128)(2,1)S(1)} %get-tuple-element.115.c, bf16[1024,1024]{1,0:T(8,128)(2,1)S(1)} %get-tuple-element.143.dkz, bf16[1024,1024]{1,0:T(8,128)(2,1)S(1)} %get-tuple-element.140.dkh, bf16[1024,1024]{1,0:T(8,128)(2,1)S(1)} %get-tuple-element.134.y, ...), custom_call_target="tpu_custom_call" | custom-call | flops 1024 | bytes 1024 | tf_op jit(solution)/shard_map/gate_grad/pallas_call | solution.py:704
  65.6 1.5 collective-permute-start.12
  67.1 5.7 %output.1 = bf16[8,128,512]{2,1,0:T(8,128)(2,1)} custom-call(f32[1024,512]{1,0:T(8,128)} %get-tuple-element.113.r1, bf16[1024,2048]{1,0:T(8,128)(2,1)S(1)} %get-tuple-element.136.act, bf16[256,256]{1,0:T(8,128)(2,1)S(1)} %copy-done.11, bf16[2048,512]{1,0:T(8,128)(2,1)S(1)} %copy-done.7), custom_call_target="tpu_custom_call" | custom-call | flops 1024 | bytes 1024 | tf_op jit(solution)/shard_map/output/pallas_call | solution.py:704
  72.7 1.3 add_convert_fusion.4
  74.0 1.5 collective-permute-start.14
  75.5 2.4 %gate_grad.3 = bf16[1536,512]{1,0:T(8,128)(2,1)S(1)} custom-call(s32[12]{0:T(128)S(1)} %concatenate.17.scal, bf16[1024,512]{1,0:T(8,128)(2,1)S(1)} %get-tuple-element.115.c, bf16[1024,1024]{1,0:T(8,128)(2,1)S(1)} %get-tuple-element.143.dkz, bf16[1024,1024]{1,0:T(8,128)(2,1)S(1)} %get-tuple-element.140.dkh, bf16[1024,1024]{1,0:T(8,128)(2,1)S(1)} %get-tuple-element.134.y, ...), custom_call_target="tpu_custom_call" | custom-call | flops 30000001024 | bytes 1024 | tf_op jit(solution)/shard_map/gate_grad/pallas_call | solution.py:704
  78.0 1.3 add_convert_fusion.2
  79.3 1.4 collective-permute-start.13
  80.8 1.6 copy-done.6
  82.4 10.2 %tail.1 = (bf16[8,128,512]{2,1,0:T(8,128)(2,1)}, f32[40,512]{1,0:T(8,128)S(1)}) custom-call(bf16[8,128,512]{2,1,0:T(8,128)(2,1)} %x.5, f32[1024,512]{1,0:T(8,128)} %get-tuple-element.137.dr1, bf16[1024,1024]{1,0:T(8,128)(2,1)S(1)} %copy-done.4, bf16[1024,1024]{1,0:T(8,128)(2,1)S(1)} %copy-done.6, bf16[256,256]{1,0:T(8,128)(2,1)} %constant.29.clone.perm.pm, ...), custom_call_target="tpu_custom_call" | custom-call | flops 1024 | bytes 1024 | tf_op jit(solution)/shard_map/tail/pallas_call | solution.py:704
  92.6 1.2 add_convert_fusion.8
  93.8 2.2 %collective-permute-start.16 = (bf16[256,512]{1,0:T(8,128)(2,1)S(1)}, bf16[256,512]{1,0:T(8,128)(2,1)S(1)}, u32[]{:S(2)}, u32[]{:S(2)}) collective-permute-start(bf16[256,512]{1,0:T(8,128)(2,1)S(1)} %get-tuple-element.212), channel_id=1, source_target_pairs={{0,8},{1,9},{2,10},{3,11},{4,20},{5,21},{6,22},{7,23},{8,0},{9,1},... | collective-permute-start | bytes 786440 | tf_op jit(solution)/shard_map/ppermute | solution.py:488
  96.0 1.3 add_convert_fusion.6
  97.4 1.2 collective-permute-start.15
  98.6 4.5 %collective-permute-done.16 = bf16[256,512]{1,0:T(8,128)(2,1)S(1)} collective-permute-done((bf16[256,512]{1,0:T(8,128)(2,1)S(1)}, bf16[256,512]{1,0:T(8,128)(2,1)S(1)}, u32[]{:S(2)}, u32[]{:S(2)}) %collective-permute-start.16) | collective-permute-done | bytes 262176 | tf_op jit(solution)/shard_map/ppermute | solution.py:488
  103.1 3.1 %collective-permute-start.18 = (bf16[128,512]{1,0:T(8,128)(2,1)S(1)}, bf16[128,512]{1,0:T(8,128)(2,1)S(1)}, u32[]{:S(2)}, u32[]{:S(2)}) collective-permute-start(bf16[128,512]{1,0:T(8,128)(2,1)S(1)} %add_convert_fusion.14), channel_id=1, source_target_pairs={{0,16},{1,17},{2,18},{3,19},{4,12},{5,13},{6,14},{7,15},{8,24},{9,... | collective-permute-start | bytes 393224 | tf_op jit(solution)/shard_map/ppermute | solution.py:488
  106.3 2.5 %collective-permute-start.17 = (bf16[192,512]{1,0:T(8,128)(2,1)S(1)}, bf16[192,512]{1,0:T(8,128)(2,1)S(1)}, u32[]{:S(2)}, u32[]{:S(2)}) collective-permute-start(bf16[192,512]{1,0:T(8,128)(2,1)S(1)} %get-tuple-element.213), channel_id=1, source_target_pairs={{0,8},{1,9},{2,10},{3,11},{4,20},{5,21},{6,22},{7,23},{8,0},{9,1},... | collective-permute-start | bytes 589832 | tf_op jit(solution)/shard_map/ppermute | solution.py:488
  108.8 0.5 collective-permute-done.18
  109.4 3.5 %collective-permute-start.20 = (bf16[128,512]{1,0:T(8,128)(2,1)S(1)}, bf16[128,512]{1,0:T(8,128)(2,1)S(1)}, u32[]{:S(2)}, u32[]{:S(2)}) collective-permute-start(bf16[128,512]{1,0:T(8,128)(2,1)S(1)} %add_convert_fusion.12.mine), channel_id=1, source_target_pairs={{0,16},{1,17},{2,18},{3,19},{4,12},{5,13},{6,14},{7,15},{8,24},{9,... | collective-permute-start | bytes 393224 | tf_op jit(solution)/shard_map/ppermute | solution.py:488
  112.9 3.7 %collective-permute-done.17 = bf16[192,512]{1,0:T(8,128)(2,1)S(1)} collective-permute-done((bf16[192,512]{1,0:T(8,128)(2,1)S(1)}, bf16[192,512]{1,0:T(8,128)(2,1)S(1)}, u32[]{:S(2)}, u32[]{:S(2)}) %collective-permute-start.17) | collective-permute-done | bytes 196640 | tf_op jit(solution)/shard_map/ppermute | solution.py:488
  116.7 0.5 collective-permute-start.19
  117.2 9.4 %collective-permute-start.23 = (bf16[256,512]{1,0:T(8,128)(2,1)S(1)}, bf16[256,512]{1,0:T(8,128)(2,1)S(1)}, u32[]{:S(2)}, u32[]{:S(2)}) collective-permute-start(bf16[256,512]{1,0:T(8,128)(2,1)S(1)} %chain.3.mine), channel_id=1, source_target_pairs={{0,8},{1,9},{2,10},{3,11},{4,20},{5,21},{6,22},{7,23},{8,0},{9,1},... | collective-permute-start | bytes 786440 | tf_op jit(solution)/shard_map/ppermute | solution.py:488
  126.6 1.0 collective-permute-done.19
  127.7 2.4 %collective-permute-start.21 = (bf16[112,512]{1,0:T(8,128)(2,1)S(1)}, bf16[112,512]{1,0:T(8,128)(2,1)S(1)}, u32[]{:S(2)}, u32[]{:S(2)}) collective-permute-start(bf16[112,512]{1,0:T(8,128)(2,1)S(1)} %pad_maximum_fusion.mine), channel_id=1, source_target_pairs={{0,16},{1,17},{2,18},{3,19},{4,12},{5,13},{6,14},{7,15},{8,24},{9,... | collective-permute-start | bytes 344072 | tf_op jit(solution)/shard_map/ppermute | solution.py:488
  130.1 5.6 %collective-permute-done.21.recv = bf16[112,512]{1,0:T(8,128)(2,1)S(1)} collective-permute-done((bf16[112,512]{1,0:T(8,128)(2,1)S(1)}, bf16[112,512]{1,0:T(8,128)(2,1)S(1)}, u32[]{:S(2)}, u32[]{:S(2)}) %collective-permute-start.21) | collective-permute-done | bytes 114720 | tf_op jit(solution)/shard_map/ppermute | solution.py:488
  135.9 1.4 collective-permute-start.25
  137.2 4.4 %collective-permute-done.22.recv = bf16[208,512]{1,0:T(8,128)(2,1)S(1)} collective-permute-done((bf16[208,512]{1,0:T(8,128)(2,1)S(1)}, bf16[208,512]{1,0:T(8,128)(2,1)S(1)}, u32[]{:S(2)}, u32[]{:S(2)}) %collective-permute-start.22) | collective-permute-done | bytes 213024 | tf_op jit(solution)/shard_map/ppermute | solution.py:488
  141.7 1.3 collective-permute-start.24
  142.9 2.2 %collective-permute-done.25.recv = bf16[512,512]{1,0:T(8,128)(2,1)S(1)} collective-permute-done((bf16[512,512]{1,0:T(8,128)(2,1)S(1)}, bf16[512,512]{1,0:T(8,128)(2,1)S(1)}, u32[]{:S(2)}, u32[]{:S(2)}) %collective-permute-start.25) | collective-permute-done | bytes 524320 | tf_op jit(solution)/shard_map/ppermute | solution.py:488
  145.3 1.4 collective-permute-start.28
  146.7 4.3 %collective-permute-done.24.recv = bf16[400,512]{1,0:T(8,128)(2,1)S(1)} collective-permute-done((bf16[400,512]{1,0:T(8,128)(2,1)S(1)}, bf16[400,512]{1,0:T(8,128)(2,1)S(1)}, u32[]{:S(2)}, u32[]{:S(2)}) %collective-permute-start.24) | collective-permute-done | bytes 409632 | tf_op jit(solution)/shard_map/ppermute | solution.py:488
  151.1 1.4 collective-permute-start.26
  152.5 2.0 %spread_ffn.4 = (f32[2048,512]{1,0:T(8,128)}, f32[512,2048]{1,0:T(8,128)}) custom-call(s32[12]{0:T(128)S(1)} %concatenate.17.scal, bf16[1024,512]{1,0:T(8,128)(2,1)S(1)} %chain.5.src), custom_call_target="tpu_custom_call" | custom-call | flops 10000000000 | bytes 1024 | tf_op jit(solution)/shard_map/spread_ffn/pallas_call | solution.py:440
  154.5 2.0 %spread_ffn.5 = (f32[2048,512]{1,0:T(8,128)}, f32[512,2048]{1,0:T(8,128)}) custom-call(s32[12]{0:T(128)S(1)} %concatenate.17.scal, bf16[1024,512]{1,0:T(8,128)(2,1)S(1)} %collective-permute-done.29.src, f32[2048,512]{1,0:T(8,128)} %get-tuple-element.167.refs_0_, f32[512,2048]{1,0:T(8,128)} %get-tuple-element.169.refs_1_), custom_call_target="tpu_custom_call", output_to_operand_aliasing={{0}: (2, {}), {1}: (3, {})} | custom-call | flops 10000000000 | bytes 1024 | tf_op jit(solution)/shard_map/spread_ffn/pallas_call | solution.py:440
  156.5 3.6 %collective-permute-done.28.src = bf16[1024,512]{1,0:T(8,128)(2,1)S(1)} collective-permute-done((bf16[1024,512]{1,0:T(8,128)(2,1)S(1)}, bf16[1024,512]{1,0:T(8,128)(2,1)S(1)}, u32[]{:S(2)}, u32[]{:S(2)}) %collective-permute-start.28) | collective-permute-done | bytes 1048608 | tf_op jit(solution)/shard_map/ppermute | solution.py:488
  160.1 0.9 collective-permute-start.30
  161.0 2.0 %spread_ffn.6 = (f32[2048,512]{1,0:T(8,128)}, f32[512,2048]{1,0:T(8,128)}) custom-call(s32[12]{0:T(128)S(1)} %concatenate.17.scal, bf16[1024,512]{1,0:T(8,128)(2,1)S(1)} %collective-permute-done.28.src, f32[2048,512]{1,0:T(8,128)} %get-tuple-element.170.refs_0_, f32[512,2048]{1,0:T(8,128)} %get-tuple-element.173.refs_1_), custom_call_target="tpu_custom_call", output_to_operand_aliasing={{0}: (2, {}), {1}: (3, {})} | custom-call | flops 10000000000 | bytes 1024 | tf_op jit(solution)/shard_map/spread_ffn/pallas_call | solution.py:440
  163.0 1.7 %spread_gates.3 = (f32[512,1024]{1,0:T(8,128)}, f32[512,1024]{1,0:T(8,128)}, f32[1024,512]{1,0:T(8,128)}) custom-call(s32[12]{0:T(128)S(1)} %concatenate.17.scal, bf16[784,512]{1,0:T(8,128)(2,1)S(1)} %get-tuple-element.175.src), custom_call_target="tpu_custom_call" | custom-call | flops 10000000000 | bytes 1024 | tf_op jit(solution)/shard_map/spread_gates/pallas_call | solution.py:440
  164.8 2.0 %spread_ffn.7 = (f32[2048,512]{1,0:T(8,128)}, f32[512,2048]{1,0:T(8,128)}) custom-call(s32[12]{0:T(128)S(1)} %concatenate.17.scal, bf16[1024,512]{1,0:T(8,128)(2,1)S(1)} %collective-permute-done.30.src, f32[2048,512]{1,0:T(8,128)} %get-tuple-element.174.refs_0_, f32[512,2048]{1,0:T(8,128)} %get-tuple-element.178.refs_1_), custom_call_target="tpu_custom_call", output_to_operand_aliasing={{0}: (2, {}), {1}: (3, {})} | custom-call | flops 10000000000 | bytes 1024 | tf_op jit(solution)/shard_map/spread_ffn/pallas_call | solution.py:440
  166.7 1.7 %spread_gates.4 = (f32[512,1024]{1,0:T(8,128)}, f32[512,1024]{1,0:T(8,128)}, f32[1024,512]{1,0:T(8,128)}) custom-call(s32[12]{0:T(128)S(1)} %concatenate.17.scal, bf16[784,512]{1,0:T(8,128)(2,1)S(1)} %collective-permute-done.27.src.theirs, f32[512,1024]{1,0:T(8,128)} %get-tuple-element.176.refs_0_, ...), custom_call_target="tpu_custom_call", output_to_operand_aliasing={{0}: (2, {}), {1}: (3, {}), {2}: (4, {})} | custom-call | flops 10000000000 | bytes 1024 | tf_op jit(solution)/shard_map/spread_gates/pallas_call | solution.py:440
  168.7 0.6 collective-permute-start.31
  169.3 1.7 %spread_gates.5 = (f32[512,1024]{1,0:T(8,128)}, f32[512,1024]{1,0:T(8,128)}, f32[1024,512]{1,0:T(8,128)}) custom-call(s32[12]{0:T(128)S(1)} %concatenate.17.scal, bf16[784,512]{1,0:T(8,128)(2,1)S(1)} %collective-permute-done.26.src.rest, f32[512,1024]{1,0:T(8,128)} %get-tuple-element.183.refs_0_, ...), custom_call_target="tpu_custom_call", output_to_operand_aliasing={{0}: (2, {}), {1}: (3, {}), {2}: (4, {})} | custom-call | flops 10000000000 | bytes 1024 | tf_op jit(solution)/shard_map/spread_gates/pallas_call | solution.py:440
  171.3 1.8 %spread_last.1 = (f32[512,1024]{1,0:T(8,128)}, f32[512,1024]{1,0:T(8,128)}, f32[1024,512]{1,0:T(8,128)}, f32[1,512]{1,0:T(1,128)}, f32[4,512]{1,0:T(4,128)}, /*index=5*/f32[1,512]{1,0:T(1,128)}, f32[1,1024]{1,0:T(1,128)}) custom-call(s32[12]{0:T(128)S(1)} %concatenate.17.scal, ...), custom_call_target="tpu_custom_call", output_to_operand_aliasing={{0}: (5, {}), {1}: (6, {}), {2}: (7, {})} | custom-call | flops 10000000000 | bytes 1024 | tf_op jit(solution)/shard_map/spread_last/pallas_call | solution.py:418
  (81 shorter events, 2.1 us)
Async XLA Ops:
  0.6 6.5 %copy-start.14 = (s32[8]{0:T(128)S(1)}, s32[8]{0:T(128)}, u32[]{:S(2)}) copy-start(s32[8]{0:T(128)} %param.15) | copy-start | bytes 100
  0.7 6.6 %copy-start.2 = (bf16[512,1024]{1,0:T(8,128)(2,1)S(1)}, bf16[512,1024]{1,0:T(8,128)(2,1)}, u32[]{:S(2)}) copy-start(bf16[512,1024]{1,0:T(8,128)(2,1)} %wc.3) | copy-start | bytes 3145732
  0.7 6.6 %copy-start.1 = (bf16[512,1024]{1,0:T(8,128)(2,1)S(1)}, bf16[512,1024]{1,0:T(8,128)(2,1)}, u32[]{:S(2)}) copy-start(bf16[512,1024]{1,0:T(8,128)(2,1)} %wg.3) | copy-start | bytes 3145732
  1.7 5.5 %collective-permute-start = (bf16[24,512]{1,0:T(8,128)(2,1)S(1)}, bf16[24,512]{1,0:T(8,128)(2,1)S(1)}, u32[]{:S(2)}, u32[]{:S(2)}) collective-permute-start(bf16[24,512]{1,0:T(8,128)(2,1)S(1)} %bitcast.19), channel_id=1, source_target_pairs={{0,4},{4,8},{8,12},{12,16},{16,20},{20,24},{24,28},{1,5},{5,9},{9,... | collective-permute-start | bytes 73736 | tf_op jit(solution)/shard_map/ppermute | solution.py:484
  7.1 18.5 %copy-start.8 = (bf16[256,256]{1,0:T(8,128)(2,1)S(1)}, bf16[256,256]{1,0:T(8,128)(2,1)}, u32[]{:S(2)}) copy-start(bf16[256,256]{1,0:T(8,128)(2,1)} %constant.29.clone.perm.pm) | copy-start | bytes 393220
  7.2 18.4 %copy-start.7 = (bf16[2048,512]{1,0:T(8,128)(2,1)S(1)}, bf16[2048,512]{1,0:T(8,128)(2,1)}, u32[]{:S(2)}) copy-start(bf16[2048,512]{1,0:T(8,128)(2,1)} %wd.3) | copy-start | bytes 6291460
  7.2 18.4 %copy-start.10 = (bf16[8,128,512]{2,1,0:T(8,128)(2,1)S(1)}, bf16[8,128,512]{2,1,0:T(8,128)(2,1)}, u32[]{:S(2)}) copy-start(bf16[8,128,512]{2,1,0:T(8,128)(2,1)} %g.1) | copy-start | bytes 3145732
  13.8 15.4 %copy-start = (bf16[8,128,512]{2,1,0:T(8,128)(2,1)S(1)}, bf16[8,128,512]{2,1,0:T(8,128)(2,1)}, u32[]{:S(2)}) copy-start(bf16[8,128,512]{2,1,0:T(8,128)(2,1)} %x.5) | copy-start | bytes 3145732
  13.8 15.4 %copy-start.9 = (bf16[512,2048]{1,0:T(8,128)(2,1)S(1)}, bf16[512,2048]{1,0:T(8,128)(2,1)}, u32[]{:S(2)}) copy-start(bf16[512,2048]{1,0:T(8,128)(2,1)} %refs_5_.1) | copy-start | bytes 6291460
  13.8 15.4 %copy-start.12 = (f32[512]{0:T(512)S(1)}, f32[512]{0:T(512)}, u32[]{:S(2)}) copy-start(f32[512]{0:T(512)} %param.22) | copy-start | bytes 6148
  13.8 3.7 %collective-permute-start.1 = (f32[16,1024]{1,0:T(8,128)S(1)}, f32[16,1024]{1,0:T(8,128)S(1)}, u32[]{:S(2)}, u32[]{:S(2)}) collective-permute-start(f32[16,1024]{1,0:T(8,128)S(1)} %get-tuple-element.112), channel_id=1, source_target_pairs={{0,4},{1,5},{2,6},{3,7},{4,0},{5,1},{6,2},{7,3},{8,12},{9,13},{10,... | collective-permute-start | bytes 196616 | tf_op jit(solution)/shard_map/ppermute | solution.py:488
  17.5 11.6 %collective-permute-start.4 = (bf16[16,1024]{1,0:T(8,128)(2,1)S(1)}, bf16[16,1024]{1,0:T(8,128)(2,1)S(1)}, u32[]{:S(2)}, u32[]{:S(2)}) collective-permute-start(bf16[16,1024]{1,0:T(8,128)(2,1)S(1)} %pad_maximum_fusion.2), channel_id=1, source_target_pairs={{0,24},{4,28},{1,25},{5,29},{2,26},{6,30},{3,27},{7,31}} | collective-permute-start | bytes 98312 | tf_op jit(solution)/shard_map/ppermute | solution.py:484
  21.8 7.4 %collective-permute-start.3 = (bf16[16,1024]{1,0:T(8,128)(2,1)S(1)}, bf16[16,1024]{1,0:T(8,128)(2,1)S(1)}, u32[]{:S(2)}, u32[]{:S(2)}) collective-permute-start(bf16[16,1024]{1,0:T(8,128)(2,1)S(1)} %pad_maximum_fusion.2), channel_id=1, source_target_pairs={{0,16},{4,20},{8,24},{12,28},{1,17},{5,21},{9,25},{13,29},{2,18},{... | collective-permute-start | bytes 98312 | tf_op jit(solution)/shard_map/ppermute | solution.py:484
  23.1 6.1 %collective-permute-start.2 = (bf16[16,1024]{1,0:T(8,128)(2,1)S(1)}, bf16[16,1024]{1,0:T(8,128)(2,1)S(1)}, u32[]{:S(2)}, u32[]{:S(2)}) collective-permute-start(bf16[16,1024]{1,0:T(8,128)(2,1)S(1)} %pad_maximum_fusion.2), channel_id=1, source_target_pairs={{0,8},{4,12},{8,16},{12,20},{16,24},{20,28},{1,9},{5,13},{9,17},{1... | collective-permute-start | bytes 98312 | tf_op jit(solution)/shard_map/ppermute | solution.py:484
  43.6 1.2 collective-permute-start.5
  44.8 7.8 %collective-permute-start.8 = (bf16[16,1024]{1,0:T(8,128)(2,1)S(1)}, bf16[16,1024]{1,0:T(8,128)(2,1)S(1)}, u32[]{:S(2)}, u32[]{:S(2)}) collective-permute-start(bf16[16,1024]{1,0:T(8,128)(2,1)S(1)} %pad_maximum_fusion.1), channel_id=1, source_target_pairs={{24,0},{28,4},{25,1},{29,5},{26,2},{30,6},{27,3},{31,7}} | collective-permute-start | bytes 98312 | tf_op jit(solution)/shard_map/ppermute | solution.py:484
  46.1 7.1 %collective-permute-start.7 = (bf16[16,1024]{1,0:T(8,128)(2,1)S(1)}, bf16[16,1024]{1,0:T(8,128)(2,1)S(1)}, u32[]{:S(2)}, u32[]{:S(2)}) collective-permute-start(bf16[16,1024]{1,0:T(8,128)(2,1)S(1)} %pad_maximum_fusion.1), channel_id=1, source_target_pairs={{16,0},{20,4},{24,8},{28,12},{17,1},{21,5},{25,9},{29,13},{18,2},{... | collective-permute-start | bytes 98312 | tf_op jit(solution)/shard_map/ppermute | solution.py:484
  47.4 6.1 %collective-permute-start.6 = (bf16[16,1024]{1,0:T(8,128)(2,1)S(1)}, bf16[16,1024]{1,0:T(8,128)(2,1)S(1)}, u32[]{:S(2)}, u32[]{:S(2)}) collective-permute-start(bf16[16,1024]{1,0:T(8,128)(2,1)S(1)} %pad_maximum_fusion.1), channel_id=1, source_target_pairs={{8,0},{12,4},{16,8},{20,12},{24,16},{28,20},{9,1},{13,5},{17,9},{2... | collective-permute-start | bytes 98312 | tf_op jit(solution)/shard_map/ppermute | solution.py:484
  52.4 4.7 %collective-permute-start.9 = (bf16[2048,512]{1,0:T(8,128)(2,1)S(1)}, bf16[2048,512]{1,0:T(8,128)(2,1)S(1)}, u32[]{:S(2)}, u32[]{:S(2)}) collective-permute-start(bf16[2048,512]{1,0:T(8,128)(2,1)S(1)} %ffn_grad.2), channel_id=1, source_target_pairs={{0,4},{1,5},{2,6},{3,7},{4,0},{5,1},{6,2},{7,3},{8,12},{9,13},{10,... | collective-permute-start | bytes 6291464 | tf_op jit(solution)/shard_map/ppermute | solution.py:488
  57.8 14.9 %collective-permute-start.10 = (bf16[1024,512]{1,0:T(8,128)(2,1)S(1)}, bf16[1024,512]{1,0:T(8,128)(2,1)S(1)}, u32[]{:S(2)}, u32[]{:S(2)}) collective-permute-start(bf16[1024,512]{1,0:T(8,128)(2,1)S(1)} %get-tuple-element.204.refs_5_), channel_id=1, source_target_pairs={{0,1},{1,0},{2,3},{3,2},{4,6},{5,7},{6,4},{7,5},{8,9},{9,8},{10,11... | collective-permute-start | bytes 3145736 | tf_op jit(solution)/shard_map/ppermute | solution.py:488
  63.1 12.5 %copy-start.3 = (bf16[1024,1024]{1,0:T(8,128)(2,1)}, bf16[1024,1024]{1,0:T(8,128)(2,1)S(1)}, u32[]{:S(2)}) copy-start(bf16[1024,1024]{1,0:T(8,128)(2,1)S(1)} %get-tuple-element.143.dkz) | copy-start | bytes 6291460
  63.1 12.5 %copy-start.5 = (bf16[1024,1024]{1,0:T(8,128)(2,1)}, bf16[1024,1024]{1,0:T(8,128)(2,1)S(1)}, u32[]{:S(2)}) copy-start(bf16[1024,1024]{1,0:T(8,128)(2,1)S(1)} %get-tuple-element.140.dkh) | copy-start | bytes 6291460
  63.1 4.0 %copy-start.11 = (bf16[256,256]{1,0:T(8,128)(2,1)S(1)}, bf16[256,256]{1,0:T(8,128)(2,1)}, u32[]{:S(2)}) copy-start(bf16[256,256]{1,0:T(8,128)(2,1)} %constant.30.clone.perm.back_pm) | copy-start | bytes 393220
  65.5 12.5 %collective-permute-start.11 = (bf16[1536,512]{1,0:T(8,128)(2,1)S(1)}, bf16[1536,512]{1,0:T(8,128)(2,1)S(1)}, u32[]{:S(2)}, u32[]{:S(2)}) collective-permute-start(bf16[1536,512]{1,0:T(8,128)(2,1)S(1)} %gate_grad.2), channel_id=1, source_target_pairs={{0,4},{1,5},{2,6},{3,7},{4,0},{5,1},{6,2},{7,3},{8,12},{9,13},{10,... | collective-permute-start | bytes 4718600 | tf_op jit(solution)/shard_map/ppermute | solution.py:488
  65.6 12.4 %collective-permute-start.12 = (bf16[24,512]{1,0:T(8,128)(2,1)S(1)}, bf16[24,512]{1,0:T(8,128)(2,1)S(1)}, u32[]{:S(2)}, u32[]{:S(2)}) collective-permute-start(bf16[24,512]{1,0:T(8,128)(2,1)S(1)} %slice.134), channel_id=1, source_target_pairs={{4,0},{8,4},{12,8},{16,12},{20,16},{24,20},{28,24},{5,1},{9,5},{13... | collective-permute-start | bytes 73736 | tf_op jit(solution)/shard_map/ppermute | solution.py:484
  74.0 18.6 %collective-permute-start.14 = (bf16[512,512]{1,0:T(8,128)(2,1)}, bf16[512,512]{1,0:T(8,128)(2,1)}, u32[]{:S(2)}, u32[]{:S(2)}) collective-permute-start(bf16[512,512]{1,0:T(8,128)(2,1)} %get-tuple-element.208), channel_id=1, source_target_pairs={{0,2},{1,3},{2,0},{3,1},{4,5},{5,4},{6,7},{7,6},{8,10},{9,11},{10,... | collective-permute-start | bytes 1572872 | tf_op jit(solution)/shard_map/ppermute | solution.py:488
  78.0 2.8 %copy-start.4 = (bf16[1024,1024]{1,0:T(8,128)(2,1)S(1)}, bf16[1024,1024]{1,0:T(8,128)(2,1)}, u32[]{:S(2)}) copy-start(bf16[1024,1024]{1,0:T(8,128)(2,1)} %copy-done.3) | copy-start | bytes 6291460
  79.3 16.7 %collective-permute-start.13 = (bf16[768,512]{1,0:T(8,128)(2,1)}, bf16[768,512]{1,0:T(8,128)(2,1)}, u32[]{:S(2)}, u32[]{:S(2)}) collective-permute-start(bf16[768,512]{1,0:T(8,128)(2,1)} %get-tuple-element.206), channel_id=1, source_target_pairs={{0,1},{1,0},{2,3},{3,2},{4,6},{5,7},{6,4},{7,5},{8,9},{9,8},{10,11... | collective-permute-start | bytes 2359304 | tf_op jit(solution)/shard_map/ppermute | solution.py:488
  80.8 1.6 copy-start.6
  82.4 10.2 %copy-start.13 = (bf16[512,512]{1,0:T(8,128)(2,1)S(1)}, bf16[512,512]{1,0:T(8,128)(2,1)}, u32[]{:S(2)}) copy-start(bf16[512,512]{1,0:T(8,128)(2,1)} %get-tuple-element.207) | copy-start | bytes 1572868
  93.8 9.2 %collective-permute-start.16 = (bf16[256,512]{1,0:T(8,128)(2,1)S(1)}, bf16[256,512]{1,0:T(8,128)(2,1)S(1)}, u32[]{:S(2)}, u32[]{:S(2)}) collective-permute-start(bf16[256,512]{1,0:T(8,128)(2,1)S(1)} %get-tuple-element.212), channel_id=1, source_target_pairs={{0,8},{1,9},{2,10},{3,11},{4,20},{5,21},{6,22},{7,23},{8,0},{9,1},... | collective-permute-start | bytes 786440 | tf_op jit(solution)/shard_map/ppermute | solution.py:488
  97.4 8.8 %collective-permute-start.15 = (bf16[384,512]{1,0:T(8,128)(2,1)S(1)}, bf16[384,512]{1,0:T(8,128)(2,1)S(1)}, u32[]{:S(2)}, u32[]{:S(2)}) collective-permute-start(bf16[384,512]{1,0:T(8,128)(2,1)S(1)} %get-tuple-element.209), channel_id=1, source_target_pairs={{0,2},{1,3},{2,0},{3,1},{4,5},{5,4},{6,7},{7,6},{8,10},{9,11},{10,... | collective-permute-start | bytes 1179656 | tf_op jit(solution)/shard_map/ppermute | solution.py:488
  103.1 6.3 %collective-permute-start.18 = (bf16[128,512]{1,0:T(8,128)(2,1)S(1)}, bf16[128,512]{1,0:T(8,128)(2,1)S(1)}, u32[]{:S(2)}, u32[]{:S(2)}) collective-permute-start(bf16[128,512]{1,0:T(8,128)(2,1)S(1)} %add_convert_fusion.14), channel_id=1, source_target_pairs={{0,16},{1,17},{2,18},{3,19},{4,12},{5,13},{6,14},{7,15},{8,24},{9,... | collective-permute-start | bytes 393224 | tf_op jit(solution)/shard_map/ppermute | solution.py:488
  106.3 10.3 %collective-permute-start.17 = (bf16[192,512]{1,0:T(8,128)(2,1)S(1)}, bf16[192,512]{1,0:T(8,128)(2,1)S(1)}, u32[]{:S(2)}, u32[]{:S(2)}) collective-permute-start(bf16[192,512]{1,0:T(8,128)(2,1)S(1)} %get-tuple-element.213), channel_id=1, source_target_pairs={{0,8},{1,9},{2,10},{3,11},{4,20},{5,21},{6,22},{7,23},{8,0},{9,1},... | collective-permute-start | bytes 589832 | tf_op jit(solution)/shard_map/ppermute | solution.py:488
  109.4 7.8 %collective-permute-start.20 = (bf16[128,512]{1,0:T(8,128)(2,1)S(1)}, bf16[128,512]{1,0:T(8,128)(2,1)S(1)}, u32[]{:S(2)}, u32[]{:S(2)}) collective-permute-start(bf16[128,512]{1,0:T(8,128)(2,1)S(1)} %add_convert_fusion.12.mine), channel_id=1, source_target_pairs={{0,16},{1,17},{2,18},{3,19},{4,12},{5,13},{6,14},{7,15},{8,24},{9,... | collective-permute-start | bytes 393224 | tf_op jit(solution)/shard_map/ppermute | solution.py:488
  116.7 10.9 %collective-permute-start.19 = (bf16[96,512]{1,0:T(8,128)(2,1)S(1)}, bf16[96,512]{1,0:T(8,128)(2,1)S(1)}, u32[]{:S(2)}, u32[]{:S(2)}) collective-permute-start(bf16[96,512]{1,0:T(8,128)(2,1)S(1)} %add_convert_fusion.16), channel_id=1, source_target_pairs={{0,16},{1,17},{2,18},{3,19},{4,12},{5,13},{6,14},{7,15},{8,24},{9,... | collective-permute-start | bytes 294920 | tf_op jit(solution)/shard_map/ppermute | solution.py:488
  117.2 18.6 %collective-permute-start.23 = (bf16[256,512]{1,0:T(8,128)(2,1)S(1)}, bf16[256,512]{1,0:T(8,128)(2,1)S(1)}, u32[]{:S(2)}, u32[]{:S(2)}) collective-permute-start(bf16[256,512]{1,0:T(8,128)(2,1)S(1)} %chain.3.mine), channel_id=1, source_target_pairs={{0,8},{1,9},{2,10},{3,11},{4,20},{5,21},{6,22},{7,23},{8,0},{9,1},... | collective-permute-start | bytes 786440 | tf_op jit(solution)/shard_map/ppermute | solution.py:488
  127.7 8.0 %collective-permute-start.21 = (bf16[112,512]{1,0:T(8,128)(2,1)S(1)}, bf16[112,512]{1,0:T(8,128)(2,1)S(1)}, u32[]{:S(2)}, u32[]{:S(2)}) collective-permute-start(bf16[112,512]{1,0:T(8,128)(2,1)S(1)} %pad_maximum_fusion.mine), channel_id=1, source_target_pairs={{0,16},{1,17},{2,18},{3,19},{4,12},{5,13},{6,14},{7,15},{8,24},{9,... | collective-permute-start | bytes 344072 | tf_op jit(solution)/shard_map/ppermute | solution.py:488
  135.7 5.9 %collective-permute-start.22 = (bf16[208,512]{1,0:T(8,128)(2,1)S(1)}, bf16[208,512]{1,0:T(8,128)(2,1)S(1)}, u32[]{:S(2)}, u32[]{:S(2)}) collective-permute-start(bf16[208,512]{1,0:T(8,128)(2,1)S(1)} %get-tuple-element.157.mine), channel_id=1, source_target_pairs={{0,8},{1,9},{2,10},{3,11},{4,20},{5,21},{6,22},{7,23},{8,0},{9,1},... | collective-permute-start | bytes 638984 | tf_op jit(solution)/shard_map/ppermute | solution.py:488
  135.9 9.2 %collective-permute-start.25 = (bf16[512,512]{1,0:T(8,128)(2,1)S(1)}, bf16[512,512]{1,0:T(8,128)(2,1)S(1)}, u32[]{:S(2)}, u32[]{:S(2)}) collective-permute-start(bf16[512,512]{1,0:T(8,128)(2,1)S(1)} %chain.4.mine), channel_id=1, source_target_pairs={{0,2},{1,3},{2,0},{3,1},{4,5},{5,4},{6,7},{7,6},{8,10},{9,11},{10,... | collective-permute-start | bytes 1572872 | tf_op jit(solution)/shard_map/ppermute | solution.py:488
  141.7 9.3 %collective-permute-start.24 = (bf16[400,512]{1,0:T(8,128)(2,1)S(1)}, bf16[400,512]{1,0:T(8,128)(2,1)S(1)}, u32[]{:S(2)}, u32[]{:S(2)}) collective-permute-start(bf16[400,512]{1,0:T(8,128)(2,1)S(1)} %get-tuple-element.161.mine), channel_id=1, source_target_pairs={{0,2},{1,3},{2,0},{3,1},{4,5},{5,4},{6,7},{7,6},{8,10},{9,11},{10,... | collective-permute-start | bytes 1228808 | tf_op jit(solution)/shard_map/ppermute | solution.py:488
  145.2 9.3 %collective-permute-start.29 = (bf16[1024,512]{1,0:T(8,128)(2,1)S(1)}, bf16[1024,512]{1,0:T(8,128)(2,1)S(1)}, u32[]{:S(2)}, u32[]{:S(2)}) collective-permute-start(bf16[1024,512]{1,0:T(8,128)(2,1)S(1)} %chain.5.src), channel_id=1, source_target_pairs={{0,4},{1,5},{2,6},{3,7},{4,0},{5,1},{6,2},{7,3},{8,12},{9,13},{10,... | collective-permute-start | bytes 3145736 | tf_op jit(solution)/shard_map/ppermute | solution.py:488
  145.3 14.9 %collective-permute-start.28 = (bf16[1024,512]{1,0:T(8,128)(2,1)S(1)}, bf16[1024,512]{1,0:T(8,128)(2,1)S(1)}, u32[]{:S(2)}, u32[]{:S(2)}) collective-permute-start(bf16[1024,512]{1,0:T(8,128)(2,1)S(1)} %chain.5.src), channel_id=1, source_target_pairs={{0,1},{1,0},{2,3},{3,2},{4,6},{5,7},{6,4},{7,5},{8,9},{9,8},{10,11... | collective-permute-start | bytes 3145736 | tf_op jit(solution)/shard_map/ppermute | solution.py:488
  151.0 15.7 %collective-permute-start.27 = (bf16[784,512]{1,0:T(8,128)(2,1)S(1)}, bf16[784,512]{1,0:T(8,128)(2,1)S(1)}, u32[]{:S(2)}, u32[]{:S(2)}) collective-permute-start(bf16[784,512]{1,0:T(8,128)(2,1)S(1)} %get-tuple-element.175.src), channel_id=1, source_target_pairs={{0,4},{1,5},{2,6},{3,7},{4,0},{5,1},{6,2},{7,3},{8,12},{9,13},{10,... | collective-permute-start | bytes 2408456 | tf_op jit(solution)/shard_map/ppermute | solution.py:488
  151.1 17.6 %collective-permute-start.26 = (bf16[784,512]{1,0:T(8,128)(2,1)S(1)}, bf16[784,512]{1,0:T(8,128)(2,1)S(1)}, u32[]{:S(2)}, u32[]{:S(2)}) collective-permute-start(bf16[784,512]{1,0:T(8,128)(2,1)S(1)} %get-tuple-element.175.src), channel_id=1, source_target_pairs={{0,1},{1,0},{2,3},{3,2},{4,6},{5,7},{6,4},{7,5},{8,9},{9,8},{10,11... | collective-permute-start | bytes 2408456 | tf_op jit(solution)/shard_map/ppermute | solution.py:488
  160.1 4.6 %collective-permute-start.30 = (bf16[1024,512]{1,0:T(8,128)(2,1)S(1)}, bf16[1024,512]{1,0:T(8,128)(2,1)S(1)}, u32[]{:S(2)}, u32[]{:S(2)}) collective-permute-start(bf16[1024,512]{1,0:T(8,128)(2,1)S(1)} %collective-permute-done.28.src), channel_id=1, source_target_pairs={{0,4},{1,5},{2,6},{3,7},{4,0},{5,1},{6,2},{7,3},{8,12},{9,13},{10,... | collective-permute-start | bytes 3145736 | tf_op jit(solution)/shard_map/ppermute | solution.py:488
  168.7 2.5 %collective-permute-start.31 = (bf16[784,512]{1,0:T(8,128)(2,1)S(1)}, bf16[784,512]{1,0:T(8,128)(2,1)S(1)}, u32[]{:S(2)}, u32[]{:S(2)}) collective-permute-start(bf16[784,512]{1,0:T(8,128)(2,1)S(1)} %collective-permute-done.26.src.rest), channel_id=1, source_target_pairs={{0,4},{1,5},{2,6},{3,7},{4,0},{5,1},{6,2},{7,3},{8,12},{9,13},{10,... | collective-permute-start | bytes 2408456 | tf_op jit(solution)/shard_map/ppermute | solution.py:488

commit v4 on v3

--- a/solution.py
+++ b/solution.py
@@ -885,7 +885,7 @@
             pltpu.VMEM((margin * R + tokens, width), f32),
         ],
         (
-            far(inputs), far(dr1), order.after(dkz), dkh, far(to_pm), far(to_rm), edge, after,
+            far(inputs), far(dr1), far(order.after(dkz)), far(dkh), far(to_pm), far(to_rm), edge, after,
             far(gain1), far(conv_weight), far(gate_weight), far(cand_weight),
         ),
         scalars=False,

time: 174 us -> 173 us (level)
  transfers between devices with their start and end apart: 32 -> 32, of which waited for: 15 -> 15; matrix products, arithmetic and copies ran while one was open for 3% -> 2% of each run, Pallas kernels for 30% -> 30%
where the time goes in v4:
time: 173 us; the launch traced here: 172 us
  Pallas kernels  75.2 us (43%)
  starting transfers between devices  55.1 us (32%)
  waiting for transfers between devices  34.6 us (20%)
  other arithmetic  4.8 us (3%)
    pallas_call x11, Pallas kernels, call(): pl.pallas_call(kernel, grid_spec=spec, out_shape=[o[0] for o in outs], co...  60 us
    ppermute x24, starting transfers between devices, flat_permute(): return lax.ppermute(value, ('seq', 'row'), pairs)  39.4 us
    ppermute x24, waiting for transfers between devices, flat_permute(): return lax.ppermute(value, ('seq', 'row'), pairs)  33.7 us
    ppermute x8, starting transfers between devices, passed_along(): lax.ppermute(value, axis, [(source, source + steps) for source in range(l...  15.7 us
    pallas_call x7, Pallas kernels, spread(): pl.pallas_call(functools.partial(spread_kernel, piece=piece, plan=plan, m...  13.2 us
    convert_element_type x10, other arithmetic, added(): return (a.astype(f32) + b.astype(f32)).astype(bf16)  4.66 us
  transfers between devices with their start and end apart: 32, of which 15 were waited for; matrix products, arithmetic and copies ran while one was open for 2% of the time, Pallas kernels for 30%

profile of v4, /device:TPU:0, one launch (start us, length us, event | category | flops | bytes accessed | tf_op | source)
XLA Modules:
  0.0 172.0 jit_solution(9229356670650780976)
XLA Ops:
  0.7 1.0 slice_bitcast_fusion
  1.7 2.4 %collective-permute-start = (bf16[24,512]{1,0:T(8,128)(2,1)S(1)}, bf16[24,512]{1,0:T(8,128)(2,1)S(1)}, u32[]{:S(2)}, u32[]{:S(2)}) collective-permute-start(bf16[24,512]{1,0:T(8,128)(2,1)S(1)} %bitcast.19), channel_id=1, source_target_pairs={{0,4},{4,8},{8,12},{12,16},{16,20},{20,24},{24,28},{1,5},{5,9},{9,... | collective-permute-start | bytes 73736 | tf_op jit(solution)/shard_map/ppermute | solution.py:484
  4.1 3.0 %norm.1.u = bf16[1024,512]{1,0:T(8,128)(2,1)S(1)} custom-call(bf16[8,128,512]{2,1,0:T(8,128)(2,1)} %x.5, bf16[256,256]{1,0:T(8,128)(2,1)} %constant.29.clone.perm.pm, f32[1,512]{1,0:T(1,128)} %bitcast.20), custom_call_target="tpu_custom_call" | custom-call | flops 1024 | bytes 1024 | tf_op jit(solution)/shard_map/norm/pallas_call | solution.py:704
  7.2 6.5 %front.1 = (bf16[1024,512]{1,0:T(8,128)(2,1)S(1)}, bf16[1024,1024]{1,0:T(8,128)(2,1)S(1)}, bf16[1024,1024]{1,0:T(8,128)(2,1)S(1)}, f32[16,1024]{1,0:T(8,128)S(1)}) custom-call(s32[12]{0:T(128)S(1)} %concatenate.17.scal, bf16[1024,512]{1,0:T(8,128)(2,1)S(1)} %norm.1.u, bf16[24,512]{1,0:T(8,128)(2,1)S(1)} %collective-permute-done.edge, f32[1,512]{1,0:T(1,128)} %bitcast.21, ...), custom_call_target="tpu_custom_call" | custom-call | flops 1024 | bytes 1024 | tf_op jit(solution)/shard_map/front/pallas_call | solution.py:704
  13.8 2.8 %collective-permute-start.1 = (f32[16,1024]{1,0:T(8,128)S(1)}, f32[16,1024]{1,0:T(8,128)S(1)}, u32[]{:S(2)}, u32[]{:S(2)}) collective-permute-start(f32[16,1024]{1,0:T(8,128)S(1)} %get-tuple-element.112), channel_id=1, source_target_pairs={{0,4},{1,5},{2,6},{3,7},{4,0},{5,1},{6,2},{7,3},{8,12},{9,13},{10,... | collective-permute-start | bytes 196616 | tf_op jit(solution)/shard_map/ppermute | solution.py:488
  16.6 0.9 collective-permute-done.1.other
  17.5 4.2 %collective-permute-start.4 = (bf16[16,1024]{1,0:T(8,128)(2,1)S(1)}, bf16[16,1024]{1,0:T(8,128)(2,1)S(1)}, u32[]{:S(2)}, u32[]{:S(2)}) collective-permute-start(bf16[16,1024]{1,0:T(8,128)(2,1)S(1)} %pad_maximum_fusion.2), channel_id=1, source_target_pairs={{0,24},{4,28},{1,25},{5,29},{2,26},{6,30},{3,27},{7,31}} | collective-permute-start | bytes 98312 | tf_op jit(solution)/shard_map/ppermute | solution.py:484
  21.8 1.3 collective-permute-start.3
  23.1 2.5 %collective-permute-start.2 = (bf16[16,1024]{1,0:T(8,128)(2,1)S(1)}, bf16[16,1024]{1,0:T(8,128)(2,1)S(1)}, u32[]{:S(2)}, u32[]{:S(2)}) collective-permute-start(bf16[16,1024]{1,0:T(8,128)(2,1)S(1)} %pad_maximum_fusion.2), channel_id=1, source_target_pairs={{0,8},{4,12},{8,16},{12,20},{16,24},{20,28},{1,9},{5,13},{9,17},{1... | collective-permute-start | bytes 98312 | tf_op jit(solution)/shard_map/ppermute | solution.py:484
  25.6 3.5 %da.1 = (bf16[1024,512]{1,0:T(8,128)(2,1)S(1)}, bf16[1024,2048]{1,0:T(8,128)(2,1)S(1)}) custom-call(bf16[8,128,512]{2,1,0:T(8,128)(2,1)S(1)} %copy-done.8, bf16[256,256]{1,0:T(8,128)(2,1)S(1)} %copy-done.6, bf16[2048,512]{1,0:T(8,128)(2,1)S(1)} %copy-done.5), custom_call_target="tpu_custom_call" | custom-call | flops 1024 | bytes 1024 | tf_op jit(solution)/shard_map/da/pallas_call | solution.py:704
  29.2 14.4 %core.1 = (f32[1024,512]{1,0:T(8,128)}, bf16[1024,1024]{1,0:T(8,128)(2,1)S(1)}, bf16[1024,1024]{1,0:T(8,128)(2,1)S(1)}, bf16[1024,512]{1,0:T(8,128)(2,1)S(1)}, b...) custom-call(s32[12]{0:T(128)S(1)} %concatenate.17.scal, ...), custom_call_target="tpu_custom_call" | custom-call | flops 1024 | bytes 1024 | tf_op jit(solution)/shard_map/core/pallas_call | solution.py:704
  43.6 1.2 collective-permute-done.5.fother
  44.8 1.3 collective-permute-start.8
  46.1 1.3 collective-permute-start.7
  47.4 1.3 collective-permute-start.6
  48.7 3.7 %ffn_grad.2 = bf16[2048,512]{1,0:T(8,128)(2,1)S(1)} custom-call(s32[12]{0:T(128)S(1)} %concatenate.17.scal, bf16[1024,2048]{1,0:T(8,128)(2,1)S(1)} %get-tuple-element.136.act, bf16[1024,512]{1,0:T(8,128)(2,1)S(1)} %get-tuple-element.106.gl, bf16[1024,512]{1,0:T(8,128)(2,1)S(1)} %get-tuple-element.121.n2, bf16[1024,2048]{1,0:T(8,128)(2,1)S(1)} %get-tuple-element.127.dp), custom_call_target="tpu_custom_call" | custom-call | flops 1024 | bytes 1024 | tf_op jit(solution)/shard_map/ffn_grad/pallas_call | solution.py:704
  52.7 0.6 collective-permute-done.7.refs_1_
  53.5 3.7 %ffn_grad.3 = bf16[2048,512]{1,0:T(8,128)(2,1)S(1)} custom-call(s32[12]{0:T(128)S(1)} %concatenate.17.scal, bf16[1024,2048]{1,0:T(8,128)(2,1)S(1)} %get-tuple-element.136.act, bf16[1024,512]{1,0:T(8,128)(2,1)S(1)} %get-tuple-element.106.gl, bf16[1024,512]{1,0:T(8,128)(2,1)S(1)} %get-tuple-element.121.n2, bf16[1024,2048]{1,0:T(8,128)(2,1)S(1)} %get-tuple-element.127.dp), custom_call_target="tpu_custom_call" | custom-call | flops 30000001024 | bytes 1024 | tf_op jit(solution)/shard_map/ffn_grad/pallas_call | solution.py:704
  57.2 0.6 add_convert_fusion
  57.8 1.6 collective-permute-start.10
  59.4 3.7 %gates.1 = (bf16[1024,1024]{1,0:T(8,128)(2,1)S(1)}, bf16[1024,1024]{1,0:T(8,128)(2,1)S(1)}, bf16[32,512]{1,0:T(8,128)(2,1)S(1)}, f32[8,1024]{1,0:T(8,128)S(1)}) custom-call(s32[12]{0:T(128)S(1)} %concatenate.17.scal, bf16[1024,1024]{1,0:T(8,128)(2,1)S(1)} %get-tuple-element.116.dh, bf16[1024,1024]{1,0:T(8,128)(2,1)S(1)} %get-tuple-element.110.zl.zl_next.zl_before, ...), custom_call_target="tpu_custom_call" | custom-call | flops 1024 | bytes 1024 | tf_op jit(solution)/shard_map/gates/pallas_call | solution.py:704
  63.1 2.4 %gate_grad.2 = bf16[1536,512]{1,0:T(8,128)(2,1)S(1)} custom-call(s32[12]{0:T(128)S(1)} %concatenate.17.scal, bf16[1024,512]{1,0:T(8,128)(2,1)S(1)} %get-tuple-element.115.c, bf16[1024,1024]{1,0:T(8,128)(2,1)S(1)} %get-tuple-element.143.dkz, bf16[1024,1024]{1,0:T(8,128)(2,1)S(1)} %get-tuple-element.140.dkh, bf16[1024,1024]{1,0:T(8,128)(2,1)S(1)} %get-tuple-element.134.y, ...), custom_call_target="tpu_custom_call" | custom-call | flops 1024 | bytes 1024 | tf_op jit(solution)/shard_map/gate_grad/pallas_call | solution.py:704
  65.6 1.5 collective-permute-start.12
  67.1 5.7 %output.1 = bf16[8,128,512]{2,1,0:T(8,128)(2,1)} custom-call(f32[1024,512]{1,0:T(8,128)} %get-tuple-element.113.r1, bf16[1024,2048]{1,0:T(8,128)(2,1)S(1)} %get-tuple-element.136.act, bf16[256,256]{1,0:T(8,128)(2,1)S(1)} %copy-done.9, bf16[2048,512]{1,0:T(8,128)(2,1)S(1)} %copy-done.5), custom_call_target="tpu_custom_call" | custom-call | flops 1024 | bytes 1024 | tf_op jit(solution)/shard_map/output/pallas_call | solution.py:704
  72.7 1.1 add_convert_fusion.4
  73.8 1.5 collective-permute-start.14
  75.3 2.4 %gate_grad.3 = bf16[1536,512]{1,0:T(8,128)(2,1)S(1)} custom-call(s32[12]{0:T(128)S(1)} %concatenate.17.scal, bf16[1024,512]{1,0:T(8,128)(2,1)S(1)} %get-tuple-element.115.c, bf16[1024,1024]{1,0:T(8,128)(2,1)S(1)} %get-tuple-element.143.dkz, bf16[1024,1024]{1,0:T(8,128)(2,1)S(1)} %get-tuple-element.140.dkh, bf16[1024,1024]{1,0:T(8,128)(2,1)S(1)} %get-tuple-element.134.y, ...), custom_call_target="tpu_custom_call" | custom-call | flops 30000001024 | bytes 1024 | tf_op jit(solution)/shard_map/gate_grad/pallas_call | solution.py:704
  77.8 1.3 add_convert_fusion.2
  79.1 1.4 collective-permute-start.13
  80.6 11.0 %tail.1 = (bf16[8,128,512]{2,1,0:T(8,128)(2,1)}, f32[40,512]{1,0:T(8,128)S(1)}) custom-call(bf16[8,128,512]{2,1,0:T(8,128)(2,1)} %x.5, f32[1024,512]{1,0:T(8,128)} %get-tuple-element.137.dr1, bf16[1024,1024]{1,0:T(8,128)(2,1)} %copy-done.3, bf16[1024,1024]{1,0:T(8,128)(2,1)} %copy-done.4, bf16[256,256]{1,0:T(8,128)(2,1)} %constant.29.clone.perm.pm, ...), custom_call_target="tpu_custom_call" | custom-call | flops 1024 | bytes 1024 | tf_op jit(solution)/shard_map/tail/pallas_call | solution.py:704
  91.6 1.2 add_convert_fusion.8
  92.8 2.2 %collective-permute-start.16 = (bf16[256,512]{1,0:T(8,128)(2,1)S(1)}, bf16[256,512]{1,0:T(8,128)(2,1)S(1)}, u32[]{:S(2)}, u32[]{:S(2)}) collective-permute-start(bf16[256,512]{1,0:T(8,128)(2,1)S(1)} %get-tuple-element.212), channel_id=1, source_target_pairs={{0,8},{1,9},{2,10},{3,11},{4,20},{5,21},{6,22},{7,23},{8,0},{9,1},... | collective-permute-start | bytes 786440 | tf_op jit(solution)/shard_map/ppermute | solution.py:488
  95.2 1.2 collective-permute-start.15
  96.4 5.6 %collective-permute-done.16 = bf16[256,512]{1,0:T(8,128)(2,1)S(1)} collective-permute-done((bf16[256,512]{1,0:T(8,128)(2,1)S(1)}, bf16[256,512]{1,0:T(8,128)(2,1)S(1)}, u32[]{:S(2)}, u32[]{:S(2)}) %collective-permute-start.16) | collective-permute-done | bytes 262176 | tf_op jit(solution)/shard_map/ppermute | solution.py:488
  102.1 3.0 %collective-permute-start.18 = (bf16[128,512]{1,0:T(8,128)(2,1)S(1)}, bf16[128,512]{1,0:T(8,128)(2,1)S(1)}, u32[]{:S(2)}, u32[]{:S(2)}) collective-permute-start(bf16[128,512]{1,0:T(8,128)(2,1)S(1)} %add_convert_fusion.14), channel_id=1, source_target_pairs={{0,16},{1,17},{2,18},{3,19},{4,12},{5,13},{6,14},{7,15},{8,24},{9,... | collective-permute-start | bytes 393224 | tf_op jit(solution)/shard_map/ppermute | solution.py:488
  105.2 2.5 %collective-permute-start.17 = (bf16[192,512]{1,0:T(8,128)(2,1)S(1)}, bf16[192,512]{1,0:T(8,128)(2,1)S(1)}, u32[]{:S(2)}, u32[]{:S(2)}) collective-permute-start(bf16[192,512]{1,0:T(8,128)(2,1)S(1)} %get-tuple-element.213), channel_id=1, source_target_pairs={{0,8},{1,9},{2,10},{3,11},{4,20},{5,21},{6,22},{7,23},{8,0},{9,1},... | collective-permute-start | bytes 589832 | tf_op jit(solution)/shard_map/ppermute | solution.py:488
  107.7 0.7 collective-permute-done.18
  108.5 3.4 %collective-permute-start.20 = (bf16[128,512]{1,0:T(8,128)(2,1)S(1)}, bf16[128,512]{1,0:T(8,128)(2,1)S(1)}, u32[]{:S(2)}, u32[]{:S(2)}) collective-permute-start(bf16[128,512]{1,0:T(8,128)(2,1)S(1)} %add_convert_fusion.12.mine), channel_id=1, source_target_pairs={{0,16},{1,17},{2,18},{3,19},{4,12},{5,13},{6,14},{7,15},{8,24},{9,... | collective-permute-start | bytes 393224 | tf_op jit(solution)/shard_map/ppermute | solution.py:488
  111.9 3.7 %collective-permute-done.17 = bf16[192,512]{1,0:T(8,128)(2,1)S(1)} collective-permute-done((bf16[192,512]{1,0:T(8,128)(2,1)S(1)}, bf16[192,512]{1,0:T(8,128)(2,1)S(1)}, u32[]{:S(2)}, u32[]{:S(2)}) %collective-permute-start.17) | collective-permute-done | bytes 196640 | tf_op jit(solution)/shard_map/ppermute | solution.py:488
  115.6 0.7 collective-permute-start.19
  116.3 9.2 %collective-permute-start.23 = (bf16[256,512]{1,0:T(8,128)(2,1)S(1)}, bf16[256,512]{1,0:T(8,128)(2,1)S(1)}, u32[]{:S(2)}, u32[]{:S(2)}) collective-permute-start(bf16[256,512]{1,0:T(8,128)(2,1)S(1)} %chain.3.mine), channel_id=1, source_target_pairs={{0,8},{1,9},{2,10},{3,11},{4,20},{5,21},{6,22},{7,23},{8,0},{9,1},... | collective-permute-start | bytes 786440 | tf_op jit(solution)/shard_map/ppermute | solution.py:488
  125.6 1.0 collective-permute-done.19
  126.6 2.5 %collective-permute-start.21 = (bf16[112,512]{1,0:T(8,128)(2,1)S(1)}, bf16[112,512]{1,0:T(8,128)(2,1)S(1)}, u32[]{:S(2)}, u32[]{:S(2)}) collective-permute-start(bf16[112,512]{1,0:T(8,128)(2,1)S(1)} %pad_maximum_fusion.mine), channel_id=1, source_target_pairs={{0,16},{1,17},{2,18},{3,19},{4,12},{5,13},{6,14},{7,15},{8,24},{9,... | collective-permute-start | bytes 344072 | tf_op jit(solution)/shard_map/ppermute | solution.py:488
  129.1 5.5 %collective-permute-done.21.recv = bf16[112,512]{1,0:T(8,128)(2,1)S(1)} collective-permute-done((bf16[112,512]{1,0:T(8,128)(2,1)S(1)}, bf16[112,512]{1,0:T(8,128)(2,1)S(1)}, u32[]{:S(2)}, u32[]{:S(2)}) %collective-permute-start.21) | collective-permute-done | bytes 114720 | tf_op jit(solution)/shard_map/ppermute | solution.py:488
  134.6 0.3 collective-permute-start.22
  135.0 1.3 collective-permute-start.25
  136.3 4.2 %collective-permute-done.22.recv = bf16[208,512]{1,0:T(8,128)(2,1)S(1)} collective-permute-done((bf16[208,512]{1,0:T(8,128)(2,1)S(1)}, bf16[208,512]{1,0:T(8,128)(2,1)S(1)}, u32[]{:S(2)}, u32[]{:S(2)}) %collective-permute-start.22) | collective-permute-done | bytes 213024 | tf_op jit(solution)/shard_map/ppermute | solution.py:488
  140.6 1.3 collective-permute-start.24
  141.9 2.3 %collective-permute-done.25.recv = bf16[512,512]{1,0:T(8,128)(2,1)S(1)} collective-permute-done((bf16[512,512]{1,0:T(8,128)(2,1)S(1)}, bf16[512,512]{1,0:T(8,128)(2,1)S(1)}, u32[]{:S(2)}, u32[]{:S(2)}) %collective-permute-start.25) | collective-permute-done | bytes 524320 | tf_op jit(solution)/shard_map/ppermute | solution.py:488
  144.4 1.5 collective-permute-start.28
  145.9 3.9 %collective-permute-done.24.recv = bf16[400,512]{1,0:T(8,128)(2,1)S(1)} collective-permute-done((bf16[400,512]{1,0:T(8,128)(2,1)S(1)}, bf16[400,512]{1,0:T(8,128)(2,1)S(1)}, u32[]{:S(2)}, u32[]{:S(2)}) %collective-permute-start.24) | collective-permute-done | bytes 409632 | tf_op jit(solution)/shard_map/ppermute | solution.py:488
  149.9 1.5 collective-permute-start.26
  151.3 2.0 %spread_ffn.4 = (f32[2048,512]{1,0:T(8,128)}, f32[512,2048]{1,0:T(8,128)}) custom-call(s32[12]{0:T(128)S(1)} %concatenate.17.scal, bf16[1024,512]{1,0:T(8,128)(2,1)S(1)} %chain.5.src), custom_call_target="tpu_custom_call" | custom-call | flops 10000000000 | bytes 1024 | tf_op jit(solution)/shard_map/spread_ffn/pallas_call | solution.py:440
  153.3 2.0 %spread_ffn.5 = (f32[2048,512]{1,0:T(8,128)}, f32[512,2048]{1,0:T(8,128)}) custom-call(s32[12]{0:T(128)S(1)} %concatenate.17.scal, bf16[1024,512]{1,0:T(8,128)(2,1)S(1)} %collective-permute-done.29.src, f32[2048,512]{1,0:T(8,128)} %get-tuple-element.167.refs_0_, f32[512,2048]{1,0:T(8,128)} %get-tuple-element.169.refs_1_), custom_call_target="tpu_custom_call", output_to_operand_aliasing={{0}: (2, {}), {1}: (3, {})} | custom-call | flops 10000000000 | bytes 1024 | tf_op jit(solution)/shard_map/spread_ffn/pallas_call | solution.py:440
  155.3 4.0 %collective-permute-done.28.src = bf16[1024,512]{1,0:T(8,128)(2,1)S(1)} collective-permute-done((bf16[1024,512]{1,0:T(8,128)(2,1)S(1)}, bf16[1024,512]{1,0:T(8,128)(2,1)S(1)}, u32[]{:S(2)}, u32[]{:S(2)}) %collective-permute-start.28) | collective-permute-done | bytes 1048608 | tf_op jit(solution)/shard_map/ppermute | solution.py:488
  159.3 0.7 collective-permute-start.30
  160.0 2.0 %spread_ffn.6 = (f32[2048,512]{1,0:T(8,128)}, f32[512,2048]{1,0:T(8,128)}) custom-call(s32[12]{0:T(128)S(1)} %concatenate.17.scal, bf16[1024,512]{1,0:T(8,128)(2,1)S(1)} %collective-permute-done.28.src, f32[2048,512]{1,0:T(8,128)} %get-tuple-element.170.refs_0_, f32[512,2048]{1,0:T(8,128)} %get-tuple-element.173.refs_1_), custom_call_target="tpu_custom_call", output_to_operand_aliasing={{0}: (2, {}), {1}: (3, {})} | custom-call | flops 10000000000 | bytes 1024 | tf_op jit(solution)/shard_map/spread_ffn/pallas_call | solution.py:440
  162.0 1.7 %spread_gates.3 = (f32[512,1024]{1,0:T(8,128)}, f32[512,1024]{1,0:T(8,128)}, f32[1024,512]{1,0:T(8,128)}) custom-call(s32[12]{0:T(128)S(1)} %concatenate.17.scal, bf16[784,512]{1,0:T(8,128)(2,1)S(1)} %get-tuple-element.175.src), custom_call_target="tpu_custom_call" | custom-call | flops 10000000000 | bytes 1024 | tf_op jit(solution)/shard_map/spread_gates/pallas_call | solution.py:440
  163.7 2.0 %spread_ffn.7 = (f32[2048,512]{1,0:T(8,128)}, f32[512,2048]{1,0:T(8,128)}) custom-call(s32[12]{0:T(128)S(1)} %concatenate.17.scal, bf16[1024,512]{1,0:T(8,128)(2,1)S(1)} %collective-permute-done.30.src, f32[2048,512]{1,0:T(8,128)} %get-tuple-element.174.refs_0_, f32[512,2048]{1,0:T(8,128)} %get-tuple-element.178.refs_1_), custom_call_target="tpu_custom_call", output_to_operand_aliasing={{0}: (2, {}), {1}: (3, {})} | custom-call | flops 10000000000 | bytes 1024 | tf_op jit(solution)/shard_map/spread_ffn/pallas_call | solution.py:440
  165.7 1.7 %spread_gates.4 = (f32[512,1024]{1,0:T(8,128)}, f32[512,1024]{1,0:T(8,128)}, f32[1024,512]{1,0:T(8,128)}) custom-call(s32[12]{0:T(128)S(1)} %concatenate.17.scal, bf16[784,512]{1,0:T(8,128)(2,1)S(1)} %collective-permute-done.27.src.theirs, f32[512,1024]{1,0:T(8,128)} %get-tuple-element.176.refs_0_, ...), custom_call_target="tpu_custom_call", output_to_operand_aliasing={{0}: (2, {}), {1}: (3, {}), {2}: (4, {})} | custom-call | flops 10000000000 | bytes 1024 | tf_op jit(solution)/shard_map/spread_gates/pallas_call | solution.py:440
  167.5 0.4 collective-permute-done.26.src.rest
  167.9 0.4 collective-permute-start.31
  168.3 1.7 %spread_gates.5 = (f32[512,1024]{1,0:T(8,128)}, f32[512,1024]{1,0:T(8,128)}, f32[1024,512]{1,0:T(8,128)}) custom-call(s32[12]{0:T(128)S(1)} %concatenate.17.scal, bf16[784,512]{1,0:T(8,128)(2,1)S(1)} %collective-permute-done.26.src.rest, f32[512,1024]{1,0:T(8,128)} %get-tuple-element.183.refs_0_, ...), custom_call_target="tpu_custom_call", output_to_operand_aliasing={{0}: (2, {}), {1}: (3, {}), {2}: (4, {})} | custom-call | flops 10000000000 | bytes 1024 | tf_op jit(solution)/shard_map/spread_gates/pallas_call | solution.py:440
  170.2 1.8 %spread_last.1 = (f32[512,1024]{1,0:T(8,128)}, f32[512,1024]{1,0:T(8,128)}, f32[1024,512]{1,0:T(8,128)}, f32[1,512]{1,0:T(1,128)}, f32[4,512]{1,0:T(4,128)}, /*index=5*/f32[1,512]{1,0:T(1,128)}, f32[1,1024]{1,0:T(1,128)}) custom-call(s32[12]{0:T(128)S(1)} %concatenate.17.scal, ...), custom_call_target="tpu_custom_call", output_to_operand_aliasing={{0}: (5, {}), {1}: (6, {}), {2}: (7, {})} | custom-call | flops 10000000000 | bytes 1024 | tf_op jit(solution)/shard_map/spread_last/pallas_call | solution.py:418
  (75 shorter events, 2.0 us)
Async XLA Ops:
  0.6 6.5 %copy-start.11 = (s32[8]{0:T(128)S(1)}, s32[8]{0:T(128)}, u32[]{:S(2)}) copy-start(s32[8]{0:T(128)} %param.15) | copy-start | bytes 100
  0.7 6.6 %copy-start.2 = (bf16[512,1024]{1,0:T(8,128)(2,1)S(1)}, bf16[512,1024]{1,0:T(8,128)(2,1)}, u32[]{:S(2)}) copy-start(bf16[512,1024]{1,0:T(8,128)(2,1)} %wc.3) | copy-start | bytes 3145732
  0.7 6.6 %copy-start.1 = (bf16[512,1024]{1,0:T(8,128)(2,1)S(1)}, bf16[512,1024]{1,0:T(8,128)(2,1)}, u32[]{:S(2)}) copy-start(bf16[512,1024]{1,0:T(8,128)(2,1)} %wg.3) | copy-start | bytes 3145732
  1.7 5.5 %collective-permute-start = (bf16[24,512]{1,0:T(8,128)(2,1)S(1)}, bf16[24,512]{1,0:T(8,128)(2,1)S(1)}, u32[]{:S(2)}, u32[]{:S(2)}) collective-permute-start(bf16[24,512]{1,0:T(8,128)(2,1)S(1)} %bitcast.19), channel_id=1, source_target_pairs={{0,4},{4,8},{8,12},{12,16},{16,20},{20,24},{24,28},{1,5},{5,9},{9,... | collective-permute-start | bytes 73736 | tf_op jit(solution)/shard_map/ppermute | solution.py:484
  7.1 18.5 %copy-start.6 = (bf16[256,256]{1,0:T(8,128)(2,1)S(1)}, bf16[256,256]{1,0:T(8,128)(2,1)}, u32[]{:S(2)}) copy-start(bf16[256,256]{1,0:T(8,128)(2,1)} %constant.29.clone.perm.pm) | copy-start | bytes 393220
  7.2 18.4 %copy-start.5 = (bf16[2048,512]{1,0:T(8,128)(2,1)S(1)}, bf16[2048,512]{1,0:T(8,128)(2,1)}, u32[]{:S(2)}) copy-start(bf16[2048,512]{1,0:T(8,128)(2,1)} %wd.3) | copy-start | bytes 6291460
  7.2 18.4 %copy-start.8 = (bf16[8,128,512]{2,1,0:T(8,128)(2,1)S(1)}, bf16[8,128,512]{2,1,0:T(8,128)(2,1)}, u32[]{:S(2)}) copy-start(bf16[8,128,512]{2,1,0:T(8,128)(2,1)} %g.1) | copy-start | bytes 3145732
  13.8 15.4 %copy-start = (bf16[8,128,512]{2,1,0:T(8,128)(2,1)S(1)}, bf16[8,128,512]{2,1,0:T(8,128)(2,1)}, u32[]{:S(2)}) copy-start(bf16[8,128,512]{2,1,0:T(8,128)(2,1)} %x.5) | copy-start | bytes 3145732
  13.8 15.4 %copy-start.7 = (bf16[512,2048]{1,0:T(8,128)(2,1)S(1)}, bf16[512,2048]{1,0:T(8,128)(2,1)}, u32[]{:S(2)}) copy-start(bf16[512,2048]{1,0:T(8,128)(2,1)} %refs_5_.1) | copy-start | bytes 6291460
  13.8 15.4 %copy-start.10 = (f32[512]{0:T(512)S(1)}, f32[512]{0:T(512)}, u32[]{:S(2)}) copy-start(f32[512]{0:T(512)} %param.22) | copy-start | bytes 6148
  13.8 3.7 %collective-permute-start.1 = (f32[16,1024]{1,0:T(8,128)S(1)}, f32[16,1024]{1,0:T(8,128)S(1)}, u32[]{:S(2)}, u32[]{:S(2)}) collective-permute-start(f32[16,1024]{1,0:T(8,128)S(1)} %get-tuple-element.112), channel_id=1, source_target_pairs={{0,4},{1,5},{2,6},{3,7},{4,0},{5,1},{6,2},{7,3},{8,12},{9,13},{10,... | collective-permute-start | bytes 196616 | tf_op jit(solution)/shard_map/ppermute | solution.py:488
  17.5 11.6 %collective-permute-start.4 = (bf16[16,1024]{1,0:T(8,128)(2,1)S(1)}, bf16[16,1024]{1,0:T(8,128)(2,1)S(1)}, u32[]{:S(2)}, u32[]{:S(2)}) collective-permute-start(bf16[16,1024]{1,0:T(8,128)(2,1)S(1)} %pad_maximum_fusion.2), channel_id=1, source_target_pairs={{0,24},{4,28},{1,25},{5,29},{2,26},{6,30},{3,27},{7,31}} | collective-permute-start | bytes 98312 | tf_op jit(solution)/shard_map/ppermute | solution.py:484
  21.8 7.4 %collective-permute-start.3 = (bf16[16,1024]{1,0:T(8,128)(2,1)S(1)}, bf16[16,1024]{1,0:T(8,128)(2,1)S(1)}, u32[]{:S(2)}, u32[]{:S(2)}) collective-permute-start(bf16[16,1024]{1,0:T(8,128)(2,1)S(1)} %pad_maximum_fusion.2), channel_id=1, source_target_pairs={{0,16},{4,20},{8,24},{12,28},{1,17},{5,21},{9,25},{13,29},{2,18},{... | collective-permute-start | bytes 98312 | tf_op jit(solution)/shard_map/ppermute | solution.py:484
  23.1 6.1 %collective-permute-start.2 = (bf16[16,1024]{1,0:T(8,128)(2,1)S(1)}, bf16[16,1024]{1,0:T(8,128)(2,1)S(1)}, u32[]{:S(2)}, u32[]{:S(2)}) collective-permute-start(bf16[16,1024]{1,0:T(8,128)(2,1)S(1)} %pad_maximum_fusion.2), channel_id=1, source_target_pairs={{0,8},{4,12},{8,16},{12,20},{16,24},{20,28},{1,9},{5,13},{9,17},{1... | collective-permute-start | bytes 98312 | tf_op jit(solution)/shard_map/ppermute | solution.py:484
  43.6 1.2 collective-permute-start.5
  44.8 7.8 %collective-permute-start.8 = (bf16[16,1024]{1,0:T(8,128)(2,1)S(1)}, bf16[16,1024]{1,0:T(8,128)(2,1)S(1)}, u32[]{:S(2)}, u32[]{:S(2)}) collective-permute-start(bf16[16,1024]{1,0:T(8,128)(2,1)S(1)} %pad_maximum_fusion.1), channel_id=1, source_target_pairs={{24,0},{28,4},{25,1},{29,5},{26,2},{30,6},{27,3},{31,7}} | collective-permute-start | bytes 98312 | tf_op jit(solution)/shard_map/ppermute | solution.py:484
  46.1 7.1 %collective-permute-start.7 = (bf16[16,1024]{1,0:T(8,128)(2,1)S(1)}, bf16[16,1024]{1,0:T(8,128)(2,1)S(1)}, u32[]{:S(2)}, u32[]{:S(2)}) collective-permute-start(bf16[16,1024]{1,0:T(8,128)(2,1)S(1)} %pad_maximum_fusion.1), channel_id=1, source_target_pairs={{16,0},{20,4},{24,8},{28,12},{17,1},{21,5},{25,9},{29,13},{18,2},{... | collective-permute-start | bytes 98312 | tf_op jit(solution)/shard_map/ppermute | solution.py:484
  47.4 6.1 %collective-permute-start.6 = (bf16[16,1024]{1,0:T(8,128)(2,1)S(1)}, bf16[16,1024]{1,0:T(8,128)(2,1)S(1)}, u32[]{:S(2)}, u32[]{:S(2)}) collective-permute-start(bf16[16,1024]{1,0:T(8,128)(2,1)S(1)} %pad_maximum_fusion.1), channel_id=1, source_target_pairs={{8,0},{12,4},{16,8},{20,12},{24,16},{28,20},{9,1},{13,5},{17,9},{2... | collective-permute-start | bytes 98312 | tf_op jit(solution)/shard_map/ppermute | solution.py:484
  52.4 4.7 %collective-permute-start.9 = (bf16[2048,512]{1,0:T(8,128)(2,1)S(1)}, bf16[2048,512]{1,0:T(8,128)(2,1)S(1)}, u32[]{:S(2)}, u32[]{:S(2)}) collective-permute-start(bf16[2048,512]{1,0:T(8,128)(2,1)S(1)} %ffn_grad.2), channel_id=1, source_target_pairs={{0,4},{1,5},{2,6},{3,7},{4,0},{5,1},{6,2},{7,3},{8,12},{9,13},{10,... | collective-permute-start | bytes 6291464 | tf_op jit(solution)/shard_map/ppermute | solution.py:488
  57.8 14.9 %collective-permute-start.10 = (bf16[1024,512]{1,0:T(8,128)(2,1)S(1)}, bf16[1024,512]{1,0:T(8,128)(2,1)S(1)}, u32[]{:S(2)}, u32[]{:S(2)}) collective-permute-start(bf16[1024,512]{1,0:T(8,128)(2,1)S(1)} %get-tuple-element.204.refs_5_), channel_id=1, source_target_pairs={{0,1},{1,0},{2,3},{3,2},{4,6},{5,7},{6,4},{7,5},{8,9},{9,8},{10,11... | collective-permute-start | bytes 3145736 | tf_op jit(solution)/shard_map/ppermute | solution.py:488
  63.1 12.3 %copy-start.3 = (bf16[1024,1024]{1,0:T(8,128)(2,1)}, bf16[1024,1024]{1,0:T(8,128)(2,1)S(1)}, u32[]{:S(2)}) copy-start(bf16[1024,1024]{1,0:T(8,128)(2,1)S(1)} %get-tuple-element.143.dkz) | copy-start | bytes 6291460
  63.1 12.3 %copy-start.4 = (bf16[1024,1024]{1,0:T(8,128)(2,1)}, bf16[1024,1024]{1,0:T(8,128)(2,1)S(1)}, u32[]{:S(2)}) copy-start(bf16[1024,1024]{1,0:T(8,128)(2,1)S(1)} %get-tuple-element.140.dkh) | copy-start | bytes 6291460
  63.1 4.0 %copy-start.9 = (bf16[256,256]{1,0:T(8,128)(2,1)S(1)}, bf16[256,256]{1,0:T(8,128)(2,1)}, u32[]{:S(2)}) copy-start(bf16[256,256]{1,0:T(8,128)(2,1)} %constant.30.clone.perm.back_pm) | copy-start | bytes 393220
  65.5 12.3 %collective-permute-start.11 = (bf16[1536,512]{1,0:T(8,128)(2,1)S(1)}, bf16[1536,512]{1,0:T(8,128)(2,1)S(1)}, u32[]{:S(2)}, u32[]{:S(2)}) collective-permute-start(bf16[1536,512]{1,0:T(8,128)(2,1)S(1)} %gate_grad.2), channel_id=1, source_target_pairs={{0,4},{1,5},{2,6},{3,7},{4,0},{5,1},{6,2},{7,3},{8,12},{9,13},{10,... | collective-permute-start | bytes 4718600 | tf_op jit(solution)/shard_map/ppermute | solution.py:488
  65.6 12.2 %collective-permute-start.12 = (bf16[24,512]{1,0:T(8,128)(2,1)S(1)}, bf16[24,512]{1,0:T(8,128)(2,1)S(1)}, u32[]{:S(2)}, u32[]{:S(2)}) collective-permute-start(bf16[24,512]{1,0:T(8,128)(2,1)S(1)} %slice.134), channel_id=1, source_target_pairs={{4,0},{8,4},{12,8},{16,12},{20,16},{24,20},{28,24},{5,1},{9,5},{13... | collective-permute-start | bytes 73736 | tf_op jit(solution)/shard_map/ppermute | solution.py:484
  73.8 17.8 %collective-permute-start.14 = (bf16[512,512]{1,0:T(8,128)(2,1)}, bf16[512,512]{1,0:T(8,128)(2,1)}, u32[]{:S(2)}, u32[]{:S(2)}) collective-permute-start(bf16[512,512]{1,0:T(8,128)(2,1)} %get-tuple-element.208), channel_id=1, source_target_pairs={{0,2},{1,3},{2,0},{3,1},{4,5},{5,4},{6,7},{7,6},{8,10},{9,11},{10,... | collective-permute-start | bytes 1572872 | tf_op jit(solution)/shard_map/ppermute | solution.py:488
  79.1 15.9 %collective-permute-start.13 = (bf16[768,512]{1,0:T(8,128)(2,1)}, bf16[768,512]{1,0:T(8,128)(2,1)S(1)}, u32[]{:S(2)}, u32[]{:S(2)}) collective-permute-start(bf16[768,512]{1,0:T(8,128)(2,1)} %get-tuple-element.206), channel_id=1, source_target_pairs={{0,1},{1,0},{2,3},{3,2},{4,6},{5,7},{6,4},{7,5},{8,9},{9,8},{10,11... | collective-permute-start | bytes 2359304 | tf_op jit(solution)/shard_map/ppermute | solution.py:488
  92.8 9.2 %collective-permute-start.16 = (bf16[256,512]{1,0:T(8,128)(2,1)S(1)}, bf16[256,512]{1,0:T(8,128)(2,1)S(1)}, u32[]{:S(2)}, u32[]{:S(2)}) collective-permute-start(bf16[256,512]{1,0:T(8,128)(2,1)S(1)} %get-tuple-element.212), channel_id=1, source_target_pairs={{0,8},{1,9},{2,10},{3,11},{4,20},{5,21},{6,22},{7,23},{8,0},{9,1},... | collective-permute-start | bytes 786440 | tf_op jit(solution)/shard_map/ppermute | solution.py:488
  95.2 9.9 %collective-permute-start.15 = (bf16[384,512]{1,0:T(8,128)(2,1)S(1)}, bf16[384,512]{1,0:T(8,128)(2,1)S(1)}, u32[]{:S(2)}, u32[]{:S(2)}) collective-permute-start(bf16[384,512]{1,0:T(8,128)(2,1)S(1)} %get-tuple-element.209), channel_id=1, source_target_pairs={{0,2},{1,3},{2,0},{3,1},{4,5},{5,4},{6,7},{7,6},{8,10},{9,11},{10,... | collective-permute-start | bytes 1179656 | tf_op jit(solution)/shard_map/ppermute | solution.py:488
  102.1 6.4 %collective-permute-start.18 = (bf16[128,512]{1,0:T(8,128)(2,1)S(1)}, bf16[128,512]{1,0:T(8,128)(2,1)S(1)}, u32[]{:S(2)}, u32[]{:S(2)}) collective-permute-start(bf16[128,512]{1,0:T(8,128)(2,1)S(1)} %add_convert_fusion.14), channel_id=1, source_target_pairs={{0,16},{1,17},{2,18},{3,19},{4,12},{5,13},{6,14},{7,15},{8,24},{9,... | collective-permute-start | bytes 393224 | tf_op jit(solution)/shard_map/ppermute | solution.py:488
  105.2 10.4 %collective-permute-start.17 = (bf16[192,512]{1,0:T(8,128)(2,1)S(1)}, bf16[192,512]{1,0:T(8,128)(2,1)S(1)}, u32[]{:S(2)}, u32[]{:S(2)}) collective-permute-start(bf16[192,512]{1,0:T(8,128)(2,1)S(1)} %get-tuple-element.213), channel_id=1, source_target_pairs={{0,8},{1,9},{2,10},{3,11},{4,20},{5,21},{6,22},{7,23},{8,0},{9,1},... | collective-permute-start | bytes 589832 | tf_op jit(solution)/shard_map/ppermute | solution.py:488
  108.5 7.8 %collective-permute-start.20 = (bf16[128,512]{1,0:T(8,128)(2,1)S(1)}, bf16[128,512]{1,0:T(8,128)(2,1)S(1)}, u32[]{:S(2)}, u32[]{:S(2)}) collective-permute-start(bf16[128,512]{1,0:T(8,128)(2,1)S(1)} %add_convert_fusion.12.mine), channel_id=1, source_target_pairs={{0,16},{1,17},{2,18},{3,19},{4,12},{5,13},{6,14},{7,15},{8,24},{9,... | collective-permute-start | bytes 393224 | tf_op jit(solution)/shard_map/ppermute | solution.py:488
  115.6 10.9 %collective-permute-start.19 = (bf16[96,512]{1,0:T(8,128)(2,1)S(1)}, bf16[96,512]{1,0:T(8,128)(2,1)S(1)}, u32[]{:S(2)}, u32[]{:S(2)}) collective-permute-start(bf16[96,512]{1,0:T(8,128)(2,1)S(1)} %add_convert_fusion.16), channel_id=1, source_target_pairs={{0,16},{1,17},{2,18},{3,19},{4,12},{5,13},{6,14},{7,15},{8,24},{9,... | collective-permute-start | bytes 294920 | tf_op jit(solution)/shard_map/ppermute | solution.py:488
  116.3 18.6 %collective-permute-start.23 = (bf16[256,512]{1,0:T(8,128)(2,1)S(1)}, bf16[256,512]{1,0:T(8,128)(2,1)S(1)}, u32[]{:S(2)}, u32[]{:S(2)}) collective-permute-start(bf16[256,512]{1,0:T(8,128)(2,1)S(1)} %chain.3.mine), channel_id=1, source_target_pairs={{0,8},{1,9},{2,10},{3,11},{4,20},{5,21},{6,22},{7,23},{8,0},{9,1},... | collective-permute-start | bytes 786440 | tf_op jit(solution)/shard_map/ppermute | solution.py:488
  126.6 8.0 %collective-permute-start.21 = (bf16[112,512]{1,0:T(8,128)(2,1)S(1)}, bf16[112,512]{1,0:T(8,128)(2,1)S(1)}, u32[]{:S(2)}, u32[]{:S(2)}) collective-permute-start(bf16[112,512]{1,0:T(8,128)(2,1)S(1)} %pad_maximum_fusion.mine), channel_id=1, source_target_pairs={{0,16},{1,17},{2,18},{3,19},{4,12},{5,13},{6,14},{7,15},{8,24},{9,... | collective-permute-start | bytes 344072 | tf_op jit(solution)/shard_map/ppermute | solution.py:488
  134.6 5.9 %collective-permute-start.22 = (bf16[208,512]{1,0:T(8,128)(2,1)S(1)}, bf16[208,512]{1,0:T(8,128)(2,1)S(1)}, u32[]{:S(2)}, u32[]{:S(2)}) collective-permute-start(bf16[208,512]{1,0:T(8,128)(2,1)S(1)} %get-tuple-element.157.mine), channel_id=1, source_target_pairs={{0,8},{1,9},{2,10},{3,11},{4,20},{5,21},{6,22},{7,23},{8,0},{9,1},... | collective-permute-start | bytes 638984 | tf_op jit(solution)/shard_map/ppermute | solution.py:488
  135.0 9.2 %collective-permute-start.25 = (bf16[512,512]{1,0:T(8,128)(2,1)S(1)}, bf16[512,512]{1,0:T(8,128)(2,1)S(1)}, u32[]{:S(2)}, u32[]{:S(2)}) collective-permute-start(bf16[512,512]{1,0:T(8,128)(2,1)S(1)} %chain.4.mine), channel_id=1, source_target_pairs={{0,2},{1,3},{2,0},{3,1},{4,5},{5,4},{6,7},{7,6},{8,10},{9,11},{10,... | collective-permute-start | bytes 1572872 | tf_op jit(solution)/shard_map/ppermute | solution.py:488
  140.6 9.1 %collective-permute-start.24 = (bf16[400,512]{1,0:T(8,128)(2,1)S(1)}, bf16[400,512]{1,0:T(8,128)(2,1)S(1)}, u32[]{:S(2)}, u32[]{:S(2)}) collective-permute-start(bf16[400,512]{1,0:T(8,128)(2,1)S(1)} %get-tuple-element.161.mine), channel_id=1, source_target_pairs={{0,2},{1,3},{2,0},{3,1},{4,5},{5,4},{6,7},{7,6},{8,10},{9,11},{10,... | collective-permute-start | bytes 1228808 | tf_op jit(solution)/shard_map/ppermute | solution.py:488
  144.3 9.0 %collective-permute-start.29 = (bf16[1024,512]{1,0:T(8,128)(2,1)S(1)}, bf16[1024,512]{1,0:T(8,128)(2,1)S(1)}, u32[]{:S(2)}, u32[]{:S(2)}) collective-permute-start(bf16[1024,512]{1,0:T(8,128)(2,1)S(1)} %chain.5.src), channel_id=1, source_target_pairs={{0,4},{1,5},{2,6},{3,7},{4,0},{5,1},{6,2},{7,3},{8,12},{9,13},{10,... | collective-permute-start | bytes 3145736 | tf_op jit(solution)/shard_map/ppermute | solution.py:488
  144.4 14.9 %collective-permute-start.28 = (bf16[1024,512]{1,0:T(8,128)(2,1)S(1)}, bf16[1024,512]{1,0:T(8,128)(2,1)S(1)}, u32[]{:S(2)}, u32[]{:S(2)}) collective-permute-start(bf16[1024,512]{1,0:T(8,128)(2,1)S(1)} %chain.5.src), channel_id=1, source_target_pairs={{0,1},{1,0},{2,3},{3,2},{4,6},{5,7},{6,4},{7,5},{8,9},{9,8},{10,11... | collective-permute-start | bytes 3145736 | tf_op jit(solution)/shard_map/ppermute | solution.py:488
  149.8 15.9 %collective-permute-start.27 = (bf16[784,512]{1,0:T(8,128)(2,1)S(1)}, bf16[784,512]{1,0:T(8,128)(2,1)S(1)}, u32[]{:S(2)}, u32[]{:S(2)}) collective-permute-start(bf16[784,512]{1,0:T(8,128)(2,1)S(1)} %get-tuple-element.175.src), channel_id=1, source_target_pairs={{0,4},{1,5},{2,6},{3,7},{4,0},{5,1},{6,2},{7,3},{8,12},{9,13},{10,... | collective-permute-start | bytes 2408456 | tf_op jit(solution)/shard_map/ppermute | solution.py:488
  149.9 18.0 %collective-permute-start.26 = (bf16[784,512]{1,0:T(8,128)(2,1)S(1)}, bf16[784,512]{1,0:T(8,128)(2,1)S(1)}, u32[]{:S(2)}, u32[]{:S(2)}) collective-permute-start(bf16[784,512]{1,0:T(8,128)(2,1)S(1)} %get-tuple-element.175.src), channel_id=1, source_target_pairs={{0,1},{1,0},{2,3},{3,2},{4,6},{5,7},{6,4},{7,5},{8,9},{9,8},{10,11... | collective-permute-start | bytes 2408456 | tf_op jit(solution)/shard_map/ppermute | solution.py:488
  159.3 4.5 %collective-permute-start.30 = (bf16[1024,512]{1,0:T(8,128)(2,1)S(1)}, bf16[1024,512]{1,0:T(8,128)(2,1)S(1)}, u32[]{:S(2)}, u32[]{:S(2)}) collective-permute-start(bf16[1024,512]{1,0:T(8,128)(2,1)S(1)} %collective-permute-done.28.src), channel_id=1, source_target_pairs={{0,4},{1,5},{2,6},{3,7},{4,0},{5,1},{6,2},{7,3},{8,12},{9,13},{10,... | collective-permute-start | bytes 3145736 | tf_op jit(solution)/shard_map/ppermute | solution.py:488
  167.9 2.4 %collective-permute-start.31 = (bf16[784,512]{1,0:T(8,128)(2,1)S(1)}, bf16[784,512]{1,0:T(8,128)(2,1)S(1)}, u32[]{:S(2)}, u32[]{:S(2)}) collective-permute-start(bf16[784,512]{1,0:T(8,128)(2,1)S(1)} %collective-permute-done.26.src.rest), channel_id=1, source_target_pairs={{0,4},{1,5},{2,6},{3,7},{4,0},{5,1},{6,2},{7,3},{8,12},{9,13},{10,... | collective-permute-start | bytes 2408456 | tf_op jit(solution)/shard_map/ppermute | solution.py:488
